TPU v7x, 32 devices: a whole 2x2x4 slice. The times are simulated.
32 devices in a mesh: groups: 2 (over x), tensor: 8 (over z, y), seq: 2 (over core).
Axes of the slice: x: 2, y: 2, z: 4, core: 2. Of those that a mesh axis runs over, the one named last changes fastest.
Arguments:
- tokens: bfloat16 [1024, 4096], P(('groups', 'tensor'), 'seq'), parts along dimension 0, may hold values from -6 to 6
- gate_weight: bfloat16 [4096, 16384], P('seq', 'tensor'), may hold values from -0.125 to 0.125
- up_weight: bfloat16 [4096, 16384], P('seq', 'tensor'), may hold values from -0.125 to 0.125
- down_weight: bfloat16 [16384, 4096], P('tensor', 'seq'), may hold values from -0.125 to 0.125
- gate_mask: int32 [32, 128], P('seq', 'tensor'), may hold values from 0 to 1, as said below
- up_mask: int32 [32, 128], P('seq', 'tensor'), may hold values from 0 to 1, as said below
- down_mask: int32 [128, 32], P('tensor', 'seq'), may hold values from 0 to 1, as said below
Outputs:
- mixed: bfloat16 [1024, 4096], P(('groups', 'tensor'), 'seq'), parts along dimension 0
There are 2 independent parts, one for each index of `groups`. A program takes and returns all parts, laid end to end along the dimension named above; an argument that names none is the same for every part. Nothing has to cross between parts.
Inputs may be any that keep to these rules, and one draw needn't show every extreme that they name: `gate_mask`: 1 keeps a 128 x 128 block of the weight, 0 removes it; the share of kept blocks varies from one block of hidden units to another. `up_mask`: as gate_mask. `down_mask`: as gate_mask, with hidden units along the first dimension.
All inputs are finite; a program needn't handle non-finite values.
Results may differ from a plain program's by a relative error of at most 0.005.
Values may be sent and summed in bfloat16 or wider, within the bound.
No kernel may reach another device: no remote copies, remote signals or barrier semaphores. Data moves between devices by JAX's collectives and lax.ppermute only.
A program may use at most 128 MiB of HBM per device.

v0:
```python
import jax
import jax.numpy as jnp
from jax import lax
from jax.sharding import PartitionSpec as P

BLOCK = 128


def pruned(weight, mask):
    rows, cols = weight.shape
    shaped = weight.reshape(rows // BLOCK, BLOCK, cols // BLOCK, BLOCK)
    kept = shaped * mask.astype(jnp.bfloat16)[:, None, :, None]
    return kept.reshape(rows, cols)


def on_device(tokens, gate_weight, up_weight, down_weight, gate_mask, up_mask, down_mask):
    gate_pruned = pruned(gate_weight, gate_mask)
    up_pruned = pruned(up_weight, up_mask)
    down_pruned = pruned(down_weight, down_mask)
    gathered = lax.all_gather(tokens, "tensor", axis=0, tiled=True)
    gate_part = jnp.dot(gathered, gate_pruned, preferred_element_type=jnp.float32)
    up_part = jnp.dot(gathered, up_pruned, preferred_element_type=jnp.float32)
    gate, up = (
        lax.psum_scatter(gate_part, "seq", scatter_dimension=0, tiled=True),
        lax.psum_scatter(up_part, "seq", scatter_dimension=0, tiled=True),
    )
    hidden = (jax.nn.silu(gate) * up).astype(jnp.bfloat16)
    full_hidden = lax.all_gather(hidden, "seq", axis=0, tiled=True)
    return lax.psum_scatter(
        jnp.dot(full_hidden, down_pruned, preferred_element_type=jnp.float32),
        "tensor",
        scatter_dimension=0,
        tiled=True,
    ).astype(jnp.bfloat16)


def solution(mesh):
    return jax.shard_map(
        on_device,
        mesh=mesh,
        in_specs=(
            P(("groups", "tensor"), "seq"),
            P("seq", "tensor"),
            P("seq", "tensor"),
            P("tensor", "seq"),
            P("seq", "tensor"),
            P("seq", "tensor"),
            P("tensor", "seq"),
        ),
        out_specs=P(("groups", "tensor"), "seq"),
        check_vma=False,
    )
```

profile of v0, /device:TPU:0, one launch (start us, length us, event | category | flops | bytes accessed | tf_op | source)
XLA Modules:
  0.0 227.9 jit_solution(9248779758720638804)
XLA Ops:
  6.5 0.7 all-gather.3.cloned.1.call-update
  7.3 0.0 reduce-scatter.4.cloned.1.call-start
  7.3 0.7 convert_element_type.15
  8.0 53.5 %all-gather.3.cloned.1.call-done = bf16[512,2048]{1,0:T(8,128)(2,1)} async-done(((bf16[64,2048]{1,0:T(8,128)(2,1)}), bf16[512,2048]{1,0:T(8,128)(2,1)}) %all-gather.3.cloned.1.call-update) | async-done | bytes 2097168 | tf_op jit(solution)/shard_map/all_gather | solution.py:20
  61.5 1.1 mul.40
  62.7 2.2 copy-done.2
  64.9 11.6 %fusion.6 = f32[512,2048]{0,1:T(8,128)} fusion(bf16[512,2048]{1,0:T(8,128)(2,1)} %all-gather.3.cloned.1.call-done, bf16[2048,2048]{1,0:T(8,128)(2,1)S(1)} %copy-done.2, bf16[256,8,16,128]{3,2,1,0:T(8,128)(2,1)S(1)} %bitcast.28), kind=kOutput, calls=%fused_computation.9 | convolution fusion | flops 4299161600 | bytes 23068672 | tf_op jit(solution)/shard_map/dot_general | solution.py:21
  76.5 0.0 reduce-scatter.4.cloned.1.call-update
  76.5 0.0 reduce-scatter.6.cloned.1.call-start
  76.5 0.6 copy-done
  77.2 1.1 mul.44
  78.3 2.4 %copy-done.3 = bf16[2048,2048]{1,0:T(8,128)(2,1)S(1)} copy-done((bf16[2048,2048]{1,0:T(8,128)(2,1)S(1)}, bf16[2048,2048]{1,0:T(8,128)(2,1)}, u32[]{:S(2)}) %copy-start.3) | copy-done | bytes 8388632
  80.7 9.9 %fusion.7 = f32[512,2048]{0,1:T(8,128)} fusion(bf16[512,2048]{1,0:T(8,128)(2,1)S(1)} %copy-done.4, bf16[2048,2048]{1,0:T(8,128)(2,1)S(1)} %copy-done.3, bf16[256,8,16,128]{3,2,1,0:T(8,128)(2,1)S(1)} %bitcast.26), kind=kOutput, calls=%fused_computation.10 | convolution fusion | flops 4299161600 | bytes 23068672 | tf_op jit(solution)/shard_map/dot_general | solution.py:22
  90.7 0.0 all-gather.5.cloned.1.call-start
  90.7 0.0 reduce-scatter.4.cloned.1.call-done
  90.7 12.2 %reduce-scatter.6.cloned.1.call-done = f32[256,2048]{0,1:T(8,128)} async-done(((f32[512,2048]{0,1:T(8,128)}), f32[256,2048]{0,1:T(8,128)}) %reduce-scatter.6.cloned.1.call-update) | async-done | bytes 2097168 | tf_op jit(solution)/shard_map/reduce_scatter | solution.py:25
  102.9 3.8 %multiply_convert_fusion = bf16[256,2048]{0,1:T(8,128)(2,1)} fusion(f32[256,2048]{0,1:T(8,128)} %reduce-scatter.6.cloned.1.call-done, f32[256,2048]{0,1:T(8,128)} %reduce-scatter.4.cloned.1.call-done), kind=kLoop, calls=%fused_computation.11 | loop fusion | flops 3145728 | bytes 5242880 | tf_op jit(solution)/shard_map/convert_element_type | solution.py:27
  106.8 0.2 reduce-scatter.8.cloned.1.call-start
  107.0 11.5 %all-gather.5.cloned.1.call-done = bf16[512,2048]{0,1:T(8,128)(2,1)} async-done(((bf16[256,2048]{0,1:T(8,128)(2,1)}), bf16[512,2048]{0,1:T(8,128)(2,1)}) %all-gather.5.cloned.1.call-update) | async-done | bytes 2097168 | tf_op jit(solution)/shard_map/all_gather | solution.py:28
  118.5 1.1 mul.48
  119.7 0.4 copy-done.5
  120.1 10.1 %fusion = f32[512,2048]{1,0:T(8,128)} fusion(bf16[512,2048]{0,1:T(8,128)(2,1)S(1)} %copy-done.5, bf16[2048,2048]{1,0:T(8,128)(2,1)} %param.10, bf16[256,8,16,128]{3,2,1,0:T(8,128)(2,1)S(1)} %bitcast.27), kind=kOutput, calls=%fused_computation.1 | convolution fusion | flops 4299161600 | bytes 23068672 | tf_op jit(solution)/shard_map/dot_general | solution.py:30
  130.2 89.4 %reduce-scatter.8.cloned.1.call-done = f32[64,2048]{1,0:T(8,128)} async-done(((f32[512,2048]{1,0:T(8,128)}), f32[64,2048]{1,0:T(8,128)}) %reduce-scatter.8.cloned.1.call-update) | async-done | bytes 524304 | tf_op jit(solution)/shard_map/reduce_scatter | solution.py:29
  219.6 1.8 convert_element_type.19
  (14 shorter events, 0.1 us)
Async XLA Ops:
  6.5 55.0 %all-gather.3.cloned.1.call-start = ((), (), s32[]{:S(2)}) async-start(), calls=%async_computation.3 | async-start | bytes 2359296 | tf_op jit(solution)/shard_map/all_gather | solution.py:20
  7.3 83.5 %reduce-scatter.4.cloned.1.call-start = ((), (), s32[]{:S(2)}) async-start(), calls=%async_computation.4 | async-start | bytes 6291456 | tf_op jit(solution)/shard_map/reduce_scatter | solution.py:24
  61.5 3.4 %copy-start.2 = (bf16[2048,2048]{1,0:T(8,128)(2,1)S(1)}, bf16[2048,2048]{1,0:T(8,128)(2,1)}, u32[]{:S(2)}) copy-start(bf16[2048,2048]{1,0:T(8,128)(2,1)} %param.8) | copy-start | bytes 25165828
  76.5 0.7 copy-start
  76.5 1.9 copy-start.4
  76.5 26.5 %reduce-scatter.6.cloned.1.call-start = ((), (), s32[]{:S(2)}) async-start(), calls=%async_computation.5 | async-start | bytes 6291456 | tf_op jit(solution)/shard_map/reduce_scatter | solution.py:25
  77.2 3.5 %copy-start.3 = (bf16[2048,2048]{1,0:T(8,128)(2,1)S(1)}, bf16[2048,2048]{1,0:T(8,128)(2,1)}, u32[]{:S(2)}) copy-start(bf16[2048,2048]{1,0:T(8,128)(2,1)} %param.9) | copy-start | bytes 25165828
  90.6 16.3 %copy-start.1 = (s32[16,16]{1,0:T(8,128)S(1)}, s32[16,16]{1,0:T(8,128)}, u32[]{:S(2)}) copy-start(s32[16,16]{1,0:T(8,128)} %param.13) | copy-start | bytes 3076
  90.7 27.9 %all-gather.5.cloned.1.call-start = ((), (), s32[]{:S(2)}) async-start(), calls=%async_computation.6 | async-start | bytes 3145728 | tf_op jit(solution)/shard_map/all_gather | solution.py:28
  106.8 112.9 %reduce-scatter.8.cloned.1.call-start = ((), (), s32[]{:S(2)}) async-start(), calls=%async_computation.7 | async-start | bytes 4718592 | tf_op jit(solution)/shard_map/reduce_scatter | solution.py:29
  118.5 1.6 copy-start.5
Sparse Core Ops, SparseCore 0:
  9.5 51.9 all-gather.2
  76.6 10.5 reduce-scatter.3
  90.8 12.1 reduce-scatter.5
  106.9 11.5 all-gather.4
  130.4 89.2 reduce-scatter.7
where the time goes:
time: 228 us
  waiting for transfers between devices  167 us (73%)
  matrix products  31.6 us (14%)
  between operations  13.2 us (6%)
  local copies, waits for them, and re-layouts  9.11 us (4%)
  other arithmetic  6.27 us (3%)
    reduce_scatter x1, waiting for transfers between devices, on_device(): lax.psum_scatter(jnp.dot(full_hidden, down_pruned, preferred_element_type...  89.4 us
    all_gather x1, waiting for transfers between devices, on_device(): gathered = lax.all_gather(tokens, 'tensor', axis=0, tiled=True)  53.5 us
    reduce_scatter x1, waiting for transfers between devices, on_device(): lax.psum_scatter(up_part, 'seq', scatter_dimension=0, tiled=True)  12.2 us
    dot_general x1, matrix products, on_device(): jnp.dot(gathered, gate_pruned, preferred_element_type=jnp.float32)  11.6 us
    all_gather x1, waiting for transfers between devices, on_device(): full_hidden = lax.all_gather(hidden, 'seq', axis=0, tiled=True)  11.5 us
    dot_general x1, matrix products, on_device(): jnp.dot(full_hidden, down_pruned, preferred_element_type=jnp.float32)  10.1 us
    dot_general x1, matrix products, on_device(): up_part = jnp.dot(gathered, up_pruned, preferred_element_type=jnp.float32)  9.92 us
    unnamed x12, local copies, waits for them, and re-layouts  5.67 us
  transfers between devices with their start and end apart: 5, of which 4 were waited for; matrix products, arithmetic and copies ran while one was open for 5% of the time, Pallas kernels for 0%

commit v1 on v0

v1 whole, which is shorter than its diff:
```python
import jax
import jax.numpy as jnp
from jax import lax
from jax.sharding import PartitionSpec as P

BLOCK = 128
BF16 = jnp.bfloat16
F32 = jnp.float32


def pruned(weight, mask):
    rows, cols = weight.shape
    shaped = weight.reshape(rows // BLOCK, BLOCK, cols // BLOCK, BLOCK)
    kept = shaped * mask.astype(BF16)[:, None, :, None]
    return kept.reshape(rows, cols)


def dot(a, b):
    return jnp.dot(a, b, preferred_element_type=F32)


def plain(tokens, gate_weight, up_weight, down_weight, gate_mask, up_mask, down_mask):
    gathered = lax.all_gather(tokens, "tensor", axis=0, tiled=True)
    gate_part = dot(gathered, pruned(gate_weight, gate_mask))
    up_part = dot(gathered, pruned(up_weight, up_mask))
    gate = lax.psum_scatter(gate_part, "seq", scatter_dimension=0, tiled=True)
    up = lax.psum_scatter(up_part, "seq", scatter_dimension=0, tiled=True)
    hidden = (jax.nn.silu(gate) * up).astype(BF16)
    full_hidden = lax.all_gather(hidden, "seq", axis=0, tiled=True)
    return lax.psum_scatter(
        dot(full_hidden, pruned(down_weight, down_mask)), "tensor", scatter_dimension=0, tiled=True
    ).astype(BF16)


ACROSS = [(2 * z + y, 2 * z + 1 - y) for z in range(4) for y in range(2)]
PAIR = [(2 * z + y, 2 * (z ^ 1) + y) for z in range(4) for y in range(2)]
MIDDLE = [(2 * z + y, 2 * (3 - z) + y) for z in (1, 2) for y in range(2)]
OUTWARD = [(2 * z + y, 2 * (z ^ 1) + y) for z in (1, 2) for y in range(2)]
INWARD = [(2 * z + y, 2 * (z ^ 1) + y) for z in (0, 3) for y in range(2)]


def move(value, perm):
    return lax.ppermute(value, "tensor", perm)


def inner():
    z = lax.axis_index("tensor") // 2
    return (z == 1) | (z == 2)


def gather(own):
    pair = move(own, PAIR)
    near = move(own, MIDDLE)
    own_y = move(own, ACROSS)
    far = move(pair, MIDDLE)
    near_out = move(near, OUTWARD)
    pair_y = move(pair, ACROSS)
    near = jnp.where(inner(), near, near_out)
    far_out = move(far, OUTWARD)
    near_y = move(near, ACROSS)
    far = jnp.where(inner(), far, far_out)
    far_y = move(far, ACROSS)
    return own, own_y, pair, pair_y, near, near_y, far, far_y


def add(a, b):
    return a.astype(F32) + b.astype(F32)


def scatter(own, own_y, pair, pair_y, near, near_y, far, far_y):
    far_s = add(far, move(far_y, ACROSS)).astype(BF16)
    near_s = add(near, move(near_y, ACROSS)).astype(BF16)
    pair_s = add(pair, move(pair_y, ACROSS))
    own_s = add(own, move(own_y, ACROSS))
    far_s = add(far_s, move(far_s, INWARD)).astype(BF16)
    near_s = add(near_s, move(near_s, INWARD)).astype(BF16)
    pair_s = add(pair_s, move(far_s, MIDDLE)).astype(BF16)
    own_s = add(own_s, move(near_s, MIDDLE))
    return add(own_s, move(pair_s, PAIR)).astype(BF16)


SWAP = [(0, 1), (1, 0)]


def lined(tokens, gate_weight, up_weight, down_weight, gate_mask, up_mask, down_mask):
    rows = tokens.shape[0]
    half = rows // 2
    gate_pruned, up_pruned, down_pruned = lax.optimization_barrier(
        (pruned(gate_weight, gate_mask), pruned(up_weight, up_mask), pruned(down_weight, down_mask))
    )
    core = lax.axis_index("seq")
    gathered = jnp.stack(gather(tokens)).reshape(8, 2, half, -1)
    theirs = lax.dynamic_index_in_dim(gathered, 1 - core, 1, keepdims=False).reshape(8 * half, -1)
    mine = lax.dynamic_index_in_dim(gathered, core, 1, keepdims=False).reshape(8 * half, -1)
    gate_sent = lax.ppermute(dot(theirs, gate_pruned).astype(BF16), "seq", SWAP)
    up_sent = lax.ppermute(dot(theirs, up_pruned).astype(BF16), "seq", SWAP)
    gate = dot(mine, gate_pruned) + gate_sent.astype(F32)
    up = dot(mine, up_pruned) + up_sent.astype(F32)
    hidden = (jax.nn.silu(gate) * up).astype(BF16)
    other = lax.ppermute(hidden, "seq", SWAP)
    parts_mine = dot(hidden, down_pruned).astype(BF16).reshape(8, half, -1)
    parts_theirs = dot(other, down_pruned).astype(BF16).reshape(8, half, -1)
    first = jnp.where(core == 0, parts_mine, parts_theirs)
    second = jnp.where(core == 0, parts_theirs, parts_mine)
    parts = jnp.stack([first, second], axis=1).reshape(8, rows, -1)
    return scatter(*(parts[i] for i in range(8)))


def solution(mesh):
    return jax.shard_map(
        lined if mesh.shape["tensor"] == 8 and mesh.shape["seq"] == 2 else plain,
        mesh=mesh,
        in_specs=(
            P(("groups", "tensor"), "seq"),
            P("seq", "tensor"),
            P("seq", "tensor"),
            P("tensor", "seq"),
            P("seq", "tensor"),
            P("seq", "tensor"),
            P("tensor", "seq"),
        ),
        out_specs=P(("groups", "tensor"), "seq"),
        check_vma=False,
    )
```

time: 228 us -> 115 us (0.50)
  waiting for transfers between devices: 167 us -> 36 us
  starting transfers between devices: 0.35 us -> 28 us
  other arithmetic: 6.27 us -> 24 us
  between operations: 13.2 us -> 0.39 us
  matrix products: 31.6 us -> 21.4 us
  local copies, waits for them, and re-layouts: 9.11 us -> 4.58 us
    reduce_scatter x3 -> x0, waiting for transfers between devices: 102 us -> none  [the longest x1 89.4 us: on_device(): lax.psum_scatter(jnp.dot(full_hidden, down_pruned, preferred_element_type...]
    all_gather x2 -> x0, waiting for transfers between devices: 65 us -> none  [the longest x1 53.5 us: on_device(): gathered = lax.all_gather(tokens, 'tensor', axis=0, tiled=True)]
    ppermute x0 -> x21, waiting for transfers between devices: none -> 36 us  [the longest x18 35.8 us: move(): return lax.ppermute(value, 'tensor', perm)]
    ppermute x0 -> x21, starting transfers between devices: none -> 28 us  [the longest x18 27.6 us: move(): return lax.ppermute(value, 'tensor', perm)]
    mul x0 -> x2, other arithmetic: none -> 20.3 us  [pruned(): kept = shaped * mask.astype(BF16)[:, None, :, None]]
    dot_general x3 -> x6, matrix products: 31.6 us -> 21.4 us  [dot(): return jnp.dot(a, b, preferred_element_type=F32)]
    unnamed x12 -> x15, local copies, waits for them, and re-layouts: 5.67 us -> 0.98 us
    convert_element_type x5 -> x9, other arithmetic: 6.27 us -> 3.37 us  [the longest x3 2.1 us: pruned(): kept = shaped * mask.astype(BF16)[:, None, :, None]]
  transfers between devices with their start and end apart: 5 -> 21, of which waited for: 4 -> 8; matrix products, arithmetic and copies ran while one was open for 5% -> 32% of each run, Pallas kernels for 0% -> 0%
where the time goes in v1:
time: 115 us; the launch traced here: 114 us
  waiting for transfers between devices  36 us (31%)
  starting transfers between devices  28 us (24%)
  other arithmetic  24 us (21%)
  matrix products  21.4 us (19%)
  local copies, waits for them, and re-layouts  4.58 us (4%)
    ppermute x18, waiting for transfers between devices, move(): return lax.ppermute(value, 'tensor', perm)  35.8 us
    ppermute x18, starting transfers between devices, move(): return lax.ppermute(value, 'tensor', perm)  27.6 us
    dot_general x6, matrix products, dot(): return jnp.dot(a, b, preferred_element_type=F32)  21.4 us
    mul x2, other arithmetic, pruned(): kept = shaped * mask.astype(BF16)[:, None, :, None]  20.3 us
    mul x3, local copies, waits for them, and re-layouts, pruned(): kept = shaped * mask.astype(BF16)[:, None, :, None]  3.43 us
  transfers between devices with their start and end apart: 21, of which 8 were waited for; matrix products, arithmetic and copies ran while one was open for 32% of the time, Pallas kernels for 0%

profile of v1, /device:TPU:0, one launch (start us, length us, event | category | flops | bytes accessed | tf_op | source)
XLA Modules:
  0.0 114.4 jit_solution(4551113982558929153)
XLA Ops:
  0.7 5.9 %collective-permute-start.1 = (bf16[64,2048]{1,0:T(8,128)(2,1)}, bf16[64,2048]{1,0:T(8,128)(2,1)S(1)}, u32[]{:S(2)}, u32[]{:S(2)}) collective-permute-start(bf16[64,2048]{1,0:T(8,128)(2,1)} %param.7), channel_id=1, source_target_pairs={{0,4},{2,6},{4,0},{6,2},{8,12},{10,14},{12,8},{14,10},{1,5},{3,7},... | collective-permute-start | bytes 786440 | tf_op jit(solution)/shard_map/ppermute | solution.py:43
  6.6 1.5 %collective-permute-start = (bf16[64,2048]{1,0:T(8,128)(2,1)}, bf16[64,2048]{1,0:T(8,128)(2,1)S(1)}, u32[]{:S(2)}, u32[]{:S(2)}) collective-permute-start(bf16[64,2048]{1,0:T(8,128)(2,1)} %param.7), channel_id=1, source_target_pairs={{0,2},{2,0},{4,6},{6,4},{8,10},{10,8},{12,14},{14,12},{1,3},{3,1},... | collective-permute-start | bytes 786440 | tf_op jit(solution)/shard_map/ppermute | solution.py:43
  12.5 12.6 %bitcast_multiply_fusion = (bf16[2048,2048]{1,0:T(8,128)(2,1)}, bf16[2048,2048]{1,0:T(8,128)(2,1)}) fusion(bf16[2048,2048]{1,0:T(8,128)(2,1)} %param.10, bf16[256,8,16,128]{3,2,1,0:T(8,128)(2,1)S(1)} %bitcast.54, bf16[2048,2048]{1,0:T(8,128)(2,1)} %param.9, bf16[256,8,16,128]{3,2,1,0:T(8,128)(2,1)S(1)} %bitcast.53), kind=kLoop, calls=%fused_computation | loop fusion | flops 8388608 | bytes 50331648 | tf_op jit(solution)/shard_map/mul | solution.py:14
  26.2 7.8 %bitcast_multiply_fusion.2 = bf16[2048,2048]{1,0:T(8,128)(2,1)} fusion(bf16[2048,2048]{1,0:T(8,128)(2,1)} %param.8, bf16[256,8,16,128]{3,2,1,0:T(8,128)(2,1)S(1)} %bitcast.52), kind=kLoop, calls=%fused_computation.2 | loop fusion | flops 4194304 | bytes 25165824 | tf_op jit(solution)/shard_map/mul | solution.py:14
  36.7 6.5 %collective-permute-done.4 = bf16[64,2048]{1,0:T(8,128)(2,1)S(1)} collective-permute-done((bf16[64,2048]{1,0:T(8,128)(2,1)S(1)}, bf16[64,2048]{1,0:T(8,128)(2,1)S(1)}, u32[]{:S(2)}, u32[]{:S(2)}) %collective-permute-start.4) | collective-permute-done | bytes 262176 | tf_op jit(solution)/shard_map/ppermute | solution.py:43
  43.8 1.7 %collective-permute-start.7 = (bf16[64,2048]{1,0:T(8,128)(2,1)S(1)}, bf16[64,2048]{1,0:T(8,128)(2,1)S(1)}, u32[]{:S(2)}, u32[]{:S(2)}) collective-permute-start(bf16[64,2048]{1,0:T(8,128)(2,1)S(1)} %collective-permute-done.6), channel_id=1, source_target_pairs={{4,0},{6,2},{8,12},{10,14},{5,1},{7,3},{9,13},{11,15},{20,16},{22,... | collective-permute-start | bytes 786440 | tf_op jit(solution)/shard_map/ppermute | solution.py:43
  45.6 7.2 %collective-permute-done.7 = bf16[64,2048]{1,0:T(8,128)(2,1)S(1)} collective-permute-done((bf16[64,2048]{1,0:T(8,128)(2,1)S(1)}, bf16[64,2048]{1,0:T(8,128)(2,1)S(1)}, u32[]{:S(2)}, u32[]{:S(2)}) %collective-permute-start.7) | collective-permute-done | bytes 262176 | tf_op jit(solution)/shard_map/ppermute | solution.py:43
  52.8 1.6 %collective-permute-start.8 = (bf16[64,2048]{1,0:T(8,128)(2,1)S(1)}, bf16[64,2048]{1,0:T(8,128)(2,1)S(1)}, u32[]{:S(2)}, u32[]{:S(2)}) collective-permute-start(bf16[64,2048]{1,0:T(8,128)(2,1)S(1)} %broadcast_select_fusion.2), channel_id=1, source_target_pairs={{0,2},{2,0},{4,6},{6,4},{8,10},{10,8},{12,14},{14,12},{1,3},{3,1},... | collective-permute-start | bytes 786440 | tf_op jit(solution)/shard_map/ppermute | solution.py:43
  54.4 4.8 %collective-permute-done.8 = bf16[64,2048]{1,0:T(8,128)(2,1)S(1)} collective-permute-done((bf16[64,2048]{1,0:T(8,128)(2,1)S(1)}, bf16[64,2048]{1,0:T(8,128)(2,1)S(1)}, u32[]{:S(2)}, u32[]{:S(2)}) %collective-permute-start.8) | collective-permute-done | bytes 262176 | tf_op jit(solution)/shard_map/ppermute | solution.py:43
  59.5 2.4 %convolution_convert_fusion.3 = bf16[256,2048]{1,0:T(8,128)(2,1)S(1)} fusion(bf16[256,2048]{1,0:T(8,128)(2,1)S(1)} %bitcast.59, bf16[2048,2048]{1,0:T(8,128)(2,1)S(1)} %copy-done), kind=kOutput, calls=%fused_computation.22 | convolution fusion | flops 2148007936 | bytes 10485760 | tf_op jit(solution)/shard_map/dot_general | solution.py:19
  62.8 2.4 %convolution_convert_fusion.2 = bf16[256,2048]{1,0:T(8,128)(2,1)S(1)} fusion(bf16[256,2048]{1,0:T(8,128)(2,1)S(1)} %bitcast.60, bf16[2048,2048]{1,0:T(8,128)(2,1)S(1)} %bitcast.56), kind=kOutput, calls=%fused_computation.21 | convolution fusion | flops 2148007936 | bytes 10485760 | tf_op jit(solution)/shard_map/dot_general | solution.py:19
  65.3 2.4 %convolution_add_fusion.1 = f32[256,2048]{1,0:T(8,128)S(1)} fusion(bf16[256,2048]{1,0:T(8,128)(2,1)S(1)} %bitcast.57, bf16[2048,2048]{1,0:T(8,128)(2,1)S(1)} %copy-done, bf16[256,2048]{1,0:T(8,128)(2,1)S(1)} %collective-permute-done.9), kind=kOutput, calls=%fused_computation.18 | convolution fusion | flops 2148532224 | bytes 12582912 | tf_op jit(solution)/shard_map/dot_general | solution.py:19
  67.9 2.8 %multiply_convert_fusion = bf16[256,2048]{1,0:T(8,128)(2,1)S(1)} fusion(f32[256,2048]{1,0:T(8,128)S(1)} %convolution_add_fusion.1, bf16[256,2048]{1,0:T(8,128)(2,1)S(1)} %collective-permute-done.10, bf16[256,2048]{1,0:T(8,128)(2,1)S(1)} %bitcast.58, bf16[2048,2048]{1,0:T(8,128)(2,1)S(1)} %bitcast.56), kind=kOutput, calls=%fused_computation.23 | convolution fusion | flops 2151677952 | bytes 13631488 | tf_op jit(solution)/shard_map/dot_general | solution.py:19
  71.0 5.7 %convolution_convert_fusion.1 = bf16[256,2048]{1,0:T(8,128)(2,1)S(1)} fusion(bf16[256,2048]{1,0:T(8,128)(2,1)S(1)} %multiply_convert_fusion, bf16[2048,2048]{1,0:T(8,128)(2,1)} %get-tuple-element.10), kind=kOutput, calls=%fused_computation.20 | convolution fusion | flops 2148007936 | bytes 10485760 | tf_op jit(solution)/shard_map/dot_general | solution.py:19
  76.8 5.7 %broadcast_select_fusion.1 = (bf16[256,2048]{1,0:T(8,128)(2,1)S(1)}, bf16[256,2048]{1,0:T(8,128)(2,1)S(1)}) fusion(bf16[256,2048]{1,0:T(8,128)(2,1)S(1)} %convolution_convert_fusion.1, pred[]{:T(512)S(6)} %eq.12, bf16[256,2048]{1,0:T(8,128)(2,1)S(1)} %collective-permute-done.11, bf16[2048,2048]{1,0:T(8,128)(2,1)} %get-tuple-element.10), kind=kOutput, calls=%fused_computation.25 | convolution fusion | flops 2149056512 | bytes 12582913 | tf_op jit(solution)/shard_map/dot_general | solution.py:19
  82.7 1.6 %collective-permute-start.17 = (bf16[64,2048]{1,0:T(8,128)(2,1)S(1)}, bf16[64,2048]{1,0:T(8,128)(2,1)S(1)}, u32[]{:S(2)}, u32[]{:S(2)}) collective-permute-start(bf16[64,2048]{1,0:T(8,128)(2,1)S(1)} %bitcast.68), channel_id=1, source_target_pairs={{0,2},{2,0},{4,6},{6,4},{8,10},{10,8},{12,14},{14,12},{1,3},{3,1},... | collective-permute-start | bytes 786440 | tf_op jit(solution)/shard_map/ppermute | solution.py:43
  84.8 1.5 %collective-permute-start.16 = (bf16[64,2048]{1,0:T(8,128)(2,1)S(1)}, bf16[64,2048]{1,0:T(8,128)(2,1)S(1)}, u32[]{:S(2)}, u32[]{:S(2)}) collective-permute-start(bf16[64,2048]{1,0:T(8,128)(2,1)S(1)} %bitcast.66), channel_id=1, source_target_pairs={{0,2},{2,0},{4,6},{6,4},{8,10},{10,8},{12,14},{14,12},{1,3},{3,1},... | collective-permute-start | bytes 786440 | tf_op jit(solution)/shard_map/ppermute | solution.py:43
  86.8 5.1 %collective-permute-done.17 = bf16[64,2048]{1,0:T(8,128)(2,1)S(1)} collective-permute-done((bf16[64,2048]{1,0:T(8,128)(2,1)S(1)}, bf16[64,2048]{1,0:T(8,128)(2,1)S(1)}, u32[]{:S(2)}, u32[]{:S(2)}) %collective-permute-start.17) | collective-permute-done | bytes 262176 | tf_op jit(solution)/shard_map/ppermute | solution.py:43
  92.0 1.5 %collective-permute-start.18 = (bf16[64,2048]{1,0:T(8,128)(2,1)S(1)}, bf16[64,2048]{1,0:T(8,128)(2,1)S(1)}, u32[]{:S(2)}, u32[]{:S(2)}) collective-permute-start(bf16[64,2048]{1,0:T(8,128)(2,1)S(1)} %fusion), channel_id=1, source_target_pairs={{0,4},{2,6},{12,8},{14,10},{1,5},{3,7},{13,9},{15,11},{16,20},{18,... | collective-permute-start | bytes 786440 | tf_op jit(solution)/shard_map/ppermute | solution.py:43
  93.5 4.0 %collective-permute-done.13 = bf16[64,2048]{1,0:T(8,128)(2,1)S(1)} collective-permute-done((bf16[64,2048]{1,0:T(8,128)(2,1)S(1)}, bf16[64,2048]{1,0:T(8,128)(2,1)S(1)}, u32[]{:S(2)}, u32[]{:S(2)}) %collective-permute-start.13) | collective-permute-done | bytes 262176 | tf_op jit(solution)/shard_map/ppermute | solution.py:43
  97.6 1.5 %collective-permute-start.14 = (bf16[64,2048]{1,0:T(8,128)(2,1)S(1)}, bf16[64,2048]{1,0:T(8,128)(2,1)S(1)}, u32[]{:S(2)}, u32[]{:S(2)}) collective-permute-start(bf16[64,2048]{1,0:T(8,128)(2,1)S(1)} %fusion.3), channel_id=1, source_target_pairs={{0,4},{2,6},{12,8},{14,10},{1,5},{3,7},{13,9},{15,11},{16,20},{18,... | collective-permute-start | bytes 786440 | tf_op jit(solution)/shard_map/ppermute | solution.py:43
  99.8 3.8 %collective-permute-done.14 = bf16[64,2048]{1,0:T(8,128)(2,1)S(1)} collective-permute-done((bf16[64,2048]{1,0:T(8,128)(2,1)S(1)}, bf16[64,2048]{1,0:T(8,128)(2,1)S(1)}, u32[]{:S(2)}, u32[]{:S(2)}) %collective-permute-start.14) | collective-permute-done | bytes 262176 | tf_op jit(solution)/shard_map/ppermute | solution.py:43
  104.5 4.7 %collective-permute-start.20 = (bf16[64,2048]{1,0:T(8,128)(2,1)S(1)}, bf16[64,2048]{1,0:T(8,128)(2,1)S(1)}, u32[]{:S(2)}, u32[]{:S(2)}) collective-permute-start(bf16[64,2048]{1,0:T(8,128)(2,1)S(1)} %fusion.2), channel_id=1, source_target_pairs={{0,4},{2,6},{4,0},{6,2},{8,12},{10,14},{12,8},{14,10},{1,5},{3,7},... | collective-permute-start | bytes 786440 | tf_op jit(solution)/shard_map/ppermute | solution.py:43
  109.2 4.3 %collective-permute-done.20 = bf16[64,2048]{1,0:T(8,128)(2,1)S(1)} collective-permute-done((bf16[64,2048]{1,0:T(8,128)(2,1)S(1)}, bf16[64,2048]{1,0:T(8,128)(2,1)S(1)}, u32[]{:S(2)}, u32[]{:S(2)}) %collective-permute-start.20) | collective-permute-done | bytes 262176 | tf_op jit(solution)/shard_map/ppermute | solution.py:43
  (59 shorter events, 15.1 us)
Async XLA Ops:
  0.0 34.0 %collective-permute-start.3 = (bf16[64,2048]{1,0:T(8,128)(2,1)}, bf16[64,2048]{1,0:T(8,128)(2,1)S(1)}, u32[]{:S(2)}, u32[]{:S(2)}) collective-permute-start(bf16[64,2048]{1,0:T(8,128)(2,1)} %param.7), channel_id=1, source_target_pairs={{4,8},{6,10},{8,4},{10,6},{5,9},{7,11},{9,5},{11,7},{20,24},{22,26... | collective-permute-start | bytes 786440 | tf_op jit(solution)/shard_map/ppermute | solution.py:43
  0.7 34.7 %collective-permute-start.1 = (bf16[64,2048]{1,0:T(8,128)(2,1)}, bf16[64,2048]{1,0:T(8,128)(2,1)S(1)}, u32[]{:S(2)}, u32[]{:S(2)}) collective-permute-start(bf16[64,2048]{1,0:T(8,128)(2,1)} %param.7), channel_id=1, source_target_pairs={{0,4},{2,6},{4,0},{6,2},{8,12},{10,14},{12,8},{14,10},{1,5},{3,7},... | collective-permute-start | bytes 786440 | tf_op jit(solution)/shard_map/ppermute | solution.py:43
  6.6 28.8 %collective-permute-start = (bf16[64,2048]{1,0:T(8,128)(2,1)}, bf16[64,2048]{1,0:T(8,128)(2,1)S(1)}, u32[]{:S(2)}, u32[]{:S(2)}) collective-permute-start(bf16[64,2048]{1,0:T(8,128)(2,1)} %param.7), channel_id=1, source_target_pairs={{0,2},{2,0},{4,6},{6,4},{8,10},{10,8},{12,14},{14,12},{1,3},{3,1},... | collective-permute-start | bytes 786440 | tf_op jit(solution)/shard_map/ppermute | solution.py:43
  26.2 7.8 %copy-start.1 = (bf16[64,2048]{1,0:T(8,128)(2,1)S(1)}, bf16[64,2048]{1,0:T(8,128)(2,1)}, u32[]{:S(2)}) copy-start(bf16[64,2048]{1,0:T(8,128)(2,1)} %param.7) | copy-start | bytes 786436
  34.1 9.1 %collective-permute-start.4 = (bf16[64,2048]{1,0:T(8,128)(2,1)S(1)}, bf16[64,2048]{1,0:T(8,128)(2,1)S(1)}, u32[]{:S(2)}, u32[]{:S(2)}) collective-permute-start(bf16[64,2048]{1,0:T(8,128)(2,1)S(1)} %collective-permute-done.3), channel_id=1, source_target_pairs={{4,0},{6,2},{8,12},{10,14},{5,1},{7,3},{9,13},{11,15},{20,16},{22,... | collective-permute-start | bytes 786440 | tf_op jit(solution)/shard_map/ppermute | solution.py:43
  35.4 10.1 %collective-permute-start.2 = (bf16[64,2048]{1,0:T(8,128)(2,1)S(1)}, bf16[64,2048]{1,0:T(8,128)(2,1)S(1)}, u32[]{:S(2)}, u32[]{:S(2)}) collective-permute-start(bf16[64,2048]{1,0:T(8,128)(2,1)S(1)} %collective-permute-done.1), channel_id=1, source_target_pairs={{0,2},{2,0},{4,6},{6,4},{8,10},{10,8},{12,14},{14,12},{1,3},{3,1},... | collective-permute-start | bytes 786440 | tf_op jit(solution)/shard_map/ppermute | solution.py:43
  36.0 7.8 %collective-permute-start.6 = (bf16[64,2048]{1,0:T(8,128)(2,1)S(1)}, bf16[64,2048]{1,0:T(8,128)(2,1)S(1)}, u32[]{:S(2)}, u32[]{:S(2)}) collective-permute-start(bf16[64,2048]{1,0:T(8,128)(2,1)S(1)} %collective-permute-done.1), channel_id=1, source_target_pairs={{4,8},{6,10},{8,4},{10,6},{5,9},{7,11},{9,5},{11,7},{20,24},{22,26... | collective-permute-start | bytes 786440 | tf_op jit(solution)/shard_map/ppermute | solution.py:43
  43.2 16.3 %copy-start = (bf16[2048,2048]{1,0:T(8,128)(2,1)S(1)}, bf16[2048,2048]{1,0:T(8,128)(2,1)}, u32[]{:S(2)}) copy-start(bf16[2048,2048]{1,0:T(8,128)(2,1)} %bitcast_multiply_fusion.2) | copy-start | bytes 25165828
  43.2 11.2 %collective-permute-start.5 = (bf16[64,2048]{1,0:T(8,128)(2,1)S(1)}, bf16[64,2048]{1,0:T(8,128)(2,1)S(1)}, u32[]{:S(2)}, u32[]{:S(2)}) collective-permute-start(bf16[64,2048]{1,0:T(8,128)(2,1)S(1)} %broadcast_select_fusion.3), channel_id=1, source_target_pairs={{0,2},{2,0},{4,6},{6,4},{8,10},{10,8},{12,14},{14,12},{1,3},{3,1},... | collective-permute-start | bytes 786440 | tf_op jit(solution)/shard_map/ppermute | solution.py:43
  43.8 9.0 %collective-permute-start.7 = (bf16[64,2048]{1,0:T(8,128)(2,1)S(1)}, bf16[64,2048]{1,0:T(8,128)(2,1)S(1)}, u32[]{:S(2)}, u32[]{:S(2)}) collective-permute-start(bf16[64,2048]{1,0:T(8,128)(2,1)S(1)} %collective-permute-done.6), channel_id=1, source_target_pairs={{4,0},{6,2},{8,12},{10,14},{5,1},{7,3},{9,13},{11,15},{20,16},{22,... | collective-permute-start | bytes 786440 | tf_op jit(solution)/shard_map/ppermute | solution.py:43
  52.8 6.4 %collective-permute-start.8 = (bf16[64,2048]{1,0:T(8,128)(2,1)S(1)}, bf16[64,2048]{1,0:T(8,128)(2,1)S(1)}, u32[]{:S(2)}, u32[]{:S(2)}) collective-permute-start(bf16[64,2048]{1,0:T(8,128)(2,1)S(1)} %broadcast_select_fusion.2), channel_id=1, source_target_pairs={{0,2},{2,0},{4,6},{6,4},{8,10},{10,8},{12,14},{14,12},{1,3},{3,1},... | collective-permute-start | bytes 786440 | tf_op jit(solution)/shard_map/ppermute | solution.py:43
  59.4 3.3 %slice-start.1 = ((s8[8388608]{0:T(1024)(128)(4,1)}), s8[4194304]{0:T(1024)(128)(4,1)S(1)}, s32[]{:S(2)}) async-start(s8[8388608]{0:T(1024)(128)(4,1)} %bitcast.55), calls=%async_computation.1 | async-start | bytes 8388608
  61.9 3.4 %collective-permute-start.9 = (bf16[256,2048]{1,0:T(8,128)(2,1)S(1)}, bf16[256,2048]{1,0:T(8,128)(2,1)S(1)}, u32[]{:S(2)}, u32[]{:S(2)}) collective-permute-start(bf16[256,2048]{1,0:T(8,128)(2,1)S(1)} %convolution_convert_fusion.3), channel_id=1, source_target_pairs={{0,1},{1,0},{2,3},{3,2},{4,5},{5,4},{6,7},{7,6},{8,9},{9,8},{10,11... | collective-permute-start | bytes 3145736 | tf_op jit(solution)/shard_map/ppermute | solution.py:95
  65.2 2.7 %collective-permute-start.10 = (bf16[256,2048]{1,0:T(8,128)(2,1)S(1)}, bf16[256,2048]{1,0:T(8,128)(2,1)S(1)}, u32[]{:S(2)}, u32[]{:S(2)}) collective-permute-start(bf16[256,2048]{1,0:T(8,128)(2,1)S(1)} %convolution_convert_fusion.2), channel_id=1, source_target_pairs={{0,1},{1,0},{2,3},{3,2},{4,5},{5,4},{6,7},{7,6},{8,9},{9,8},{10,11... | collective-permute-start | bytes 3145736 | tf_op jit(solution)/shard_map/ppermute | solution.py:96
  70.7 6.1 %collective-permute-start.11 = (bf16[256,2048]{1,0:T(8,128)(2,1)S(1)}, bf16[256,2048]{1,0:T(8,128)(2,1)S(1)}, u32[]{:S(2)}, u32[]{:S(2)}) collective-permute-start(bf16[256,2048]{1,0:T(8,128)(2,1)S(1)} %multiply_convert_fusion), channel_id=1, source_target_pairs={{0,1},{1,0},{2,3},{3,2},{4,5},{5,4},{6,7},{7,6},{8,9},{9,8},{10,11... | collective-permute-start | bytes 3145736 | tf_op jit(solution)/shard_map/ppermute | solution.py:100
  82.7 9.2 %collective-permute-start.17 = (bf16[64,2048]{1,0:T(8,128)(2,1)S(1)}, bf16[64,2048]{1,0:T(8,128)(2,1)S(1)}, u32[]{:S(2)}, u32[]{:S(2)}) collective-permute-start(bf16[64,2048]{1,0:T(8,128)(2,1)S(1)} %bitcast.68), channel_id=1, source_target_pairs={{0,2},{2,0},{4,6},{6,4},{8,10},{10,8},{12,14},{14,12},{1,3},{3,1},... | collective-permute-start | bytes 786440 | tf_op jit(solution)/shard_map/ppermute | solution.py:43
  84.3 13.2 %collective-permute-start.13 = (bf16[64,2048]{1,0:T(8,128)(2,1)S(1)}, bf16[64,2048]{1,0:T(8,128)(2,1)S(1)}, u32[]{:S(2)}, u32[]{:S(2)}) collective-permute-start(bf16[64,2048]{1,0:T(8,128)(2,1)S(1)} %bitcast.67), channel_id=1, source_target_pairs={{0,2},{2,0},{4,6},{6,4},{8,10},{10,8},{12,14},{14,12},{1,3},{3,1},... | collective-permute-start | bytes 786440 | tf_op jit(solution)/shard_map/ppermute | solution.py:43
  84.8 19.6 %collective-permute-start.16 = (bf16[64,2048]{1,0:T(8,128)(2,1)S(1)}, bf16[64,2048]{1,0:T(8,128)(2,1)S(1)}, u32[]{:S(2)}, u32[]{:S(2)}) collective-permute-start(bf16[64,2048]{1,0:T(8,128)(2,1)S(1)} %bitcast.66), channel_id=1, source_target_pairs={{0,2},{2,0},{4,6},{6,4},{8,10},{10,8},{12,14},{14,12},{1,3},{3,1},... | collective-permute-start | bytes 786440 | tf_op jit(solution)/shard_map/ppermute | solution.py:43
  86.3 22.9 %collective-permute-start.12 = (bf16[64,2048]{1,0:T(8,128)(2,1)S(1)}, bf16[64,2048]{1,0:T(8,128)(2,1)S(1)}, u32[]{:S(2)}, u32[]{:S(2)}) collective-permute-start(bf16[64,2048]{1,0:T(8,128)(2,1)S(1)} %bitcast.65), channel_id=1, source_target_pairs={{0,2},{2,0},{4,6},{6,4},{8,10},{10,8},{12,14},{14,12},{1,3},{3,1},... | collective-permute-start | bytes 786440 | tf_op jit(solution)/shard_map/ppermute | solution.py:43
  92.0 7.1 %collective-permute-start.18 = (bf16[64,2048]{1,0:T(8,128)(2,1)S(1)}, bf16[64,2048]{1,0:T(8,128)(2,1)S(1)}, u32[]{:S(2)}, u32[]{:S(2)}) collective-permute-start(bf16[64,2048]{1,0:T(8,128)(2,1)S(1)} %fusion), channel_id=1, source_target_pairs={{0,4},{2,6},{12,8},{14,10},{1,5},{3,7},{13,9},{15,11},{16,20},{18,... | collective-permute-start | bytes 786440 | tf_op jit(solution)/shard_map/ppermute | solution.py:43
  97.6 6.0 %collective-permute-start.14 = (bf16[64,2048]{1,0:T(8,128)(2,1)S(1)}, bf16[64,2048]{1,0:T(8,128)(2,1)S(1)}, u32[]{:S(2)}, u32[]{:S(2)}) collective-permute-start(bf16[64,2048]{1,0:T(8,128)(2,1)S(1)} %fusion.3), channel_id=1, source_target_pairs={{0,4},{2,6},{12,8},{14,10},{1,5},{3,7},{13,9},{15,11},{16,20},{18,... | collective-permute-start | bytes 786440 | tf_op jit(solution)/shard_map/ppermute | solution.py:43
  99.2 5.2 %collective-permute-start.19 = (bf16[64,2048]{1,0:T(8,128)(2,1)S(1)}, bf16[64,2048]{1,0:T(8,128)(2,1)S(1)}, u32[]{:S(2)}, u32[]{:S(2)}) collective-permute-start(bf16[64,2048]{1,0:T(8,128)(2,1)S(1)} %add_convert_fusion), channel_id=1, source_target_pairs={{4,8},{6,10},{8,4},{10,6},{5,9},{7,11},{9,5},{11,7},{20,24},{22,26... | collective-permute-start | bytes 786440 | tf_op jit(solution)/shard_map/ppermute | solution.py:43
  103.7 5.5 %collective-permute-start.15 = (bf16[64,2048]{1,0:T(8,128)(2,1)S(1)}, bf16[64,2048]{1,0:T(8,128)(2,1)S(1)}, u32[]{:S(2)}, u32[]{:S(2)}) collective-permute-start(bf16[64,2048]{1,0:T(8,128)(2,1)S(1)} %add_convert_fusion.1), channel_id=1, source_target_pairs={{4,8},{6,10},{8,4},{10,6},{5,9},{7,11},{9,5},{11,7},{20,24},{22,26... | collective-permute-start | bytes 786440 | tf_op jit(solution)/shard_map/ppermute | solution.py:43
  104.5 9.0 %collective-permute-start.20 = (bf16[64,2048]{1,0:T(8,128)(2,1)S(1)}, bf16[64,2048]{1,0:T(8,128)(2,1)S(1)}, u32[]{:S(2)}, u32[]{:S(2)}) collective-permute-start(bf16[64,2048]{1,0:T(8,128)(2,1)S(1)} %fusion.2), channel_id=1, source_target_pairs={{0,4},{2,6},{4,0},{6,2},{8,12},{10,14},{12,8},{14,10},{1,5},{3,7},... | collective-permute-start | bytes 786440 | tf_op jit(solution)/shard_map/ppermute | solution.py:43
  (1 other events, 2.7 us)

commit v2 on v1

--- a/solution.py
+++ b/solution.py
@@ -1,9 +1,12 @@
 import jax
 import jax.numpy as jnp
 from jax import lax
+from jax.experimental import pallas as pl
+from jax.experimental.pallas import tpu as pltpu
 from jax.sharding import PartitionSpec as P
 
 BLOCK = 128
+LIMIT = 16 << 20
 BF16 = jnp.bfloat16
 F32 = jnp.float32
 
@@ -48,19 +51,25 @@
     return (z == 1) | (z == 2)
 
 
-def gather(own):
+def after(value, *others):
+    return lax.optimization_barrier((value, *others))[0]
+
+
+def gather(own, early):
     pair = move(own, PAIR)
     near = move(own, MIDDLE)
     own_y = move(own, ACROSS)
     far = move(pair, MIDDLE)
     near_out = move(near, OUTWARD)
-    pair_y = move(pair, ACROSS)
+    pair_y = move(after(pair, own_y), ACROSS)
     near = jnp.where(inner(), near, near_out)
     far_out = move(far, OUTWARD)
-    near_y = move(near, ACROSS)
+    near_y = move(after(near, pair_y), ACROSS)
     far = jnp.where(inner(), far, far_out)
+    sums = early((own, own_y, pair, pair_y))
+    far, near_y, *sums = lax.optimization_barrier((far, near_y, *sums))
     far_y = move(far, ACROSS)
-    return own, own_y, pair, pair_y, near, near_y, far, far_y
+    return sums, (near, near_y, far, far_y)
 
 
 def add(a, b):
@@ -80,30 +89,138 @@
 
 
 SWAP = [(0, 1), (1, 0)]
+WHOLE = pl.BlockSpec(memory_space=pltpu.VMEM)
+SCALAR = pl.BlockSpec(memory_space=pltpu.SMEM)
+IN_HBM = pl.BlockSpec(memory_space=pltpu.HBM)
+PIECES = 8
+TILE = 512
+
+
+def swap(value):
+    return lax.ppermute(value, "seq", SWAP)
+
+
+def prune_kernel(mask, weight, out, arrived):
+    rows = out.shape[0] // PIECES
+    copies = [
+        pltpu.make_async_copy(
+            weight.at[pl.ds(i * rows, rows), :], out.at[pl.ds(i * rows, rows), :], arrived.at[i]
+        )
+        for i in range(PIECES)
+    ]
+    for copy in copies:
+        copy.start()
+    for i, copy in enumerate(copies):
+        copy.wait()
+        for k in range(rows // BLOCK):
+            at = i * rows + k * BLOCK
+
+            @pl.loop(0, out.shape[1] // BLOCK)
+            def _(j):
+                @pl.when(mask[at // BLOCK, j] == 0)
+                def _():
+                    columns = pl.ds(pl.multiple_of(j * BLOCK, BLOCK), BLOCK)
+                    out[at : at + BLOCK, columns] = jnp.zeros((BLOCK, BLOCK), BF16)
+
+
+def prune(weight, mask):
+    return pl.pallas_call(
+        prune_kernel,
+        out_shape=pltpu.VMEM(weight.shape, BF16),
+        in_specs=[SCALAR, IN_HBM],
+        out_specs=WHOLE,
+        scratch_shapes=[pltpu.SemaphoreType.DMA((PIECES,))],
+        compiler_params=pltpu.CompilerParams(vmem_limit_bytes=LIMIT),
+        cost_estimate=pl.CostEstimate(flops=0, bytes_accessed=2 * weight.size, transcendentals=0),
+        name="prune",
+    )(mask, pltpu.with_memory_space_constraint(weight, pltpu.HBM))
+
+
+def partial_kernel(core, *refs):
+    *blocks, gate_w, up_w, theirs, mine, lhs = refs
+    rows = blocks[0].shape[0]
+    half = len(blocks) // 2
+    for i, block in enumerate(blocks):
+        side = core[0] if i < half else 1 - core[0]
+        at = pl.multiple_of((1 - side) * half * rows + (i % half) * rows, rows)
+        lhs[pl.ds(at, rows), :] = block[...]
+
+    for which, weight in enumerate((gate_w, up_w)):
+
+        @pl.loop(0, weight.shape[1] // TILE)
+        def _(j):
+            columns = pl.ds(pl.multiple_of(j * TILE, TILE), TILE)
+            sums = dot(lhs[...], weight[:, columns])
+            theirs[which, :, columns] = sums[: half * rows]
+            mine[which, :, columns] = sums[half * rows :]
+
+
+def partials(core, blocks, gate_w, up_w):
+    rows = blocks[0].shape[0] * len(blocks)
+    depth, width = gate_w.shape
+    out = jax.ShapeDtypeStruct((2, rows // 2, width), F32)
+    return pl.pallas_call(
+        partial_kernel,
+        out_shape=[out, out],
+        in_specs=[SCALAR] + [WHOLE] * (len(blocks) + 2),
+        out_specs=[WHOLE, WHOLE],
+        scratch_shapes=[pltpu.VMEM((rows, depth), BF16)],
+        compiler_params=pltpu.CompilerParams(vmem_limit_bytes=LIMIT),
+        cost_estimate=pl.CostEstimate(flops=4 * rows * depth * width, bytes_accessed=2 * rows * depth, transcendentals=0),
+        name="partials",
+    )(core, *blocks, gate_w, up_w)
+
+
+def down_kernel(core, mine, theirs, weight, *refs):
+    outs, lhs = refs[:-1], refs[-1]
+    rows = outs[0].shape[0]
+    half = mine.shape[0]
+    lhs[pl.ds(pl.multiple_of(core[0] * half, half), half), :] = mine[...]
+    lhs[pl.ds(pl.multiple_of((1 - core[0]) * half, half), half), :] = theirs[...]
+
+    @pl.loop(0, weight.shape[1] // TILE)
+    def _(j):
+        columns = pl.ds(pl.multiple_of(j * TILE, TILE), TILE)
+        sums = dot(lhs[...], weight[:, columns]).astype(BF16)
+        for i, out in enumerate(outs):
+            out[:, columns] = sums[i * rows : (i + 1) * rows, :]
+
+
+def down_of(core, mine, theirs, weight, n):
+    half = mine.shape[0]
+    depth, width = weight.shape
+    return pl.pallas_call(
+        down_kernel,
+        out_shape=[jax.ShapeDtypeStruct((2 * half // n, width), BF16)] * n,
+        in_specs=[SCALAR, WHOLE, WHOLE, WHOLE],
+        out_specs=[WHOLE] * n,
+        scratch_shapes=[pltpu.VMEM((2 * half, depth), BF16)],
+        compiler_params=pltpu.CompilerParams(vmem_limit_bytes=LIMIT),
+        cost_estimate=pl.CostEstimate(flops=4 * half * depth * width, bytes_accessed=4 * half * depth, transcendentals=0),
+        name="down",
+    )(core, mine, theirs, weight)
 
 
 def lined(tokens, gate_weight, up_weight, down_weight, gate_mask, up_mask, down_mask):
-    rows = tokens.shape[0]
-    half = rows // 2
-    gate_pruned, up_pruned, down_pruned = lax.optimization_barrier(
-        (pruned(gate_weight, gate_mask), pruned(up_weight, up_mask), pruned(down_weight, down_mask))
-    )
-    core = lax.axis_index("seq")
-    gathered = jnp.stack(gather(tokens)).reshape(8, 2, half, -1)
-    theirs = lax.dynamic_index_in_dim(gathered, 1 - core, 1, keepdims=False).reshape(8 * half, -1)
-    mine = lax.dynamic_index_in_dim(gathered, core, 1, keepdims=False).reshape(8 * half, -1)
-    gate_sent = lax.ppermute(dot(theirs, gate_pruned).astype(BF16), "seq", SWAP)
-    up_sent = lax.ppermute(dot(theirs, up_pruned).astype(BF16), "seq", SWAP)
-    gate = dot(mine, gate_pruned) + gate_sent.astype(F32)
-    up = dot(mine, up_pruned) + up_sent.astype(F32)
-    hidden = (jax.nn.silu(gate) * up).astype(BF16)
-    other = lax.ppermute(hidden, "seq", SWAP)
-    parts_mine = dot(hidden, down_pruned).astype(BF16).reshape(8, half, -1)
-    parts_theirs = dot(other, down_pruned).astype(BF16).reshape(8, half, -1)
-    first = jnp.where(core == 0, parts_mine, parts_theirs)
-    second = jnp.where(core == 0, parts_theirs, parts_mine)
-    parts = jnp.stack([first, second], axis=1).reshape(8, rows, -1)
-    return scatter(*(parts[i] for i in range(8)))
+    core = jnp.reshape(lax.axis_index("seq"), (1,)).astype(jnp.int32)
+    gate_w, up_w, down_w = prune(gate_weight, gate_mask), prune(up_weight, up_mask), prune(down_weight, down_mask)
+
+    def hidden(theirs, mine):
+        gate, up = mine + swap(theirs)
+        return (jax.nn.silu(gate) * up).astype(BF16)
+
+    (theirs, mine), blocks = gather(tokens, lambda blocks: partials(core, blocks, gate_w, up_w))
+    first = hidden(theirs, mine)
+    *blocks, first, down_w = lax.optimization_barrier((*blocks, first, down_w))
+    first_in = swap(first)
+    theirs, mine = partials(core, blocks, gate_w, up_w)
+    theirs, first_in = lax.optimization_barrier((theirs, first_in))
+    theirs_sent = swap(theirs)
+    parts = down_of(core, first, first_in, down_w, 4)
+    gate, up = mine + theirs_sent
+    second = (jax.nn.silu(gate) * up).astype(BF16)
+    parts += down_of(core, second, swap(second), down_w, 4)
+    return scatter(*parts)
 
 
 def solution(mesh):

time: 115 us -> 121 us (1.052)
  Pallas kernels: 0 us -> 36.3 us
  other arithmetic: 24 us -> 2.55 us
  matrix products: 21.4 us -> 0 us
  waiting for transfers between devices: 36 us -> 49.8 us
  local copies, waits for them, and re-layouts: 4.58 us -> 0.71 us
  starting transfers between devices: 28 us -> 31.1 us
    pallas_call x0 -> x7, Pallas kernels: none -> 36.3 us  [the longest x3 18.7 us: prune(): pl.pallas_call(prune_kernel, out_shape=pltpu.VMEM(weight.shape, BF16), in...]
    dot_general x6 -> x0, matrix products: 21.4 us -> none  [dot(): return jnp.dot(a, b, preferred_element_type=F32)]
    mul x2 -> x0, other arithmetic: 20.3 us -> none  [pruned(): kept = shaped * mask.astype(BF16)[:, None, :, None]]
    ppermute x18, waiting for transfers between devices: 35.8 us -> 44.5 us  [move(): return lax.ppermute(value, 'tensor', perm)]
    ppermute x3 -> x4, waiting for transfers between devices: 0.23 us -> 5.33 us  [swap(): return lax.ppermute(value, 'seq', SWAP)]
    mul x3 -> x0, local copies, waits for them, and re-layouts: 3.43 us -> none  [pruned(): kept = shaped * mask.astype(BF16)[:, None, :, None]]
    ppermute x18, starting transfers between devices: 27.6 us -> 30 us  [move(): return lax.ppermute(value, 'tensor', perm)]
    convert_element_type x3 -> x2, other arithmetic: 2.1 us -> 0.59 us  [the longest x1 0.29 us: hidden(): return (jax.nn.silu(gate) * up).astype(BF16)]
  transfers between devices with their start and end apart: 21 -> 22, of which waited for: 8 -> 9; matrix products, arithmetic and copies ran while one was open for 32% -> 1% of each run, Pallas kernels for 0% -> 28%
where the time goes in v2:
time: 121 us
  waiting for transfers between devices  49.8 us (41%)
  Pallas kernels  36.3 us (30%)
  starting transfers between devices  31.1 us (26%)
  other arithmetic  2.55 us (2%)
    ppermute x18, waiting for transfers between devices, move(): return lax.ppermute(value, 'tensor', perm)  44.5 us
    ppermute x18, starting transfers between devices, move(): return lax.ppermute(value, 'tensor', perm)  30 us
    pallas_call x3, Pallas kernels, prune(): pl.pallas_call(prune_kernel, out_shape=pltpu.VMEM(weight.shape, BF16), in...  18.7 us
    pallas_call x2, Pallas kernels, partials(): pl.pallas_call(partial_kernel, out_shape=[out, out], in_specs=[SCALAR] +...  11.7 us
    pallas_call x2, Pallas kernels, down_of(): pl.pallas_call(down_kernel, out_shape=[jax.ShapeDtypeStruct((2 * half //...  5.9 us
    ppermute x4, waiting for transfers between devices, swap(): return lax.ppermute(value, 'seq', SWAP)  5.33 us
  transfers between devices with their start and end apart: 22, of which 9 were waited for; matrix products, arithmetic and copies ran while one was open for 1% of the time, Pallas kernels for 28%

profile of v2, /device:TPU:0, one launch (start us, length us, event | category | flops | bytes accessed | tf_op | source)
XLA Modules:
  0.0 120.8 jit_solution(10656554422344988791)
XLA Ops:
  0.7 5.9 %collective-permute-start.2 = (bf16[64,2048]{1,0:T(8,128)(2,1)}, bf16[64,2048]{1,0:T(8,128)(2,1)S(1)}, u32[]{:S(2)}, u32[]{:S(2)}) collective-permute-start(bf16[64,2048]{1,0:T(8,128)(2,1)} %refs_0_.1), channel_id=1, source_target_pairs={{0,4},{2,6},{4,0},{6,2},{8,12},{10,14},{12,8},{14,10},{1,5},{3,7},... | collective-permute-start | bytes 786440 | tf_op jit(solution)/shard_map/ppermute | solution.py:46
  6.6 1.5 %collective-permute-start.5 = (bf16[64,2048]{1,0:T(8,128)(2,1)}, bf16[64,2048]{1,0:T(8,128)(2,1)S(1)}, u32[]{:S(2)}, u32[]{:S(2)}) collective-permute-start(bf16[64,2048]{1,0:T(8,128)(2,1)} %refs_0_.1), channel_id=1, source_target_pairs={{0,2},{2,0},{4,6},{6,4},{8,10},{10,8},{12,14},{14,12},{1,3},{3,1},... | collective-permute-start | bytes 786440 | tf_op jit(solution)/shard_map/ppermute | solution.py:46
  8.1 1.3 %collective-permute-start.1 = (bf16[64,2048]{1,0:T(8,128)(2,1)S(1)}, bf16[64,2048]{1,0:T(8,128)(2,1)S(1)}, u32[]{:S(2)}, u32[]{:S(2)}) collective-permute-start(bf16[64,2048]{1,0:T(8,128)(2,1)S(1)} %collective-permute-done), channel_id=1, source_target_pairs={{4,0},{6,2},{8,12},{10,14},{5,1},{7,3},{9,13},{11,15},{20,16},{22,... | collective-permute-start | bytes 786440 | tf_op jit(solution)/shard_map/ppermute | solution.py:46
  10.1 6.2 %prune.3.refs_4_ = bf16[2048,2048]{1,0:T(8,128)(2,1)S(1)} custom-call(s32[16,16]{1,0:T(8,128)S(1)} %copy-done.1, bf16[2048,2048]{1,0:T(8,128)(2,1)} %weight.3), custom_call_target="tpu_custom_call" | custom-call | bytes 8388608 | tf_op jit(solution)/shard_map/prune/pallas_call | solution.py:127
  16.4 6.2 %prune.4.refs_5_ = bf16[2048,2048]{1,0:T(8,128)(2,1)S(1)} custom-call(s32[16,16]{1,0:T(8,128)S(1)} %copy-done.2, bf16[2048,2048]{1,0:T(8,128)(2,1)} %weight.4), custom_call_target="tpu_custom_call" | custom-call | bytes 8388608 | tf_op jit(solution)/shard_map/prune/pallas_call | solution.py:127
  23.8 6.1 %collective-permute-done.6.refs_3_ = bf16[64,2048]{1,0:T(8,128)(2,1)S(1)} collective-permute-done((bf16[64,2048]{1,0:T(8,128)(2,1)S(1)}, bf16[64,2048]{1,0:T(8,128)(2,1)S(1)}, u32[]{:S(2)}, u32[]{:S(2)}) %collective-permute-start.6) | collective-permute-done | bytes 262176 | tf_op jit(solution)/shard_map/ppermute | solution.py:46
  31.5 5.8 %partials.2 = (f32[2,128,2048]{2,1,0:T(8,128)S(1)}, f32[2,128,2048]{2,1,0:T(8,128)S(1)}) custom-call(s32[1]{0:T(128)} %bitcast.core, bf16[64,2048]{1,0:T(8,128)(2,1)S(1)} %copy-done, bf16[64,2048]{1,0:T(8,128)(2,1)S(1)} %collective-permute-done.5.refs_1_, bf16[64,2048]{1,0:T(8,128)(2,1)S(1)} %collective-permute-done.2.refs_2_, ...), custom_call_target="tpu_custom_call" | custom-call | flops 4294967296 | bytes 1048576 | tf_op jit(solution)/shard_map/partials/pallas_call | solution.py:162
  37.4 6.3 %collective-permute-done.4 = bf16[64,2048]{1,0:T(8,128)(2,1)S(1)} collective-permute-done((bf16[64,2048]{1,0:T(8,128)(2,1)S(1)}, bf16[64,2048]{1,0:T(8,128)(2,1)S(1)}, u32[]{:S(2)}, u32[]{:S(2)}) %collective-permute-start.4) | collective-permute-done | bytes 262176 | tf_op jit(solution)/shard_map/ppermute | solution.py:46
  43.8 6.2 %prune.5.weight = bf16[2048,2048]{1,0:T(8,128)(2,1)S(1)} custom-call(s32[16,16]{1,0:T(8,128)S(1)} %copy-done.3, bf16[2048,2048]{1,0:T(8,128)(2,1)} %weight.5), custom_call_target="tpu_custom_call" | custom-call | bytes 8388608 | tf_op jit(solution)/shard_map/prune/pallas_call | solution.py:127
  51.0 7.8 %collective-permute-done.8.refs_3_ = bf16[64,2048]{1,0:T(8,128)(2,1)S(1)} collective-permute-done((bf16[64,2048]{1,0:T(8,128)(2,1)S(1)}, bf16[64,2048]{1,0:T(8,128)(2,1)S(1)}, u32[]{:S(2)}, u32[]{:S(2)}) %collective-permute-start.8) | collective-permute-done | bytes 262176 | tf_op jit(solution)/shard_map/ppermute | solution.py:46
  58.8 5.8 %partials.3 = (f32[2,128,2048]{2,1,0:T(8,128)S(1)}, f32[2,128,2048]{2,1,0:T(8,128)S(1)}) custom-call(s32[1]{0:T(128)} %bitcast.core, bf16[64,2048]{1,0:T(8,128)(2,1)S(1)} %broadcast_select_fusion.1.refs_0_, bf16[64,2048]{1,0:T(8,128)(2,1)S(1)} %collective-permute-done.7.refs_1_, bf16[64,2048]{1,0:T(8,128)(2,1)S(1)} %broadcast_select_fusion.refs_2_, ...), custom_call_target="tpu_custom_call" | custom-call | flops 4294967296 | bytes 1048576 | tf_op jit(solution)/shard_map/partials/pallas_call | solution.py:162
  65.3 3.8 %collective-permute-done.12 = f32[2,128,2048]{2,1,0:T(8,128)S(1)} collective-permute-done((f32[2,128,2048]{2,1,0:T(8,128)S(1)}, f32[2,128,2048]{2,1,0:T(8,128)S(1)}, u32[]{:S(2)}, u32[]{:S(2)}) %collective-permute-start.12) | collective-permute-done | bytes 2097184 | tf_op jit(solution)/shard_map/ppermute | solution.py:100
  70.1 1.5 %collective-permute-done.13.theirs = bf16[128,2048]{1,0:T(8,128)(2,1)S(1)} collective-permute-done((bf16[128,2048]{1,0:T(8,128)(2,1)S(1)}, bf16[128,2048]{1,0:T(8,128)(2,1)S(1)}, u32[]{:S(2)}, u32[]{:S(2)}) %collective-permute-start.13) | collective-permute-done | bytes 524320 | tf_op jit(solution)/shard_map/ppermute | solution.py:100
  71.7 2.9 %down.3 = (bf16[64,2048]{1,0:T(8,128)(2,1)S(1)}, bf16[64,2048]{1,0:T(8,128)(2,1)S(1)}, bf16[64,2048]{1,0:T(8,128)(2,1)S(1)}, bf16[64,2048]{1,0:T(8,128)(2,1)S(1)}) custom-call(s32[1]{0:T(128)} %bitcast.core, bf16[128,2048]{1,0:T(8,128)(2,1)S(1)} %fusion.1.mine, bf16[128,2048]{1,0:T(8,128)(2,1)S(1)} %collective-permute-done.13.theirs, ...), custom_call_target="tpu_custom_call" | custom-call | flops 2147483648 | bytes 1048576 | tf_op jit(solution)/shard_map/down/pallas_call | solution.py:192
  75.1 3.0 %down.2 = (bf16[64,2048]{1,0:T(8,128)(2,1)S(1)}, bf16[64,2048]{1,0:T(8,128)(2,1)S(1)}, bf16[64,2048]{1,0:T(8,128)(2,1)S(1)}, bf16[64,2048]{1,0:T(8,128)(2,1)S(1)}) custom-call(s32[1]{0:T(128)} %bitcast.core, bf16[128,2048]{1,0:T(8,128)(2,1)S(1)} %fusion.3.mine, bf16[128,2048]{1,0:T(8,128)(2,1)S(1)} %collective-permute-done.10.theirs, ...), custom_call_target="tpu_custom_call" | custom-call | flops 2147483648 | bytes 1048576 | tf_op jit(solution)/shard_map/down/pallas_call | solution.py:192
  78.1 1.7 %collective-permute-start.11 = (bf16[64,2048]{1,0:T(8,128)(2,1)S(1)}, bf16[64,2048]{1,0:T(8,128)(2,1)S(1)}, u32[]{:S(2)}, u32[]{:S(2)}) collective-permute-start(bf16[64,2048]{1,0:T(8,128)(2,1)S(1)} %get-tuple-element.48), channel_id=1, source_target_pairs={{0,2},{2,0},{4,6},{6,4},{8,10},{10,8},{12,14},{14,12},{1,3},{3,1},... | collective-permute-start | bytes 786440 | tf_op jit(solution)/shard_map/ppermute | solution.py:46
  80.2 1.6 %collective-permute-start.14 = (bf16[64,2048]{1,0:T(8,128)(2,1)S(1)}, bf16[64,2048]{1,0:T(8,128)(2,1)S(1)}, u32[]{:S(2)}, u32[]{:S(2)}) collective-permute-start(bf16[64,2048]{1,0:T(8,128)(2,1)S(1)} %get-tuple-element.52), channel_id=1, source_target_pairs={{0,2},{2,0},{4,6},{6,4},{8,10},{10,8},{12,14},{14,12},{1,3},{3,1},... | collective-permute-start | bytes 786440 | tf_op jit(solution)/shard_map/ppermute | solution.py:46
  81.8 2.0 %collective-permute-done.18 = bf16[64,2048]{1,0:T(8,128)(2,1)S(1)} collective-permute-done((bf16[64,2048]{1,0:T(8,128)(2,1)S(1)}, bf16[64,2048]{1,0:T(8,128)(2,1)S(1)}, u32[]{:S(2)}, u32[]{:S(2)}) %collective-permute-start.18) | collective-permute-done | bytes 262176 | tf_op jit(solution)/shard_map/ppermute | solution.py:46
  83.9 3.3 %collective-permute-start.19 = (bf16[64,2048]{1,0:T(8,128)(2,1)S(1)}, bf16[64,2048]{1,0:T(8,128)(2,1)S(1)}, u32[]{:S(2)}, u32[]{:S(2)}) collective-permute-start(bf16[64,2048]{1,0:T(8,128)(2,1)S(1)} %add_convert_fusion.3), channel_id=1, source_target_pairs={{0,4},{2,6},{12,8},{14,10},{1,5},{3,7},{13,9},{15,11},{16,20},{18,... | collective-permute-start | bytes 786440 | tf_op jit(solution)/shard_map/ppermute | solution.py:46
  87.3 12.9 %collective-permute-done.14 = bf16[64,2048]{1,0:T(8,128)(2,1)S(1)} collective-permute-done((bf16[64,2048]{1,0:T(8,128)(2,1)S(1)}, bf16[64,2048]{1,0:T(8,128)(2,1)S(1)}, u32[]{:S(2)}, u32[]{:S(2)}) %collective-permute-start.14) | collective-permute-done | bytes 262176 | tf_op jit(solution)/shard_map/ppermute | solution.py:46
  100.2 3.3 %collective-permute-start.15 = (bf16[64,2048]{1,0:T(8,128)(2,1)S(1)}, bf16[64,2048]{1,0:T(8,128)(2,1)S(1)}, u32[]{:S(2)}, u32[]{:S(2)}) collective-permute-start(bf16[64,2048]{1,0:T(8,128)(2,1)S(1)} %add_convert_fusion.5), channel_id=1, source_target_pairs={{0,4},{2,6},{12,8},{14,10},{1,5},{3,7},{13,9},{15,11},{16,20},{18,... | collective-permute-start | bytes 786440 | tf_op jit(solution)/shard_map/ppermute | solution.py:46
  104.3 4.5 %collective-permute-done.15 = bf16[64,2048]{1,0:T(8,128)(2,1)S(1)} collective-permute-done((bf16[64,2048]{1,0:T(8,128)(2,1)S(1)}, bf16[64,2048]{1,0:T(8,128)(2,1)S(1)}, u32[]{:S(2)}, u32[]{:S(2)}) %collective-permute-start.15) | collective-permute-done | bytes 262176 | tf_op jit(solution)/shard_map/ppermute | solution.py:46
  109.7 5.4 %collective-permute-start.21 = (bf16[64,2048]{1,0:T(8,128)(2,1)S(1)}, bf16[64,2048]{1,0:T(8,128)(2,1)S(1)}, u32[]{:S(2)}, u32[]{:S(2)}) collective-permute-start(bf16[64,2048]{1,0:T(8,128)(2,1)S(1)} %add_convert_fusion.1), channel_id=1, source_target_pairs={{0,4},{2,6},{4,0},{6,2},{8,12},{10,14},{12,8},{14,10},{1,5},{3,7},... | collective-permute-start | bytes 786440 | tf_op jit(solution)/shard_map/ppermute | solution.py:46
  115.1 4.8 %collective-permute-done.21 = bf16[64,2048]{1,0:T(8,128)(2,1)S(1)} collective-permute-done((bf16[64,2048]{1,0:T(8,128)(2,1)S(1)}, bf16[64,2048]{1,0:T(8,128)(2,1)S(1)}, u32[]{:S(2)}, u32[]{:S(2)}) %collective-permute-start.21) | collective-permute-done | bytes 262176 | tf_op jit(solution)/shard_map/ppermute | solution.py:46
  (47 shorter events, 10.3 us)
Async XLA Ops:
  0.0 8.1 %collective-permute-start = (bf16[64,2048]{1,0:T(8,128)(2,1)}, bf16[64,2048]{1,0:T(8,128)(2,1)S(1)}, u32[]{:S(2)}, u32[]{:S(2)}) collective-permute-start(bf16[64,2048]{1,0:T(8,128)(2,1)} %refs_0_.1), channel_id=1, source_target_pairs={{4,8},{6,10},{8,4},{10,6},{5,9},{7,11},{9,5},{11,7},{20,24},{22,26... | collective-permute-start | bytes 786440 | tf_op jit(solution)/shard_map/ppermute | solution.py:46
  0.7 21.9 %collective-permute-start.2 = (bf16[64,2048]{1,0:T(8,128)(2,1)}, bf16[64,2048]{1,0:T(8,128)(2,1)S(1)}, u32[]{:S(2)}, u32[]{:S(2)}) collective-permute-start(bf16[64,2048]{1,0:T(8,128)(2,1)} %refs_0_.1), channel_id=1, source_target_pairs={{0,4},{2,6},{4,0},{6,2},{8,12},{10,14},{12,8},{14,10},{1,5},{3,7},... | collective-permute-start | bytes 786440 | tf_op jit(solution)/shard_map/ppermute | solution.py:46
  6.6 16.0 %collective-permute-start.5 = (bf16[64,2048]{1,0:T(8,128)(2,1)}, bf16[64,2048]{1,0:T(8,128)(2,1)S(1)}, u32[]{:S(2)}, u32[]{:S(2)}) collective-permute-start(bf16[64,2048]{1,0:T(8,128)(2,1)} %refs_0_.1), channel_id=1, source_target_pairs={{0,2},{2,0},{4,6},{6,4},{8,10},{10,8},{12,14},{14,12},{1,3},{3,1},... | collective-permute-start | bytes 786440 | tf_op jit(solution)/shard_map/ppermute | solution.py:46
  8.1 15.6 %collective-permute-start.1 = (bf16[64,2048]{1,0:T(8,128)(2,1)S(1)}, bf16[64,2048]{1,0:T(8,128)(2,1)S(1)}, u32[]{:S(2)}, u32[]{:S(2)}) collective-permute-start(bf16[64,2048]{1,0:T(8,128)(2,1)S(1)} %collective-permute-done), channel_id=1, source_target_pairs={{4,0},{6,2},{8,12},{10,14},{5,1},{7,3},{9,13},{11,15},{20,16},{22,... | collective-permute-start | bytes 786440 | tf_op jit(solution)/shard_map/ppermute | solution.py:46
  16.4 15.1 %copy-start = (bf16[64,2048]{1,0:T(8,128)(2,1)S(1)}, bf16[64,2048]{1,0:T(8,128)(2,1)}, u32[]{:S(2)}) copy-start(bf16[64,2048]{1,0:T(8,128)(2,1)} %refs_0_.1) | copy-start | bytes 786436
  22.6 7.3 %collective-permute-start.6 = (bf16[64,2048]{1,0:T(8,128)(2,1)S(1)}, bf16[64,2048]{1,0:T(8,128)(2,1)S(1)}, u32[]{:S(2)}, u32[]{:S(2)}) collective-permute-start(bf16[64,2048]{1,0:T(8,128)(2,1)S(1)} %collective-permute-done.2.refs_2_), channel_id=1, source_target_pairs={{0,2},{2,0},{4,6},{6,4},{8,10},{10,8},{12,14},{14,12},{1,3},{3,1},... | collective-permute-start | bytes 786440 | tf_op jit(solution)/shard_map/ppermute | solution.py:46
  23.1 7.1 %collective-permute-start.3 = (bf16[64,2048]{1,0:T(8,128)(2,1)S(1)}, bf16[64,2048]{1,0:T(8,128)(2,1)S(1)}, u32[]{:S(2)}, u32[]{:S(2)}) collective-permute-start(bf16[64,2048]{1,0:T(8,128)(2,1)S(1)} %collective-permute-done.2.refs_2_), channel_id=1, source_target_pairs={{4,8},{6,10},{8,4},{10,6},{5,9},{7,11},{9,5},{11,7},{20,24},{22,26... | collective-permute-start | bytes 786440 | tf_op jit(solution)/shard_map/ppermute | solution.py:46
  29.9 13.8 %collective-permute-start.7 = (bf16[64,2048]{1,0:T(8,128)(2,1)S(1)}, bf16[64,2048]{1,0:T(8,128)(2,1)S(1)}, u32[]{:S(2)}, u32[]{:S(2)}) collective-permute-start(bf16[64,2048]{1,0:T(8,128)(2,1)S(1)} %broadcast_select_fusion.1.refs_0_), channel_id=1, source_target_pairs={{0,2},{2,0},{4,6},{6,4},{8,10},{10,8},{12,14},{14,12},{1,3},{3,1},... | collective-permute-start | bytes 786440 | tf_op jit(solution)/shard_map/ppermute | solution.py:46
  30.2 13.5 %collective-permute-start.4 = (bf16[64,2048]{1,0:T(8,128)(2,1)S(1)}, bf16[64,2048]{1,0:T(8,128)(2,1)S(1)}, u32[]{:S(2)}, u32[]{:S(2)}) collective-permute-start(bf16[64,2048]{1,0:T(8,128)(2,1)S(1)} %collective-permute-done.3), channel_id=1, source_target_pairs={{4,0},{6,2},{8,12},{10,14},{5,1},{7,3},{9,13},{11,15},{20,16},{22,... | collective-permute-start | bytes 786440 | tf_op jit(solution)/shard_map/ppermute | solution.py:46
  31.5 12.3 %copy-start.3 = (s32[16,16]{1,0:T(8,128)S(1)}, s32[16,16]{1,0:T(8,128)}, u32[]{:S(2)}) copy-start(s32[16,16]{1,0:T(8,128)} %mask.5) | copy-start | bytes 3076
  43.7 6.7 %collective-permute-start.9 = (f32[2,128,2048]{2,1,0:T(8,128)S(1)}, f32[2,128,2048]{2,1,0:T(8,128)S(1)}, u32[]{:S(2)}, u32[]{:S(2)}) collective-permute-start(f32[2,128,2048]{2,1,0:T(8,128)S(1)} %get-tuple-element.38), channel_id=1, source_target_pairs={{0,1},{1,0},{2,3},{3,2},{4,5},{5,4},{6,7},{7,6},{8,9},{9,8},{10,11... | collective-permute-start | bytes 6291464 | tf_op jit(solution)/shard_map/ppermute | solution.py:100
  50.0 8.8 %collective-permute-start.8 = (bf16[64,2048]{1,0:T(8,128)(2,1)S(1)}, bf16[64,2048]{1,0:T(8,128)(2,1)S(1)}, u32[]{:S(2)}, u32[]{:S(2)}) collective-permute-start(bf16[64,2048]{1,0:T(8,128)(2,1)S(1)} %broadcast_select_fusion.refs_2_), channel_id=1, source_target_pairs={{0,2},{2,0},{4,6},{6,4},{8,10},{10,8},{12,14},{14,12},{1,3},{3,1},... | collective-permute-start | bytes 786440 | tf_op jit(solution)/shard_map/ppermute | solution.py:46
  58.8 5.8 %collective-permute-start.10 = (bf16[128,2048]{1,0:T(8,128)(2,1)S(1)}, bf16[128,2048]{1,0:T(8,128)(2,1)S(1)}, u32[]{:S(2)}, u32[]{:S(2)}) collective-permute-start(bf16[128,2048]{1,0:T(8,128)(2,1)S(1)} %fusion.3.mine), channel_id=1, source_target_pairs={{0,1},{1,0},{2,3},{3,2},{4,5},{5,4},{6,7},{7,6},{8,9},{9,8},{10,11... | collective-permute-start | bytes 1572872 | tf_op jit(solution)/shard_map/ppermute | solution.py:100
  64.7 4.4 %collective-permute-start.12 = (f32[2,128,2048]{2,1,0:T(8,128)S(1)}, f32[2,128,2048]{2,1,0:T(8,128)S(1)}, u32[]{:S(2)}, u32[]{:S(2)}) collective-permute-start(f32[2,128,2048]{2,1,0:T(8,128)S(1)} %get-tuple-element.50), channel_id=1, source_target_pairs={{0,1},{1,0},{2,3},{3,2},{4,5},{5,4},{6,7},{7,6},{8,9},{9,8},{10,11... | collective-permute-start | bytes 6291464 | tf_op jit(solution)/shard_map/ppermute | solution.py:100
  69.7 2.0 %collective-permute-start.13 = (bf16[128,2048]{1,0:T(8,128)(2,1)S(1)}, bf16[128,2048]{1,0:T(8,128)(2,1)S(1)}, u32[]{:S(2)}, u32[]{:S(2)}) collective-permute-start(bf16[128,2048]{1,0:T(8,128)(2,1)S(1)} %fusion.1.mine), channel_id=1, source_target_pairs={{0,1},{1,0},{2,3},{3,2},{4,5},{5,4},{6,7},{7,6},{8,9},{9,8},{10,11... | collective-permute-start | bytes 1572872 | tf_op jit(solution)/shard_map/ppermute | solution.py:100
  74.6 9.2 %collective-permute-start.18 = (bf16[64,2048]{1,0:T(8,128)(2,1)S(1)}, bf16[64,2048]{1,0:T(8,128)(2,1)S(1)}, u32[]{:S(2)}, u32[]{:S(2)}) collective-permute-start(bf16[64,2048]{1,0:T(8,128)(2,1)S(1)} %get-tuple-element.56), channel_id=1, source_target_pairs={{0,2},{2,0},{4,6},{6,4},{8,10},{10,8},{12,14},{14,12},{1,3},{3,1},... | collective-permute-start | bytes 786440 | tf_op jit(solution)/shard_map/ppermute | solution.py:46
  78.1 37.0 %collective-permute-start.11 = (bf16[64,2048]{1,0:T(8,128)(2,1)S(1)}, bf16[64,2048]{1,0:T(8,128)(2,1)S(1)}, u32[]{:S(2)}, u32[]{:S(2)}) collective-permute-start(bf16[64,2048]{1,0:T(8,128)(2,1)S(1)} %get-tuple-element.48), channel_id=1, source_target_pairs={{0,2},{2,0},{4,6},{6,4},{8,10},{10,8},{12,14},{14,12},{1,3},{3,1},... | collective-permute-start | bytes 786440 | tf_op jit(solution)/shard_map/ppermute | solution.py:46
  79.8 29.8 %collective-permute-start.17 = (bf16[64,2048]{1,0:T(8,128)(2,1)S(1)}, bf16[64,2048]{1,0:T(8,128)(2,1)S(1)}, u32[]{:S(2)}, u32[]{:S(2)}) collective-permute-start(bf16[64,2048]{1,0:T(8,128)(2,1)S(1)} %get-tuple-element.54), channel_id=1, source_target_pairs={{0,2},{2,0},{4,6},{6,4},{8,10},{10,8},{12,14},{14,12},{1,3},{3,1},... | collective-permute-start | bytes 786440 | tf_op jit(solution)/shard_map/ppermute | solution.py:46
  80.2 20.0 %collective-permute-start.14 = (bf16[64,2048]{1,0:T(8,128)(2,1)S(1)}, bf16[64,2048]{1,0:T(8,128)(2,1)S(1)}, u32[]{:S(2)}, u32[]{:S(2)}) collective-permute-start(bf16[64,2048]{1,0:T(8,128)(2,1)S(1)} %get-tuple-element.52), channel_id=1, source_target_pairs={{0,2},{2,0},{4,6},{6,4},{8,10},{10,8},{12,14},{14,12},{1,3},{3,1},... | collective-permute-start | bytes 786440 | tf_op jit(solution)/shard_map/ppermute | solution.py:46
  83.9 19.7 %collective-permute-start.19 = (bf16[64,2048]{1,0:T(8,128)(2,1)S(1)}, bf16[64,2048]{1,0:T(8,128)(2,1)S(1)}, u32[]{:S(2)}, u32[]{:S(2)}) collective-permute-start(bf16[64,2048]{1,0:T(8,128)(2,1)S(1)} %add_convert_fusion.3), channel_id=1, source_target_pairs={{0,4},{2,6},{12,8},{14,10},{1,5},{3,7},{13,9},{15,11},{16,20},{18,... | collective-permute-start | bytes 786440 | tf_op jit(solution)/shard_map/ppermute | solution.py:46
  100.2 8.6 %collective-permute-start.15 = (bf16[64,2048]{1,0:T(8,128)(2,1)S(1)}, bf16[64,2048]{1,0:T(8,128)(2,1)S(1)}, u32[]{:S(2)}, u32[]{:S(2)}) collective-permute-start(bf16[64,2048]{1,0:T(8,128)(2,1)S(1)} %add_convert_fusion.5), channel_id=1, source_target_pairs={{0,4},{2,6},{12,8},{14,10},{1,5},{3,7},{13,9},{15,11},{16,20},{18,... | collective-permute-start | bytes 786440 | tf_op jit(solution)/shard_map/ppermute | solution.py:46
  103.7 5.9 %collective-permute-start.20 = (bf16[64,2048]{1,0:T(8,128)(2,1)S(1)}, bf16[64,2048]{1,0:T(8,128)(2,1)S(1)}, u32[]{:S(2)}, u32[]{:S(2)}) collective-permute-start(bf16[64,2048]{1,0:T(8,128)(2,1)S(1)} %add_convert_fusion.2), channel_id=1, source_target_pairs={{4,8},{6,10},{8,4},{10,6},{5,9},{7,11},{9,5},{11,7},{20,24},{22,26... | collective-permute-start | bytes 786440 | tf_op jit(solution)/shard_map/ppermute | solution.py:46
  108.9 6.2 %collective-permute-start.16 = (bf16[64,2048]{1,0:T(8,128)(2,1)S(1)}, bf16[64,2048]{1,0:T(8,128)(2,1)S(1)}, u32[]{:S(2)}, u32[]{:S(2)}) collective-permute-start(bf16[64,2048]{1,0:T(8,128)(2,1)S(1)} %add_convert_fusion.4), channel_id=1, source_target_pairs={{4,8},{6,10},{8,4},{10,6},{5,9},{7,11},{9,5},{11,7},{20,24},{22,26... | collective-permute-start | bytes 786440 | tf_op jit(solution)/shard_map/ppermute | solution.py:46
  109.7 10.2 %collective-permute-start.21 = (bf16[64,2048]{1,0:T(8,128)(2,1)S(1)}, bf16[64,2048]{1,0:T(8,128)(2,1)S(1)}, u32[]{:S(2)}, u32[]{:S(2)}) collective-permute-start(bf16[64,2048]{1,0:T(8,128)(2,1)S(1)} %add_convert_fusion.1), channel_id=1, source_target_pairs={{0,4},{2,6},{4,0},{6,2},{8,12},{10,14},{12,8},{14,10},{1,5},{3,7},... | collective-permute-start | bytes 786440 | tf_op jit(solution)/shard_map/ppermute | solution.py:46
  (2 other events, 7.0 us)

commit v3 on v1

--- a/solution.py
+++ b/solution.py
@@ -1,9 +1,12 @@
 import jax
 import jax.numpy as jnp
 from jax import lax
+from jax.experimental import pallas as pl
+from jax.experimental.pallas import tpu as pltpu
 from jax.sharding import PartitionSpec as P
 
 BLOCK = 128
+LIMIT = 16 << 20
 BF16 = jnp.bfloat16
 F32 = jnp.float32
 
@@ -48,19 +51,26 @@
     return (z == 1) | (z == 2)
 
 
-def gather(own):
+def after(value, *others):
+    return lax.optimization_barrier((value, *others))[0]
+
+
+def gather(own, early):
     pair = move(own, PAIR)
     near = move(own, MIDDLE)
     own_y = move(own, ACROSS)
     far = move(pair, MIDDLE)
     near_out = move(near, OUTWARD)
-    pair_y = move(pair, ACROSS)
+    pair_y = move(after(pair, own_y), ACROSS)
     near = jnp.where(inner(), near, near_out)
+    far_first = far
     far_out = move(far, OUTWARD)
-    near_y = move(near, ACROSS)
+    near_y = move(after(near, pair_y), ACROSS)
     far = jnp.where(inner(), far, far_out)
+    sums = early((own, own_y, pair, after(pair_y, far_first)))
+    far, near_y, *sums = lax.optimization_barrier((far, near_y, *sums))
     far_y = move(far, ACROSS)
-    return own, own_y, pair, pair_y, near, near_y, far, far_y
+    return sums, (near, near_y, far, far_y)
 
 
 def add(a, b):
@@ -68,42 +78,102 @@
 
 
 def scatter(own, own_y, pair, pair_y, near, near_y, far, far_y):
-    far_s = add(far, move(far_y, ACROSS)).astype(BF16)
-    near_s = add(near, move(near_y, ACROSS)).astype(BF16)
-    pair_s = add(pair, move(pair_y, ACROSS))
-    own_s = add(own, move(own_y, ACROSS))
+    far_in = move(far_y, ACROSS)
+    near_in = move(near_y, ACROSS)
+    pair_in = move(after(pair_y, far_in), ACROSS)
+    own_in = move(after(own_y, near_in), ACROSS)
+    far_s = add(far, far_in).astype(BF16)
+    near_s = add(after(near, far_s), near_in).astype(BF16)
     far_s = add(far_s, move(far_s, INWARD)).astype(BF16)
     near_s = add(near_s, move(near_s, INWARD)).astype(BF16)
-    pair_s = add(pair_s, move(far_s, MIDDLE)).astype(BF16)
-    own_s = add(own_s, move(near_s, MIDDLE))
+    pair_s = (add(pair, pair_in) + move(far_s, MIDDLE).astype(F32)).astype(BF16)
+    own_s = add(own, own_in) + move(near_s, MIDDLE).astype(F32)
     return add(own_s, move(pair_s, PAIR)).astype(BF16)
 
 
 SWAP = [(0, 1), (1, 0)]
+WHOLE = pl.BlockSpec(memory_space=pltpu.VMEM)
+SCALAR = pl.BlockSpec(memory_space=pltpu.SMEM)
+IN_HBM = pl.BlockSpec(memory_space=pltpu.HBM)
+PIECES = 8
+
+
+def swap(value):
+    return lax.ppermute(value, "seq", SWAP)
+
+
+def prune_kernel(mask, weight, out, arrived):
+    rows = out.shape[0] // PIECES
+    copies = [
+        pltpu.make_async_copy(
+            weight.at[pl.ds(i * rows, rows), :], out.at[pl.ds(i * rows, rows), :], arrived.at[i]
+        )
+        for i in range(PIECES)
+    ]
+    for copy in copies:
+        copy.start()
+    for i, copy in enumerate(copies):
+        copy.wait()
+        for k in range(i * rows // BLOCK, (i + 1) * rows // BLOCK):
+            for j in range(out.shape[1] // BLOCK):
+
+                @pl.when(mask[k, j] == 0)
+                def _():
+                    at = (slice(k * BLOCK, (k + 1) * BLOCK), slice(j * BLOCK, (j + 1) * BLOCK))
+                    out[at] = jnp.zeros((BLOCK, BLOCK), BF16)
+
+
+def prune(weight, mask):
+    return pl.pallas_call(
+        prune_kernel,
+        out_shape=pltpu.VMEM(weight.shape, BF16),
+        in_specs=[SCALAR, IN_HBM],
+        out_specs=WHOLE,
+        scratch_shapes=[pltpu.SemaphoreType.DMA((PIECES,))],
+        compiler_params=pltpu.CompilerParams(vmem_limit_bytes=LIMIT),
+        cost_estimate=pl.CostEstimate(flops=0, bytes_accessed=2 * weight.size, transcendentals=0),
+        name="prune",
+    )(mask, pltpu.with_memory_space_constraint(weight, pltpu.HBM))
+
+
+def of_core(core, first, second):
+    return jnp.where(core == 0, first, second)
 
 
 def lined(tokens, gate_weight, up_weight, down_weight, gate_mask, up_mask, down_mask):
-    rows = tokens.shape[0]
-    half = rows // 2
-    gate_pruned, up_pruned, down_pruned = lax.optimization_barrier(
-        (pruned(gate_weight, gate_mask), pruned(up_weight, up_mask), pruned(down_weight, down_mask))
-    )
     core = lax.axis_index("seq")
-    gathered = jnp.stack(gather(tokens)).reshape(8, 2, half, -1)
-    theirs = lax.dynamic_index_in_dim(gathered, 1 - core, 1, keepdims=False).reshape(8 * half, -1)
-    mine = lax.dynamic_index_in_dim(gathered, core, 1, keepdims=False).reshape(8 * half, -1)
-    gate_sent = lax.ppermute(dot(theirs, gate_pruned).astype(BF16), "seq", SWAP)
-    up_sent = lax.ppermute(dot(theirs, up_pruned).astype(BF16), "seq", SWAP)
-    gate = dot(mine, gate_pruned) + gate_sent.astype(F32)
-    up = dot(mine, up_pruned) + up_sent.astype(F32)
-    hidden = (jax.nn.silu(gate) * up).astype(BF16)
-    other = lax.ppermute(hidden, "seq", SWAP)
-    parts_mine = dot(hidden, down_pruned).astype(BF16).reshape(8, half, -1)
-    parts_theirs = dot(other, down_pruned).astype(BF16).reshape(8, half, -1)
-    first = jnp.where(core == 0, parts_mine, parts_theirs)
-    second = jnp.where(core == 0, parts_theirs, parts_mine)
-    parts = jnp.stack([first, second], axis=1).reshape(8, rows, -1)
-    return scatter(*(parts[i] for i in range(8)))
+    weights = []
+
+    def halves(blocks):
+        n = len(blocks) // 2
+        low, high = jnp.concatenate(blocks[:n]), jnp.concatenate(blocks[n:])
+        return of_core(core, high, low), of_core(core, low, high)
+
+    def early(blocks):
+        gate_w = prune(gate_weight, gate_mask)
+        up_w = prune(after(up_weight, blocks[1]), up_mask)
+        theirs, mine = halves(blocks)
+        return dot(theirs, gate_w), dot(theirs, up_w), mine, gate_w, up_w
+
+    def hidden(mine, gate_w, up_w, gate_in, up_in):
+        gate, up = dot(mine, gate_w) + gate_in, dot(mine, up_w) + up_in
+        return (jax.nn.silu(gate) * up).astype(BF16)
+
+    def down(mine, theirs, down_w, n):
+        low, high = of_core(core, mine, theirs), of_core(core, theirs, mine)
+        sums = dot(jnp.concatenate([low, high]), down_w).astype(BF16)
+        return jnp.split(sums, n)
+
+    (gate_out, up_out, mine, gate_w, up_w), blocks = gather(tokens, early)
+    down_w = prune(after(down_weight, blocks[1]), down_mask)
+    first = hidden(mine, gate_w, up_w, swap(gate_out), swap(up_out))
+    *blocks, first, down_w = lax.optimization_barrier((*blocks, first, down_w))
+    theirs, mine = halves(blocks)
+    gate_out, up_out = dot(theirs, gate_w), dot(theirs, up_w)
+    second = hidden(mine, gate_w, up_w, swap(gate_out), swap(up_out))
+    parts_far = down(second, swap(second), down_w, 4)
+    parts_near = down(first, swap(first), down_w, 4)
+    return scatter(*parts_near, *parts_far)
 
 
 def solution(mesh):

time: 115 us -> 96 us (0.83)
  other arithmetic: 24 us -> 1.48 us
  Pallas kernels: 0 us -> 13.3 us
  matrix products: 21.4 us -> 16.2 us
  local copies, waits for them, and re-layouts: 4.58 us -> 0.95 us
    mul x2 -> x0, other arithmetic: 20.3 us -> none  [pruned(): kept = shaped * mask.astype(BF16)[:, None, :, None]]
    pallas_call x0 -> x3, Pallas kernels: none -> 13.3 us  [prune(): pl.pallas_call(prune_kernel, out_shape=pltpu.VMEM(weight.shape, BF16), in...]
    dot_general x6 -> x10, matrix products: 21.4 us -> 16.2 us  [dot(): return jnp.dot(a, b, preferred_element_type=F32)]
    mul x3 -> x0, local copies, waits for them, and re-layouts: 3.43 us -> none  [pruned(): kept = shaped * mask.astype(BF16)[:, None, :, None]]
    ppermute x18, waiting for transfers between devices: 35.8 us -> 33.5 us  [move(): return lax.ppermute(value, 'tensor', perm)]
    convert_element_type x6 -> x3, other arithmetic: 2.39 us -> 0.24 us  [the longest x1 0.1 us: scatter(): pair_s = (add(pair, pair_in) + move(far_s, MIDDLE).astype(F32)).astype(BF16)]
    ppermute x3 -> x6, waiting for transfers between devices: 0.23 us -> 1.49 us  [swap(): return lax.ppermute(value, 'seq', SWAP)]
  transfers between devices with their start and end apart: 21 -> 24, of which waited for: 8 -> 10; matrix products, arithmetic and copies ran while one was open for 32% -> 12% of each run, Pallas kernels for 0% -> 14%
where the time goes in v3:
time: 96 us; the launch traced here: 95.7 us
  waiting for transfers between devices  34.9 us (36%)
  starting transfers between devices  28.4 us (30%)
  matrix products  16.2 us (17%)
  Pallas kernels  13.3 us (14%)
  other arithmetic  1.48 us (2%)
    ppermute x18, waiting for transfers between devices, move(): return lax.ppermute(value, 'tensor', perm)  33.5 us
    ppermute x18, starting transfers between devices, move(): return lax.ppermute(value, 'tensor', perm)  26.9 us
    dot_general x10, matrix products, dot(): return jnp.dot(a, b, preferred_element_type=F32)  16.2 us
    pallas_call x3, Pallas kernels, prune(): pl.pallas_call(prune_kernel, out_shape=pltpu.VMEM(weight.shape, BF16), in...  13.3 us
  transfers between devices with their start and end apart: 24, of which 10 were waited for; matrix products, arithmetic and copies ran while one was open for 12% of the time, Pallas kernels for 14%

profile of v3, /device:TPU:0, one launch (start us, length us, event | category | flops | bytes accessed | tf_op | source)
XLA Modules:
  0.0 95.7 jit_solution(12657363863054497438)
XLA Ops:
  0.0 3.0 %collective-permute-start.2 = (bf16[64,2048]{1,0:T(8,128)(2,1)}, bf16[64,2048]{1,0:T(8,128)(2,1)S(1)}, u32[]{:S(2)}, u32[]{:S(2)}) collective-permute-start(bf16[64,2048]{1,0:T(8,128)(2,1)} %param.7), channel_id=1, source_target_pairs={{0,4},{2,6},{4,0},{6,2},{8,12},{10,14},{12,8},{14,10},{1,5},{3,7},... | collective-permute-start | bytes 786440 | tf_op jit(solution)/shard_map/ppermute | solution.py:46
  3.0 1.5 %collective-permute-start.5 = (bf16[64,2048]{1,0:T(8,128)(2,1)}, bf16[64,2048]{1,0:T(8,128)(2,1)S(1)}, u32[]{:S(2)}, u32[]{:S(2)}) collective-permute-start(bf16[64,2048]{1,0:T(8,128)(2,1)} %param.7), channel_id=1, source_target_pairs={{0,2},{2,0},{4,6},{6,4},{8,10},{10,8},{12,14},{14,12},{1,3},{3,1},... | collective-permute-start | bytes 786440 | tf_op jit(solution)/shard_map/ppermute | solution.py:46
  5.9 4.4 %prune.3 = bf16[2048,2048]{1,0:T(8,128)(2,1)S(1)} custom-call(s32[16,16]{1,0:T(8,128)S(1)} %copy-done, bf16[2048,2048]{1,0:T(8,128)(2,1)} %weight.1), custom_call_target="tpu_custom_call" | custom-call | bytes 8388608 | tf_op jit(solution)/shard_map/prune/pallas_call | solution.py:127
  11.0 1.5 %collective-permute-start.6 = (bf16[64,2048]{1,0:T(8,128)(2,1)S(1)}, bf16[64,2048]{1,0:T(8,128)(2,1)S(1)}, u32[]{:S(2)}, u32[]{:S(2)}) collective-permute-start(bf16[64,2048]{1,0:T(8,128)(2,1)S(1)} %collective-permute-done.2), channel_id=1, source_target_pairs={{0,2},{2,0},{4,6},{6,4},{8,10},{10,8},{12,14},{14,12},{1,3},{3,1},... | collective-permute-start | bytes 786440 | tf_op jit(solution)/shard_map/ppermute | solution.py:46
  12.5 4.4 %prune.4 = bf16[2048,2048]{1,0:T(8,128)(2,1)S(1)} custom-call(s32[16,16]{1,0:T(8,128)S(1)} %copy-done.1, bf16[2048,2048]{1,0:T(8,128)(2,1)} %weight.2), custom_call_target="tpu_custom_call" | custom-call | bytes 8388608 | tf_op jit(solution)/shard_map/prune/pallas_call | solution.py:127
  19.0 9.2 %collective-permute-done.1 = bf16[64,2048]{1,0:T(8,128)(2,1)S(1)} collective-permute-done((bf16[64,2048]{1,0:T(8,128)(2,1)S(1)}, bf16[64,2048]{1,0:T(8,128)(2,1)S(1)}, u32[]{:S(2)}, u32[]{:S(2)}) %collective-permute-start.1) | collective-permute-done | bytes 262176 | tf_op jit(solution)/shard_map/ppermute | solution.py:46
  28.2 1.5 %collective-permute-start.7 = (bf16[64,2048]{1,0:T(8,128)(2,1)S(1)}, bf16[64,2048]{1,0:T(8,128)(2,1)S(1)}, u32[]{:S(2)}, u32[]{:S(2)}) collective-permute-start(bf16[64,2048]{1,0:T(8,128)(2,1)S(1)} %broadcast_select_fusion.9), channel_id=1, source_target_pairs={{0,2},{2,0},{4,6},{6,4},{8,10},{10,8},{12,14},{14,12},{1,3},{3,1},... | collective-permute-start | bytes 786440 | tf_op jit(solution)/shard_map/ppermute | solution.py:46
  33.9 6.9 %collective-permute-done.4 = bf16[64,2048]{1,0:T(8,128)(2,1)S(1)} collective-permute-done((bf16[64,2048]{1,0:T(8,128)(2,1)S(1)}, bf16[64,2048]{1,0:T(8,128)(2,1)S(1)}, u32[]{:S(2)}, u32[]{:S(2)}) %collective-permute-start.4) | collective-permute-done | bytes 262176 | tf_op jit(solution)/shard_map/ppermute | solution.py:46
  42.0 4.5 %prune.5 = bf16[2048,2048]{1,0:T(8,128)(2,1)S(1)} custom-call(s32[16,16]{1,0:T(8,128)S(1)} %copy-done.2, bf16[2048,2048]{1,0:T(8,128)(2,1)} %weight.3), custom_call_target="tpu_custom_call" | custom-call | bytes 8388608 | tf_op jit(solution)/shard_map/prune/pallas_call | solution.py:127
  47.9 1.7 %multiply_convert_fusion.1 = bf16[128,2048]{1,0:T(8,128)(2,1)S(1)} fusion(f32[128,2048]{1,0:T(8,128)S(1)} %convolution_add_fusion.3, f32[128,2048]{1,0:T(8,128)S(1)} %collective-permute-done.10, bf16[128,2048]{1,0:T(8,128)(2,1)S(1)} %broadcast_select_fusion.6, bf16[2048,2048]{1,0:T(8,128)(2,1)S(1)} %prune.4), kind=kOutput, calls=%fused_computation.13 | convolution fusion | flops 1075576832 | bytes 11534336 | tf_op jit(solution)/shard_map/dot_general | solution.py:22
  53.2 1.4 %collective-permute-done.11 = bf16[128,2048]{1,0:T(8,128)(2,1)S(1)} collective-permute-done((bf16[128,2048]{1,0:T(8,128)(2,1)S(1)}, bf16[128,2048]{1,0:T(8,128)(2,1)S(1)}, u32[]{:S(2)}, u32[]{:S(2)}) %collective-permute-start.11) | collective-permute-done | bytes 524320 | tf_op jit(solution)/shard_map/ppermute | solution.py:102
  56.1 1.6 %multiply_convert_fusion = bf16[128,2048]{1,0:T(8,128)(2,1)S(1)} fusion(f32[128,2048]{1,0:T(8,128)S(1)} %convolution_add_fusion.1, f32[128,2048]{1,0:T(8,128)S(1)} %collective-permute-done.13, bf16[2048,2048]{1,0:T(8,128)(2,1)S(1)} %prune.4, bf16[128,2048]{1,0:T(8,128)(2,1)S(1)} %get-tuple-element.56, bf16[128,2048]{1,0:T(8,128)(2,1)S(1)} %get-tuple-element.57, ...), kind=kOutput, calls=%fused_computation.12 | convolution fusion | flops 1075838976 | bytes 12058625 | tf_op jit(solution)/shard_map/dot_general | solution.py:22
  58.0 2.4 %convolution_convert_fusion.1 = bf16[256,2048]{1,0:T(8,128)(2,1)S(1)} fusion(bf16[2048,2048]{1,0:T(8,128)(2,1)S(1)} %prune.5, bf16[128,2048]{1,0:T(8,128)(2,1)S(1)} %get-tuple-element.53, bf16[128,2048]{1,0:T(8,128)(2,1)S(1)} %get-tuple-element.52), kind=kOutput, calls=%fused_computation.1 | convolution fusion | flops 2150105088 | bytes 10485760 | tf_op jit(solution)/shard_map/dot_general | solution.py:22
  60.5 2.4 %convolution_convert_fusion = bf16[256,2048]{1,0:T(8,128)(2,1)S(1)} fusion(bf16[2048,2048]{1,0:T(8,128)(2,1)S(1)} %prune.5, bf16[128,2048]{1,0:T(8,128)(2,1)S(1)} %get-tuple-element.55, bf16[128,2048]{1,0:T(8,128)(2,1)S(1)} %get-tuple-element.54), kind=kOutput, calls=%fused_computation | convolution fusion | flops 2150105088 | bytes 10485760 | tf_op jit(solution)/shard_map/dot_general | solution.py:22
  62.9 1.5 %collective-permute-start.17 = (bf16[64,2048]{1,0:T(8,128)(2,1)S(1)}, bf16[64,2048]{1,0:T(8,128)(2,1)S(1)}, u32[]{:S(2)}, u32[]{:S(2)}) collective-permute-start(bf16[64,2048]{1,0:T(8,128)(2,1)S(1)} %get-tuple-element.50), channel_id=1, source_target_pairs={{0,2},{2,0},{4,6},{6,4},{8,10},{10,8},{12,14},{14,12},{1,3},{3,1},... | collective-permute-start | bytes 786440 | tf_op jit(solution)/shard_map/ppermute | solution.py:46
  65.2 7.0 %collective-permute-done.17 = bf16[64,2048]{1,0:T(8,128)(2,1)S(1)} collective-permute-done((bf16[64,2048]{1,0:T(8,128)(2,1)S(1)}, bf16[64,2048]{1,0:T(8,128)(2,1)S(1)}, u32[]{:S(2)}, u32[]{:S(2)}) %collective-permute-start.17) | collective-permute-done | bytes 262176 | tf_op jit(solution)/shard_map/ppermute | solution.py:46
  72.2 1.5 %collective-permute-start.21 = (bf16[64,2048]{1,0:T(8,128)(2,1)S(1)}, bf16[64,2048]{1,0:T(8,128)(2,1)S(1)}, u32[]{:S(2)}, u32[]{:S(2)}) collective-permute-start(bf16[64,2048]{1,0:T(8,128)(2,1)S(1)} %add_convert_fusion.5), channel_id=1, source_target_pairs={{0,4},{2,6},{12,8},{14,10},{1,5},{3,7},{13,9},{15,11},{16,20},{18,... | collective-permute-start | bytes 786440 | tf_op jit(solution)/shard_map/ppermute | solution.py:46
  73.7 1.4 %collective-permute-start.20 = (bf16[64,2048]{1,0:T(8,128)(2,1)S(1)}, bf16[64,2048]{1,0:T(8,128)(2,1)S(1)}, u32[]{:S(2)}, u32[]{:S(2)}) collective-permute-start(bf16[64,2048]{1,0:T(8,128)(2,1)S(1)} %get-tuple-element.46), channel_id=1, source_target_pairs={{0,2},{2,0},{4,6},{6,4},{8,10},{10,8},{12,14},{14,12},{1,3},{3,1},... | collective-permute-start | bytes 786440 | tf_op jit(solution)/shard_map/ppermute | solution.py:46
  75.1 2.6 %collective-permute-done.15 = bf16[64,2048]{1,0:T(8,128)(2,1)S(1)} collective-permute-done((bf16[64,2048]{1,0:T(8,128)(2,1)S(1)}, bf16[64,2048]{1,0:T(8,128)(2,1)S(1)}, u32[]{:S(2)}, u32[]{:S(2)}) %collective-permute-start.15) | collective-permute-done | bytes 262176 | tf_op jit(solution)/shard_map/ppermute | solution.py:46
  77.8 1.5 %collective-permute-start.18 = (bf16[64,2048]{1,0:T(8,128)(2,1)S(1)}, bf16[64,2048]{1,0:T(8,128)(2,1)S(1)}, u32[]{:S(2)}, u32[]{:S(2)}) collective-permute-start(bf16[64,2048]{1,0:T(8,128)(2,1)S(1)} %add_convert_fusion.4), channel_id=1, source_target_pairs={{0,4},{2,6},{12,8},{14,10},{1,5},{3,7},{13,9},{15,11},{16,20},{18,... | collective-permute-start | bytes 786440 | tf_op jit(solution)/shard_map/ppermute | solution.py:46
  79.3 1.4 %collective-permute-start.16 = (bf16[64,2048]{1,0:T(8,128)(2,1)S(1)}, bf16[64,2048]{1,0:T(8,128)(2,1)S(1)}, u32[]{:S(2)}, u32[]{:S(2)}) collective-permute-start(bf16[64,2048]{1,0:T(8,128)(2,1)S(1)} %get-tuple-element.44), channel_id=1, source_target_pairs={{0,2},{2,0},{4,6},{6,4},{8,10},{10,8},{12,14},{14,12},{1,3},{3,1},... | collective-permute-start | bytes 786440 | tf_op jit(solution)/shard_map/ppermute | solution.py:46
  81.5 2.6 %collective-permute-done.18 = bf16[64,2048]{1,0:T(8,128)(2,1)S(1)} collective-permute-done((bf16[64,2048]{1,0:T(8,128)(2,1)S(1)}, bf16[64,2048]{1,0:T(8,128)(2,1)S(1)}, u32[]{:S(2)}, u32[]{:S(2)}) %collective-permute-start.18) | collective-permute-done | bytes 262176 | tf_op jit(solution)/shard_map/ppermute | solution.py:46
  85.0 5.5 %collective-permute-start.23 = (bf16[64,2048]{1,0:T(8,128)(2,1)S(1)}, bf16[64,2048]{1,0:T(8,128)(2,1)S(1)}, u32[]{:S(2)}, u32[]{:S(2)}) collective-permute-start(bf16[64,2048]{1,0:T(8,128)(2,1)S(1)} %add_convert_fusion.1), channel_id=1, source_target_pairs={{0,4},{2,6},{4,0},{6,2},{8,12},{10,14},{12,8},{14,10},{1,5},{3,7},... | collective-permute-start | bytes 786440 | tf_op jit(solution)/shard_map/ppermute | solution.py:46
  90.5 4.4 %collective-permute-done.23 = bf16[64,2048]{1,0:T(8,128)(2,1)S(1)} collective-permute-done((bf16[64,2048]{1,0:T(8,128)(2,1)S(1)}, bf16[64,2048]{1,0:T(8,128)(2,1)S(1)}, u32[]{:S(2)}, u32[]{:S(2)}) %collective-permute-start.23) | collective-permute-done | bytes 262176 | tf_op jit(solution)/shard_map/ppermute | solution.py:46
  (65 shorter events, 19.4 us)
Async XLA Ops:
  0.0 10.4 %collective-permute-start.2 = (bf16[64,2048]{1,0:T(8,128)(2,1)}, bf16[64,2048]{1,0:T(8,128)(2,1)S(1)}, u32[]{:S(2)}, u32[]{:S(2)}) collective-permute-start(bf16[64,2048]{1,0:T(8,128)(2,1)} %param.7), channel_id=1, source_target_pairs={{0,4},{2,6},{4,0},{6,2},{8,12},{10,14},{12,8},{14,10},{1,5},{3,7},... | collective-permute-start | bytes 786440 | tf_op jit(solution)/shard_map/ppermute | solution.py:46
  3.0 8.0 %collective-permute-start.5 = (bf16[64,2048]{1,0:T(8,128)(2,1)}, bf16[64,2048]{1,0:T(8,128)(2,1)S(1)}, u32[]{:S(2)}, u32[]{:S(2)}) collective-permute-start(bf16[64,2048]{1,0:T(8,128)(2,1)} %param.7), channel_id=1, source_target_pairs={{0,2},{2,0},{4,6},{6,4},{8,10},{10,8},{12,14},{14,12},{1,3},{3,1},... | collective-permute-start | bytes 786440 | tf_op jit(solution)/shard_map/ppermute | solution.py:46
  4.5 13.1 %collective-permute-start = (bf16[64,2048]{1,0:T(8,128)(2,1)}, bf16[64,2048]{1,0:T(8,128)(2,1)S(1)}, u32[]{:S(2)}, u32[]{:S(2)}) collective-permute-start(bf16[64,2048]{1,0:T(8,128)(2,1)} %param.7), channel_id=1, source_target_pairs={{4,8},{6,10},{8,4},{10,6},{5,9},{7,11},{9,5},{11,7},{20,24},{22,26... | collective-permute-start | bytes 786440 | tf_op jit(solution)/shard_map/ppermute | solution.py:46
  11.0 17.2 %collective-permute-start.6 = (bf16[64,2048]{1,0:T(8,128)(2,1)S(1)}, bf16[64,2048]{1,0:T(8,128)(2,1)S(1)}, u32[]{:S(2)}, u32[]{:S(2)}) collective-permute-start(bf16[64,2048]{1,0:T(8,128)(2,1)S(1)} %collective-permute-done.2), channel_id=1, source_target_pairs={{0,2},{2,0},{4,6},{6,4},{8,10},{10,8},{12,14},{14,12},{1,3},{3,1},... | collective-permute-start | bytes 786440 | tf_op jit(solution)/shard_map/ppermute | solution.py:46
  16.9 12.8 %collective-permute-start.3 = (bf16[64,2048]{1,0:T(8,128)(2,1)S(1)}, bf16[64,2048]{1,0:T(8,128)(2,1)S(1)}, u32[]{:S(2)}, u32[]{:S(2)}) collective-permute-start(bf16[64,2048]{1,0:T(8,128)(2,1)S(1)} %collective-permute-done.2), channel_id=1, source_target_pairs={{4,8},{6,10},{8,4},{10,6},{5,9},{7,11},{9,5},{11,7},{20,24},{22,26... | collective-permute-start | bytes 786440 | tf_op jit(solution)/shard_map/ppermute | solution.py:46
  17.6 10.5 %collective-permute-start.1 = (bf16[64,2048]{1,0:T(8,128)(2,1)S(1)}, bf16[64,2048]{1,0:T(8,128)(2,1)S(1)}, u32[]{:S(2)}, u32[]{:S(2)}) collective-permute-start(bf16[64,2048]{1,0:T(8,128)(2,1)S(1)} %collective-permute-done), channel_id=1, source_target_pairs={{4,0},{6,2},{8,12},{10,14},{5,1},{7,3},{9,13},{11,15},{20,16},{22,... | collective-permute-start | bytes 786440 | tf_op jit(solution)/shard_map/ppermute | solution.py:46
  28.2 12.6 %collective-permute-start.7 = (bf16[64,2048]{1,0:T(8,128)(2,1)S(1)}, bf16[64,2048]{1,0:T(8,128)(2,1)S(1)}, u32[]{:S(2)}, u32[]{:S(2)}) collective-permute-start(bf16[64,2048]{1,0:T(8,128)(2,1)S(1)} %broadcast_select_fusion.9), channel_id=1, source_target_pairs={{0,2},{2,0},{4,6},{6,4},{8,10},{10,8},{12,14},{14,12},{1,3},{3,1},... | collective-permute-start | bytes 786440 | tf_op jit(solution)/shard_map/ppermute | solution.py:46
  32.5 8.3 %collective-permute-start.4 = (bf16[64,2048]{1,0:T(8,128)(2,1)S(1)}, bf16[64,2048]{1,0:T(8,128)(2,1)S(1)}, u32[]{:S(2)}, u32[]{:S(2)}) collective-permute-start(bf16[64,2048]{1,0:T(8,128)(2,1)S(1)} %collective-permute-done.3), channel_id=1, source_target_pairs={{4,0},{6,2},{8,12},{10,14},{5,1},{7,3},{9,13},{11,15},{20,16},{22,... | collective-permute-start | bytes 786440 | tf_op jit(solution)/shard_map/ppermute | solution.py:46
  40.8 5.6 %collective-permute-start.9 = (f32[128,2048]{1,0:T(8,128)S(1)}, f32[128,2048]{1,0:T(8,128)S(1)}, u32[]{:S(2)}, u32[]{:S(2)}) collective-permute-start(f32[128,2048]{1,0:T(8,128)S(1)} %fusion.7), channel_id=1, source_target_pairs={{0,1},{1,0},{2,3},{3,2},{4,5},{5,4},{6,7},{7,6},{8,9},{9,8},{10,11... | collective-permute-start | bytes 3145736 | tf_op jit(solution)/shard_map/ppermute | solution.py:102
  40.9 6.9 %collective-permute-start.10 = (f32[128,2048]{1,0:T(8,128)S(1)}, f32[128,2048]{1,0:T(8,128)S(1)}, u32[]{:S(2)}, u32[]{:S(2)}) collective-permute-start(f32[128,2048]{1,0:T(8,128)S(1)} %fusion.6), channel_id=1, source_target_pairs={{0,1},{1,0},{2,3},{3,2},{4,5},{5,4},{6,7},{7,6},{8,9},{9,8},{10,11... | collective-permute-start | bytes 3145736 | tf_op jit(solution)/shard_map/ppermute | solution.py:102
  41.4 8.3 %collective-permute-start.8 = (bf16[64,2048]{1,0:T(8,128)(2,1)S(1)}, bf16[64,2048]{1,0:T(8,128)(2,1)S(1)}, u32[]{:S(2)}, u32[]{:S(2)}) collective-permute-start(bf16[64,2048]{1,0:T(8,128)(2,1)S(1)} %broadcast_select_fusion.8), channel_id=1, source_target_pairs={{0,2},{2,0},{4,6},{6,4},{8,10},{10,8},{12,14},{14,12},{1,3},{3,1},... | collective-permute-start | bytes 786440 | tf_op jit(solution)/shard_map/ppermute | solution.py:46
  51.1 3.6 %collective-permute-start.12 = (f32[128,2048]{1,0:T(8,128)S(1)}, f32[128,2048]{1,0:T(8,128)S(1)}, u32[]{:S(2)}, u32[]{:S(2)}) collective-permute-start(f32[128,2048]{1,0:T(8,128)S(1)} %fusion.9), channel_id=1, source_target_pairs={{0,1},{1,0},{2,3},{3,2},{4,5},{5,4},{6,7},{7,6},{8,9},{9,8},{10,11... | collective-permute-start | bytes 3145736 | tf_op jit(solution)/shard_map/ppermute | solution.py:102
  51.2 3.4 %collective-permute-start.11 = (bf16[128,2048]{1,0:T(8,128)(2,1)S(1)}, bf16[128,2048]{1,0:T(8,128)(2,1)S(1)}, u32[]{:S(2)}, u32[]{:S(2)}) collective-permute-start(bf16[128,2048]{1,0:T(8,128)(2,1)S(1)} %multiply_convert_fusion.1), channel_id=1, source_target_pairs={{0,1},{1,0},{2,3},{3,2},{4,5},{5,4},{6,7},{7,6},{8,9},{9,8},{10,11... | collective-permute-start | bytes 1572872 | tf_op jit(solution)/shard_map/ppermute | solution.py:102
  53.0 3.1 %collective-permute-start.13 = (f32[128,2048]{1,0:T(8,128)S(1)}, f32[128,2048]{1,0:T(8,128)S(1)}, u32[]{:S(2)}, u32[]{:S(2)}) collective-permute-start(f32[128,2048]{1,0:T(8,128)S(1)} %fusion.8), channel_id=1, source_target_pairs={{0,1},{1,0},{2,3},{3,2},{4,5},{5,4},{6,7},{7,6},{8,9},{9,8},{10,11... | collective-permute-start | bytes 3145736 | tf_op jit(solution)/shard_map/ppermute | solution.py:102
  57.7 2.6 %collective-permute-start.14 = (bf16[128,2048]{1,0:T(8,128)(2,1)S(1)}, bf16[128,2048]{1,0:T(8,128)(2,1)S(1)}, u32[]{:S(2)}, u32[]{:S(2)}) collective-permute-start(bf16[128,2048]{1,0:T(8,128)(2,1)S(1)} %multiply_convert_fusion), channel_id=1, source_target_pairs={{0,1},{1,0},{2,3},{3,2},{4,5},{5,4},{6,7},{7,6},{8,9},{9,8},{10,11... | collective-permute-start | bytes 1572872 | tf_op jit(solution)/shard_map/ppermute | solution.py:102
  62.9 9.2 %collective-permute-start.17 = (bf16[64,2048]{1,0:T(8,128)(2,1)S(1)}, bf16[64,2048]{1,0:T(8,128)(2,1)S(1)}, u32[]{:S(2)}, u32[]{:S(2)}) collective-permute-start(bf16[64,2048]{1,0:T(8,128)(2,1)S(1)} %get-tuple-element.50), channel_id=1, source_target_pairs={{0,2},{2,0},{4,6},{6,4},{8,10},{10,8},{12,14},{14,12},{1,3},{3,1},... | collective-permute-start | bytes 786440 | tf_op jit(solution)/shard_map/ppermute | solution.py:46
  64.5 13.3 %collective-permute-start.15 = (bf16[64,2048]{1,0:T(8,128)(2,1)S(1)}, bf16[64,2048]{1,0:T(8,128)(2,1)S(1)}, u32[]{:S(2)}, u32[]{:S(2)}) collective-permute-start(bf16[64,2048]{1,0:T(8,128)(2,1)S(1)} %get-tuple-element.51), channel_id=1, source_target_pairs={{0,2},{2,0},{4,6},{6,4},{8,10},{10,8},{12,14},{14,12},{1,3},{3,1},... | collective-permute-start | bytes 786440 | tf_op jit(solution)/shard_map/ppermute | solution.py:46
  72.2 8.5 %collective-permute-start.21 = (bf16[64,2048]{1,0:T(8,128)(2,1)S(1)}, bf16[64,2048]{1,0:T(8,128)(2,1)S(1)}, u32[]{:S(2)}, u32[]{:S(2)}) collective-permute-start(bf16[64,2048]{1,0:T(8,128)(2,1)S(1)} %add_convert_fusion.5), channel_id=1, source_target_pairs={{0,4},{2,6},{12,8},{14,10},{1,5},{3,7},{13,9},{15,11},{16,20},{18,... | collective-permute-start | bytes 786440 | tf_op jit(solution)/shard_map/ppermute | solution.py:46
  73.7 11.2 %collective-permute-start.20 = (bf16[64,2048]{1,0:T(8,128)(2,1)S(1)}, bf16[64,2048]{1,0:T(8,128)(2,1)S(1)}, u32[]{:S(2)}, u32[]{:S(2)}) collective-permute-start(bf16[64,2048]{1,0:T(8,128)(2,1)S(1)} %get-tuple-element.46), channel_id=1, source_target_pairs={{0,2},{2,0},{4,6},{6,4},{8,10},{10,8},{12,14},{14,12},{1,3},{3,1},... | collective-permute-start | bytes 786440 | tf_op jit(solution)/shard_map/ppermute | solution.py:46
  77.8 6.3 %collective-permute-start.18 = (bf16[64,2048]{1,0:T(8,128)(2,1)S(1)}, bf16[64,2048]{1,0:T(8,128)(2,1)S(1)}, u32[]{:S(2)}, u32[]{:S(2)}) collective-permute-start(bf16[64,2048]{1,0:T(8,128)(2,1)S(1)} %add_convert_fusion.4), channel_id=1, source_target_pairs={{0,4},{2,6},{12,8},{14,10},{1,5},{3,7},{13,9},{15,11},{16,20},{18,... | collective-permute-start | bytes 786440 | tf_op jit(solution)/shard_map/ppermute | solution.py:46
  79.3 11.1 %collective-permute-start.16 = (bf16[64,2048]{1,0:T(8,128)(2,1)S(1)}, bf16[64,2048]{1,0:T(8,128)(2,1)S(1)}, u32[]{:S(2)}, u32[]{:S(2)}) collective-permute-start(bf16[64,2048]{1,0:T(8,128)(2,1)S(1)} %get-tuple-element.44), channel_id=1, source_target_pairs={{0,2},{2,0},{4,6},{6,4},{8,10},{10,8},{12,14},{14,12},{1,3},{3,1},... | collective-permute-start | bytes 786440 | tf_op jit(solution)/shard_map/ppermute | solution.py:46
  80.8 4.0 %collective-permute-start.22 = (bf16[64,2048]{1,0:T(8,128)(2,1)S(1)}, bf16[64,2048]{1,0:T(8,128)(2,1)S(1)}, u32[]{:S(2)}, u32[]{:S(2)}) collective-permute-start(bf16[64,2048]{1,0:T(8,128)(2,1)S(1)} %add_convert_fusion.2), channel_id=1, source_target_pairs={{4,8},{6,10},{8,4},{10,6},{5,9},{7,11},{9,5},{11,7},{20,24},{22,26... | collective-permute-start | bytes 786440 | tf_op jit(solution)/shard_map/ppermute | solution.py:46
  84.2 6.3 %collective-permute-start.19 = (bf16[64,2048]{1,0:T(8,128)(2,1)S(1)}, bf16[64,2048]{1,0:T(8,128)(2,1)S(1)}, u32[]{:S(2)}, u32[]{:S(2)}) collective-permute-start(bf16[64,2048]{1,0:T(8,128)(2,1)S(1)} %add_convert_fusion.3), channel_id=1, source_target_pairs={{4,8},{6,10},{8,4},{10,6},{5,9},{7,11},{9,5},{11,7},{20,24},{22,26... | collective-permute-start | bytes 786440 | tf_op jit(solution)/shard_map/ppermute | solution.py:46
  85.0 9.8 %collective-permute-start.23 = (bf16[64,2048]{1,0:T(8,128)(2,1)S(1)}, bf16[64,2048]{1,0:T(8,128)(2,1)S(1)}, u32[]{:S(2)}, u32[]{:S(2)}) collective-permute-start(bf16[64,2048]{1,0:T(8,128)(2,1)S(1)} %add_convert_fusion.1), channel_id=1, source_target_pairs={{0,4},{2,6},{4,0},{6,2},{8,12},{10,14},{12,8},{14,10},{1,5},{3,7},... | collective-permute-start | bytes 786440 | tf_op jit(solution)/shard_map/ppermute | solution.py:46
  (4 other events, 22.5 us)

commit v4 on v3

--- a/solution.py
+++ b/solution.py
@@ -6,7 +6,7 @@
 from jax.sharding import PartitionSpec as P
 
 BLOCK = 128
-LIMIT = 16 << 20
+LIMIT = 8 << 20
 BF16 = jnp.bfloat16
 F32 = jnp.float32
 
@@ -62,12 +62,14 @@
     far = move(pair, MIDDLE)
     near_out = move(near, OUTWARD)
     pair_y = move(after(pair, own_y), ACROSS)
+    near_first = near
     near = jnp.where(inner(), near, near_out)
     far_first = far
     far_out = move(far, OUTWARD)
     near_y = move(after(near, pair_y), ACROSS)
     far = jnp.where(inner(), far, far_out)
-    sums = early((own, own_y, pair, after(pair_y, far_first)))
+    late = dict(own_y=own_y, pair=pair, near_first=near_first, pair_y=pair_y, far_first=far_first, far_out=far_out, near_y=near_y, near=near, far=far)
+    sums = early((own, own_y, pair, after(pair_y, far_out)), late)
     far, near_y, *sums = lax.optimization_barrier((far, near_y, *sums))
     far_y = move(far, ACROSS)
     return sums, (near, near_y, far, far_y)
@@ -93,16 +95,35 @@
 
 SWAP = [(0, 1), (1, 0)]
 WHOLE = pl.BlockSpec(memory_space=pltpu.VMEM)
-SCALAR = pl.BlockSpec(memory_space=pltpu.SMEM)
 IN_HBM = pl.BlockSpec(memory_space=pltpu.HBM)
 PIECES = 8
+SCALAR = pl.BlockSpec(memory_space=pltpu.SMEM)
 
 
 def swap(value):
     return lax.ppermute(value, "seq", SWAP)
 
 
-def prune_kernel(mask, weight, out, arrived):
+def prune_kernel(mask, weight, out):
+    for k in range(out.shape[0] // BLOCK):
+        for j in range(out.shape[1] // BLOCK):
+            at = (slice(k * BLOCK, (k + 1) * BLOCK), slice(j * BLOCK, (j + 1) * BLOCK))
+            out[at] = jnp.where(mask[k, j] != 0, weight[at], jnp.zeros((BLOCK, BLOCK), BF16))
+
+
+def prune(weight, mask):
+    return pl.pallas_call(
+        prune_kernel,
+        out_shape=pltpu.VMEM(weight.shape, BF16),
+        in_specs=[SCALAR, WHOLE],
+        out_specs=WHOLE,
+        compiler_params=pltpu.CompilerParams(vmem_limit_bytes=LIMIT),
+        cost_estimate=pl.CostEstimate(flops=0, bytes_accessed=1024, transcendentals=0),
+        name="prune",
+    )(mask, weight)
+
+
+def fetch_prune_kernel(mask, weight, out, arrived):
     rows = out.shape[0] // PIECES
     copies = [
         pltpu.make_async_copy(
@@ -123,15 +144,15 @@
                     out[at] = jnp.zeros((BLOCK, BLOCK), BF16)
 
 
-def prune(weight, mask):
+def fetch_prune(weight, mask):
     return pl.pallas_call(
-        prune_kernel,
+        fetch_prune_kernel,
         out_shape=pltpu.VMEM(weight.shape, BF16),
         in_specs=[SCALAR, IN_HBM],
         out_specs=WHOLE,
         scratch_shapes=[pltpu.SemaphoreType.DMA((PIECES,))],
         compiler_params=pltpu.CompilerParams(vmem_limit_bytes=LIMIT),
-        cost_estimate=pl.CostEstimate(flops=0, bytes_accessed=2 * weight.size, transcendentals=0),
+        cost_estimate=pl.CostEstimate(flops=0, bytes_accessed=1024, transcendentals=0),
         name="prune",
     )(mask, pltpu.with_memory_space_constraint(weight, pltpu.HBM))
 
@@ -149,9 +170,9 @@
         low, high = jnp.concatenate(blocks[:n]), jnp.concatenate(blocks[n:])
         return of_core(core, high, low), of_core(core, low, high)
 
-    def early(blocks):
-        gate_w = prune(gate_weight, gate_mask)
-        up_w = prune(after(up_weight, blocks[1]), up_mask)
+    def early(blocks, late):
+        gate_w = fetch_prune(gate_weight, gate_mask)
+        up_w = fetch_prune(after(up_weight, late['own_y'], late['near_first'], late['pair']), up_mask)
         theirs, mine = halves(blocks)
         return dot(theirs, gate_w), dot(theirs, up_w), mine, gate_w, up_w
 

time: 96 us -> 87.9 us (0.916)
  waiting for transfers between devices: 34.9 us -> 26.4 us
  starting transfers between devices: 28.4 us -> 29.7 us
  Pallas kernels: 13.3 us -> 12.1 us
    pallas_call x3 -> x1, Pallas kernels: 13.3 us -> 3.31 us  [prune(): pl.pallas_call(prune_kernel, out_shape=pltpu.VMEM(weight.shape, BF16), in...]
    pallas_call x0 -> x2, Pallas kernels: none -> 8.77 us  [fetch_prune(): pl.pallas_call(fetch_prune_kernel, out_shape=pltpu.VMEM(weight.shape, BF1...]
    ppermute x18, waiting for transfers between devices: 33.5 us -> 24.9 us  [move(): return lax.ppermute(value, 'tensor', perm)]
    ppermute x18, starting transfers between devices: 26.9 us -> 28.2 us  [move(): return lax.ppermute(value, 'tensor', perm)]
  transfers between devices with their start and end apart: 24 -> 24, of which waited for: 10 -> 10; matrix products, arithmetic and copies ran while one was open for 12% -> 13% of each run, Pallas kernels for 14% -> 14%
where the time goes in v4:
time: 87.9 us; the launch traced here: 87.5 us
  starting transfers between devices  29.7 us (34%)
  waiting for transfers between devices  26.4 us (30%)
  matrix products  16.4 us (19%)
  Pallas kernels  12.1 us (14%)
  other arithmetic  1.5 us (2%)
  local copies, waits for them, and re-layouts  0.96 us (1%)
    ppermute x18, starting transfers between devices, move(): return lax.ppermute(value, 'tensor', perm)  28.2 us
    ppermute x18, waiting for transfers between devices, move(): return lax.ppermute(value, 'tensor', perm)  24.9 us
    dot_general x10, matrix products, dot(): return jnp.dot(a, b, preferred_element_type=F32)  16.4 us
    pallas_call x2, Pallas kernels, fetch_prune(): pl.pallas_call(fetch_prune_kernel, out_shape=pltpu.VMEM(weight.shape, BF1...  8.77 us
    pallas_call x1, Pallas kernels, prune(): pl.pallas_call(prune_kernel, out_shape=pltpu.VMEM(weight.shape, BF16), in...  3.31 us
  transfers between devices with their start and end apart: 24, of which 10 were waited for; matrix products, arithmetic and copies ran while one was open for 13% of the time, Pallas kernels for 14%

profile of v4, /device:TPU:0, one launch (start us, length us, event | category | flops | bytes accessed | tf_op | source)
XLA Modules:
  0.0 87.5 jit_solution(1473975181188680336)
XLA Ops:
  0.0 3.0 %collective-permute-start.2 = (bf16[64,2048]{1,0:T(8,128)(2,1)}, bf16[64,2048]{1,0:T(8,128)(2,1)S(1)}, u32[]{:S(2)}, u32[]{:S(2)}) collective-permute-start(bf16[64,2048]{1,0:T(8,128)(2,1)} %param.7), channel_id=1, source_target_pairs={{0,4},{2,6},{4,0},{6,2},{8,12},{10,14},{12,8},{14,10},{1,5},{3,7},... | collective-permute-start | bytes 786440 | tf_op jit(solution)/shard_map/ppermute | solution.py:46
  3.0 1.5 %collective-permute-start.5 = (bf16[64,2048]{1,0:T(8,128)(2,1)}, bf16[64,2048]{1,0:T(8,128)(2,1)S(1)}, u32[]{:S(2)}, u32[]{:S(2)}) collective-permute-start(bf16[64,2048]{1,0:T(8,128)(2,1)} %param.7), channel_id=1, source_target_pairs={{0,2},{2,0},{4,6},{6,4},{8,10},{10,8},{12,14},{14,12},{1,3},{3,1},... | collective-permute-start | bytes 786440 | tf_op jit(solution)/shard_map/ppermute | solution.py:46
  5.9 4.4 %prune.3 = bf16[2048,2048]{1,0:T(8,128)(2,1)S(1)} custom-call(s32[16,16]{1,0:T(8,128)S(1)} %copy-done, bf16[2048,2048]{1,0:T(8,128)(2,1)} %weight.1), custom_call_target="tpu_custom_call" | custom-call | bytes 1024 | tf_op jit(solution)/shard_map/prune/pallas_call | solution.py:148
  11.0 1.5 %collective-permute-start.6 = (bf16[64,2048]{1,0:T(8,128)(2,1)S(1)}, bf16[64,2048]{1,0:T(8,128)(2,1)S(1)}, u32[]{:S(2)}, u32[]{:S(2)}) collective-permute-start(bf16[64,2048]{1,0:T(8,128)(2,1)S(1)} %collective-permute-done.2), channel_id=1, source_target_pairs={{0,2},{2,0},{4,6},{6,4},{8,10},{10,8},{12,14},{14,12},{1,3},{3,1},... | collective-permute-start | bytes 786440 | tf_op jit(solution)/shard_map/ppermute | solution.py:46
  14.5 4.4 %prune.4 = bf16[2048,2048]{1,0:T(8,128)(2,1)S(1)} custom-call(s32[16,16]{1,0:T(8,128)S(1)} %copy-done.1, bf16[2048,2048]{1,0:T(8,128)(2,1)} %weight.2), custom_call_target="tpu_custom_call" | custom-call | bytes 1024 | tf_op jit(solution)/shard_map/prune/pallas_call | solution.py:148
  19.0 1.5 %collective-permute-start.4 = (bf16[64,2048]{1,0:T(8,128)(2,1)S(1)}, bf16[64,2048]{1,0:T(8,128)(2,1)S(1)}, u32[]{:S(2)}, u32[]{:S(2)}) collective-permute-start(bf16[64,2048]{1,0:T(8,128)(2,1)S(1)} %collective-permute-done.3), channel_id=1, source_target_pairs={{4,0},{6,2},{8,12},{10,14},{5,1},{7,3},{9,13},{11,15},{20,16},{22,... | collective-permute-start | bytes 786440 | tf_op jit(solution)/shard_map/ppermute | solution.py:46
  20.5 3.3 %collective-permute-done.1 = bf16[64,2048]{1,0:T(8,128)(2,1)S(1)} collective-permute-done((bf16[64,2048]{1,0:T(8,128)(2,1)S(1)}, bf16[64,2048]{1,0:T(8,128)(2,1)S(1)}, u32[]{:S(2)}, u32[]{:S(2)}) %collective-permute-start.1) | collective-permute-done | bytes 262176 | tf_op jit(solution)/shard_map/ppermute | solution.py:46
  23.8 1.6 %collective-permute-start.7 = (bf16[64,2048]{1,0:T(8,128)(2,1)S(1)}, bf16[64,2048]{1,0:T(8,128)(2,1)S(1)}, u32[]{:S(2)}, u32[]{:S(2)}) collective-permute-start(bf16[64,2048]{1,0:T(8,128)(2,1)S(1)} %broadcast_select_fusion.9), channel_id=1, source_target_pairs={{0,2},{2,0},{4,6},{6,4},{8,10},{10,8},{12,14},{14,12},{1,3},{3,1},... | collective-permute-start | bytes 786440 | tf_op jit(solution)/shard_map/ppermute | solution.py:46
  25.4 4.4 %collective-permute-done.4 = bf16[64,2048]{1,0:T(8,128)(2,1)S(1)} collective-permute-done((bf16[64,2048]{1,0:T(8,128)(2,1)S(1)}, bf16[64,2048]{1,0:T(8,128)(2,1)S(1)}, u32[]{:S(2)}, u32[]{:S(2)}) %collective-permute-start.4) | collective-permute-done | bytes 262176 | tf_op jit(solution)/shard_map/ppermute | solution.py:46
  33.2 1.5 %collective-permute-start.8 = (bf16[64,2048]{1,0:T(8,128)(2,1)S(1)}, bf16[64,2048]{1,0:T(8,128)(2,1)S(1)}, u32[]{:S(2)}, u32[]{:S(2)}) collective-permute-start(bf16[64,2048]{1,0:T(8,128)(2,1)S(1)} %broadcast_select_fusion.8), channel_id=1, source_target_pairs={{0,2},{2,0},{4,6},{6,4},{8,10},{10,8},{12,14},{14,12},{1,3},{3,1},... | collective-permute-start | bytes 786440 | tf_op jit(solution)/shard_map/ppermute | solution.py:46
  34.8 3.3 %prune.5 = bf16[2048,2048]{1,0:T(8,128)(2,1)S(1)} custom-call(s32[16,16]{1,0:T(8,128)S(1)} %copy-done.2, bf16[2048,2048]{1,0:T(8,128)(2,1)S(1)} %bitcast.13), custom_call_target="tpu_custom_call" | custom-call | bytes 1024 | tf_op jit(solution)/shard_map/prune/pallas_call | solution.py:115
  39.5 1.7 %multiply_convert_fusion.1 = bf16[128,2048]{1,0:T(8,128)(2,1)S(1)} fusion(f32[128,2048]{1,0:T(8,128)S(1)} %convolution_add_fusion.3, f32[128,2048]{1,0:T(8,128)S(1)} %collective-permute-done.10, bf16[128,2048]{1,0:T(8,128)(2,1)S(1)} %broadcast_select_fusion.6, bf16[2048,2048]{1,0:T(8,128)(2,1)S(1)} %prune.4), kind=kOutput, calls=%fused_computation.13 | convolution fusion | flops 1075576832 | bytes 11534336 | tf_op jit(solution)/shard_map/dot_general | solution.py:22
  47.9 1.9 %multiply_convert_fusion = bf16[128,2048]{1,0:T(8,128)(2,1)S(1)} fusion(f32[128,2048]{1,0:T(8,128)S(1)} %convolution_add_fusion.1, f32[128,2048]{1,0:T(8,128)S(1)} %collective-permute-done.13, bf16[2048,2048]{1,0:T(8,128)(2,1)S(1)} %prune.4, bf16[128,2048]{1,0:T(8,128)(2,1)S(1)} %get-tuple-element.56, bf16[128,2048]{1,0:T(8,128)(2,1)S(1)} %get-tuple-element.57, ...), kind=kOutput, calls=%fused_computation.12 | convolution fusion | flops 1075838976 | bytes 12058625 | tf_op jit(solution)/shard_map/dot_general | solution.py:22
  50.0 2.4 %convolution_convert_fusion.1 = bf16[256,2048]{1,0:T(8,128)(2,1)S(1)} fusion(bf16[2048,2048]{1,0:T(8,128)(2,1)S(1)} %prune.5, bf16[128,2048]{1,0:T(8,128)(2,1)S(1)} %get-tuple-element.53, bf16[128,2048]{1,0:T(8,128)(2,1)S(1)} %get-tuple-element.52), kind=kOutput, calls=%fused_computation.1 | convolution fusion | flops 2150105088 | bytes 10485760 | tf_op jit(solution)/shard_map/dot_general | solution.py:22
  52.5 2.4 %convolution_convert_fusion = bf16[256,2048]{1,0:T(8,128)(2,1)S(1)} fusion(bf16[2048,2048]{1,0:T(8,128)(2,1)S(1)} %prune.5, bf16[128,2048]{1,0:T(8,128)(2,1)S(1)} %get-tuple-element.55, bf16[128,2048]{1,0:T(8,128)(2,1)S(1)} %get-tuple-element.54), kind=kOutput, calls=%fused_computation | convolution fusion | flops 2150105088 | bytes 10485760 | tf_op jit(solution)/shard_map/dot_general | solution.py:22
  55.0 1.6 %collective-permute-start.17 = (bf16[64,2048]{1,0:T(8,128)(2,1)S(1)}, bf16[64,2048]{1,0:T(8,128)(2,1)S(1)}, u32[]{:S(2)}, u32[]{:S(2)}) collective-permute-start(bf16[64,2048]{1,0:T(8,128)(2,1)S(1)} %get-tuple-element.50), channel_id=1, source_target_pairs={{0,2},{2,0},{4,6},{6,4},{8,10},{10,8},{12,14},{14,12},{1,3},{3,1},... | collective-permute-start | bytes 786440 | tf_op jit(solution)/shard_map/ppermute | solution.py:46
  57.2 7.0 %collective-permute-done.17 = bf16[64,2048]{1,0:T(8,128)(2,1)S(1)} collective-permute-done((bf16[64,2048]{1,0:T(8,128)(2,1)S(1)}, bf16[64,2048]{1,0:T(8,128)(2,1)S(1)}, u32[]{:S(2)}, u32[]{:S(2)}) %collective-permute-start.17) | collective-permute-done | bytes 262176 | tf_op jit(solution)/shard_map/ppermute | solution.py:46
  64.3 1.5 %collective-permute-start.21 = (bf16[64,2048]{1,0:T(8,128)(2,1)S(1)}, bf16[64,2048]{1,0:T(8,128)(2,1)S(1)}, u32[]{:S(2)}, u32[]{:S(2)}) collective-permute-start(bf16[64,2048]{1,0:T(8,128)(2,1)S(1)} %add_convert_fusion.5), channel_id=1, source_target_pairs={{0,4},{2,6},{12,8},{14,10},{1,5},{3,7},{13,9},{15,11},{16,20},{18,... | collective-permute-start | bytes 786440 | tf_op jit(solution)/shard_map/ppermute | solution.py:46
  65.7 1.6 %collective-permute-start.20 = (bf16[64,2048]{1,0:T(8,128)(2,1)S(1)}, bf16[64,2048]{1,0:T(8,128)(2,1)S(1)}, u32[]{:S(2)}, u32[]{:S(2)}) collective-permute-start(bf16[64,2048]{1,0:T(8,128)(2,1)S(1)} %get-tuple-element.46), channel_id=1, source_target_pairs={{0,2},{2,0},{4,6},{6,4},{8,10},{10,8},{12,14},{14,12},{1,3},{3,1},... | collective-permute-start | bytes 786440 | tf_op jit(solution)/shard_map/ppermute | solution.py:46
  67.3 2.5 %collective-permute-done.15 = bf16[64,2048]{1,0:T(8,128)(2,1)S(1)} collective-permute-done((bf16[64,2048]{1,0:T(8,128)(2,1)S(1)}, bf16[64,2048]{1,0:T(8,128)(2,1)S(1)}, u32[]{:S(2)}, u32[]{:S(2)}) %collective-permute-start.15) | collective-permute-done | bytes 262176 | tf_op jit(solution)/shard_map/ppermute | solution.py:46
  71.4 1.6 %collective-permute-start.16 = (bf16[64,2048]{1,0:T(8,128)(2,1)S(1)}, bf16[64,2048]{1,0:T(8,128)(2,1)S(1)}, u32[]{:S(2)}, u32[]{:S(2)}) collective-permute-start(bf16[64,2048]{1,0:T(8,128)(2,1)S(1)} %get-tuple-element.44), channel_id=1, source_target_pairs={{0,2},{2,0},{4,6},{6,4},{8,10},{10,8},{12,14},{14,12},{1,3},{3,1},... | collective-permute-start | bytes 786440 | tf_op jit(solution)/shard_map/ppermute | solution.py:46
  73.7 2.5 %collective-permute-done.18 = bf16[64,2048]{1,0:T(8,128)(2,1)S(1)} collective-permute-done((bf16[64,2048]{1,0:T(8,128)(2,1)S(1)}, bf16[64,2048]{1,0:T(8,128)(2,1)S(1)}, u32[]{:S(2)}, u32[]{:S(2)}) %collective-permute-start.18) | collective-permute-done | bytes 262176 | tf_op jit(solution)/shard_map/ppermute | solution.py:46
  77.1 5.2 %collective-permute-start.23 = (bf16[64,2048]{1,0:T(8,128)(2,1)S(1)}, bf16[64,2048]{1,0:T(8,128)(2,1)S(1)}, u32[]{:S(2)}, u32[]{:S(2)}) collective-permute-start(bf16[64,2048]{1,0:T(8,128)(2,1)S(1)} %add_convert_fusion.1), channel_id=1, source_target_pairs={{0,4},{2,6},{4,0},{6,2},{8,12},{10,14},{12,8},{14,10},{1,5},{3,7},... | collective-permute-start | bytes 786440 | tf_op jit(solution)/shard_map/ppermute | solution.py:46
  82.3 4.4 %collective-permute-done.23 = bf16[64,2048]{1,0:T(8,128)(2,1)S(1)} collective-permute-done((bf16[64,2048]{1,0:T(8,128)(2,1)S(1)}, bf16[64,2048]{1,0:T(8,128)(2,1)S(1)}, u32[]{:S(2)}, u32[]{:S(2)}) %collective-permute-start.23) | collective-permute-done | bytes 262176 | tf_op jit(solution)/shard_map/ppermute | solution.py:46
  (70 shorter events, 20.5 us)
Async XLA Ops:
  0.0 10.4 %collective-permute-start.2 = (bf16[64,2048]{1,0:T(8,128)(2,1)}, bf16[64,2048]{1,0:T(8,128)(2,1)S(1)}, u32[]{:S(2)}, u32[]{:S(2)}) collective-permute-start(bf16[64,2048]{1,0:T(8,128)(2,1)} %param.7), channel_id=1, source_target_pairs={{0,4},{2,6},{4,0},{6,2},{8,12},{10,14},{12,8},{14,10},{1,5},{3,7},... | collective-permute-start | bytes 786440 | tf_op jit(solution)/shard_map/ppermute | solution.py:46
  3.0 8.0 %collective-permute-start.5 = (bf16[64,2048]{1,0:T(8,128)(2,1)}, bf16[64,2048]{1,0:T(8,128)(2,1)S(1)}, u32[]{:S(2)}, u32[]{:S(2)}) collective-permute-start(bf16[64,2048]{1,0:T(8,128)(2,1)} %param.7), channel_id=1, source_target_pairs={{0,2},{2,0},{4,6},{6,4},{8,10},{10,8},{12,14},{14,12},{1,3},{3,1},... | collective-permute-start | bytes 786440 | tf_op jit(solution)/shard_map/ppermute | solution.py:46
  4.5 8.7 %collective-permute-start = (bf16[64,2048]{1,0:T(8,128)(2,1)}, bf16[64,2048]{1,0:T(8,128)(2,1)S(1)}, u32[]{:S(2)}, u32[]{:S(2)}) collective-permute-start(bf16[64,2048]{1,0:T(8,128)(2,1)} %param.7), channel_id=1, source_target_pairs={{4,8},{6,10},{8,4},{10,6},{5,9},{7,11},{9,5},{11,7},{20,24},{22,26... | collective-permute-start | bytes 786440 | tf_op jit(solution)/shard_map/ppermute | solution.py:46
  11.0 12.8 %collective-permute-start.6 = (bf16[64,2048]{1,0:T(8,128)(2,1)S(1)}, bf16[64,2048]{1,0:T(8,128)(2,1)S(1)}, u32[]{:S(2)}, u32[]{:S(2)}) collective-permute-start(bf16[64,2048]{1,0:T(8,128)(2,1)S(1)} %collective-permute-done.2), channel_id=1, source_target_pairs={{0,2},{2,0},{4,6},{6,4},{8,10},{10,8},{12,14},{14,12},{1,3},{3,1},... | collective-permute-start | bytes 786440 | tf_op jit(solution)/shard_map/ppermute | solution.py:46
  12.5 6.5 %collective-permute-start.3 = (bf16[64,2048]{1,0:T(8,128)(2,1)S(1)}, bf16[64,2048]{1,0:T(8,128)(2,1)S(1)}, u32[]{:S(2)}, u32[]{:S(2)}) collective-permute-start(bf16[64,2048]{1,0:T(8,128)(2,1)S(1)} %collective-permute-done.2), channel_id=1, source_target_pairs={{4,8},{6,10},{8,4},{10,6},{5,9},{7,11},{9,5},{11,7},{20,24},{22,26... | collective-permute-start | bytes 786440 | tf_op jit(solution)/shard_map/ppermute | solution.py:46
  13.2 10.5 %collective-permute-start.1 = (bf16[64,2048]{1,0:T(8,128)(2,1)S(1)}, bf16[64,2048]{1,0:T(8,128)(2,1)S(1)}, u32[]{:S(2)}, u32[]{:S(2)}) collective-permute-start(bf16[64,2048]{1,0:T(8,128)(2,1)S(1)} %collective-permute-done), channel_id=1, source_target_pairs={{4,0},{6,2},{8,12},{10,14},{5,1},{7,3},{9,13},{11,15},{20,16},{22,... | collective-permute-start | bytes 786440 | tf_op jit(solution)/shard_map/ppermute | solution.py:46
  19.0 10.8 %collective-permute-start.4 = (bf16[64,2048]{1,0:T(8,128)(2,1)S(1)}, bf16[64,2048]{1,0:T(8,128)(2,1)S(1)}, u32[]{:S(2)}, u32[]{:S(2)}) collective-permute-start(bf16[64,2048]{1,0:T(8,128)(2,1)S(1)} %collective-permute-done.3), channel_id=1, source_target_pairs={{4,0},{6,2},{8,12},{10,14},{5,1},{7,3},{9,13},{11,15},{20,16},{22,... | collective-permute-start | bytes 786440 | tf_op jit(solution)/shard_map/ppermute | solution.py:46
  23.8 8.9 %collective-permute-start.7 = (bf16[64,2048]{1,0:T(8,128)(2,1)S(1)}, bf16[64,2048]{1,0:T(8,128)(2,1)S(1)}, u32[]{:S(2)}, u32[]{:S(2)}) collective-permute-start(bf16[64,2048]{1,0:T(8,128)(2,1)S(1)} %broadcast_select_fusion.9), channel_id=1, source_target_pairs={{0,2},{2,0},{4,6},{6,4},{8,10},{10,8},{12,14},{14,12},{1,3},{3,1},... | collective-permute-start | bytes 786440 | tf_op jit(solution)/shard_map/ppermute | solution.py:46
  32.7 5.5 %collective-permute-start.9 = (f32[128,2048]{1,0:T(8,128)S(1)}, f32[128,2048]{1,0:T(8,128)S(1)}, u32[]{:S(2)}, u32[]{:S(2)}) collective-permute-start(f32[128,2048]{1,0:T(8,128)S(1)} %fusion.7), channel_id=1, source_target_pairs={{0,1},{1,0},{2,3},{3,2},{4,5},{5,4},{6,7},{7,6},{8,9},{9,8},{10,11... | collective-permute-start | bytes 3145736 | tf_op jit(solution)/shard_map/ppermute | solution.py:104
  32.7 6.8 %collective-permute-start.10 = (f32[128,2048]{1,0:T(8,128)S(1)}, f32[128,2048]{1,0:T(8,128)S(1)}, u32[]{:S(2)}, u32[]{:S(2)}) collective-permute-start(f32[128,2048]{1,0:T(8,128)S(1)} %fusion.6), channel_id=1, source_target_pairs={{0,1},{1,0},{2,3},{3,2},{4,5},{5,4},{6,7},{7,6},{8,9},{9,8},{10,11... | collective-permute-start | bytes 3145736 | tf_op jit(solution)/shard_map/ppermute | solution.py:104
  33.2 8.3 %collective-permute-start.8 = (bf16[64,2048]{1,0:T(8,128)(2,1)S(1)}, bf16[64,2048]{1,0:T(8,128)(2,1)S(1)}, u32[]{:S(2)}, u32[]{:S(2)}) collective-permute-start(bf16[64,2048]{1,0:T(8,128)(2,1)S(1)} %broadcast_select_fusion.8), channel_id=1, source_target_pairs={{0,2},{2,0},{4,6},{6,4},{8,10},{10,8},{12,14},{14,12},{1,3},{3,1},... | collective-permute-start | bytes 786440 | tf_op jit(solution)/shard_map/ppermute | solution.py:46
  43.0 3.6 %collective-permute-start.12 = (f32[128,2048]{1,0:T(8,128)S(1)}, f32[128,2048]{1,0:T(8,128)S(1)}, u32[]{:S(2)}, u32[]{:S(2)}) collective-permute-start(f32[128,2048]{1,0:T(8,128)S(1)} %fusion.9), channel_id=1, source_target_pairs={{0,1},{1,0},{2,3},{3,2},{4,5},{5,4},{6,7},{7,6},{8,9},{9,8},{10,11... | collective-permute-start | bytes 3145736 | tf_op jit(solution)/shard_map/ppermute | solution.py:104
  43.0 3.4 %collective-permute-start.11 = (bf16[128,2048]{1,0:T(8,128)(2,1)S(1)}, bf16[128,2048]{1,0:T(8,128)(2,1)S(1)}, u32[]{:S(2)}, u32[]{:S(2)}) collective-permute-start(bf16[128,2048]{1,0:T(8,128)(2,1)S(1)} %multiply_convert_fusion.1), channel_id=1, source_target_pairs={{0,1},{1,0},{2,3},{3,2},{4,5},{5,4},{6,7},{7,6},{8,9},{9,8},{10,11... | collective-permute-start | bytes 1572872 | tf_op jit(solution)/shard_map/ppermute | solution.py:104
  44.9 3.1 %collective-permute-start.13 = (f32[128,2048]{1,0:T(8,128)S(1)}, f32[128,2048]{1,0:T(8,128)S(1)}, u32[]{:S(2)}, u32[]{:S(2)}) collective-permute-start(f32[128,2048]{1,0:T(8,128)S(1)} %fusion.8), channel_id=1, source_target_pairs={{0,1},{1,0},{2,3},{3,2},{4,5},{5,4},{6,7},{7,6},{8,9},{9,8},{10,11... | collective-permute-start | bytes 3145736 | tf_op jit(solution)/shard_map/ppermute | solution.py:104
  49.8 2.6 %collective-permute-start.14 = (bf16[128,2048]{1,0:T(8,128)(2,1)S(1)}, bf16[128,2048]{1,0:T(8,128)(2,1)S(1)}, u32[]{:S(2)}, u32[]{:S(2)}) collective-permute-start(bf16[128,2048]{1,0:T(8,128)(2,1)S(1)} %multiply_convert_fusion), channel_id=1, source_target_pairs={{0,1},{1,0},{2,3},{3,2},{4,5},{5,4},{6,7},{7,6},{8,9},{9,8},{10,11... | collective-permute-start | bytes 1572872 | tf_op jit(solution)/shard_map/ppermute | solution.py:104
  55.0 9.2 %collective-permute-start.17 = (bf16[64,2048]{1,0:T(8,128)(2,1)S(1)}, bf16[64,2048]{1,0:T(8,128)(2,1)S(1)}, u32[]{:S(2)}, u32[]{:S(2)}) collective-permute-start(bf16[64,2048]{1,0:T(8,128)(2,1)S(1)} %get-tuple-element.50), channel_id=1, source_target_pairs={{0,2},{2,0},{4,6},{6,4},{8,10},{10,8},{12,14},{14,12},{1,3},{3,1},... | collective-permute-start | bytes 786440 | tf_op jit(solution)/shard_map/ppermute | solution.py:46
  56.7 13.1 %collective-permute-start.15 = (bf16[64,2048]{1,0:T(8,128)(2,1)S(1)}, bf16[64,2048]{1,0:T(8,128)(2,1)S(1)}, u32[]{:S(2)}, u32[]{:S(2)}) collective-permute-start(bf16[64,2048]{1,0:T(8,128)(2,1)S(1)} %get-tuple-element.51), channel_id=1, source_target_pairs={{0,2},{2,0},{4,6},{6,4},{8,10},{10,8},{12,14},{14,12},{1,3},{3,1},... | collective-permute-start | bytes 786440 | tf_op jit(solution)/shard_map/ppermute | solution.py:46
  64.3 8.7 %collective-permute-start.21 = (bf16[64,2048]{1,0:T(8,128)(2,1)S(1)}, bf16[64,2048]{1,0:T(8,128)(2,1)S(1)}, u32[]{:S(2)}, u32[]{:S(2)}) collective-permute-start(bf16[64,2048]{1,0:T(8,128)(2,1)S(1)} %add_convert_fusion.5), channel_id=1, source_target_pairs={{0,4},{2,6},{12,8},{14,10},{1,5},{3,7},{13,9},{15,11},{16,20},{18,... | collective-permute-start | bytes 786440 | tf_op jit(solution)/shard_map/ppermute | solution.py:46
  65.7 11.2 %collective-permute-start.20 = (bf16[64,2048]{1,0:T(8,128)(2,1)S(1)}, bf16[64,2048]{1,0:T(8,128)(2,1)S(1)}, u32[]{:S(2)}, u32[]{:S(2)}) collective-permute-start(bf16[64,2048]{1,0:T(8,128)(2,1)S(1)} %get-tuple-element.46), channel_id=1, source_target_pairs={{0,2},{2,0},{4,6},{6,4},{8,10},{10,8},{12,14},{14,12},{1,3},{3,1},... | collective-permute-start | bytes 786440 | tf_op jit(solution)/shard_map/ppermute | solution.py:46
  69.9 6.3 %collective-permute-start.18 = (bf16[64,2048]{1,0:T(8,128)(2,1)S(1)}, bf16[64,2048]{1,0:T(8,128)(2,1)S(1)}, u32[]{:S(2)}, u32[]{:S(2)}) collective-permute-start(bf16[64,2048]{1,0:T(8,128)(2,1)S(1)} %add_convert_fusion.4), channel_id=1, source_target_pairs={{0,4},{2,6},{12,8},{14,10},{1,5},{3,7},{13,9},{15,11},{16,20},{18,... | collective-permute-start | bytes 786440 | tf_op jit(solution)/shard_map/ppermute | solution.py:46
  71.4 11.0 %collective-permute-start.16 = (bf16[64,2048]{1,0:T(8,128)(2,1)S(1)}, bf16[64,2048]{1,0:T(8,128)(2,1)S(1)}, u32[]{:S(2)}, u32[]{:S(2)}) collective-permute-start(bf16[64,2048]{1,0:T(8,128)(2,1)S(1)} %get-tuple-element.44), channel_id=1, source_target_pairs={{0,2},{2,0},{4,6},{6,4},{8,10},{10,8},{12,14},{14,12},{1,3},{3,1},... | collective-permute-start | bytes 786440 | tf_op jit(solution)/shard_map/ppermute | solution.py:46
  73.0 3.9 %collective-permute-start.22 = (bf16[64,2048]{1,0:T(8,128)(2,1)S(1)}, bf16[64,2048]{1,0:T(8,128)(2,1)S(1)}, u32[]{:S(2)}, u32[]{:S(2)}) collective-permute-start(bf16[64,2048]{1,0:T(8,128)(2,1)S(1)} %add_convert_fusion.2), channel_id=1, source_target_pairs={{4,8},{6,10},{8,4},{10,6},{5,9},{7,11},{9,5},{11,7},{20,24},{22,26... | collective-permute-start | bytes 786440 | tf_op jit(solution)/shard_map/ppermute | solution.py:46
  76.3 6.1 %collective-permute-start.19 = (bf16[64,2048]{1,0:T(8,128)(2,1)S(1)}, bf16[64,2048]{1,0:T(8,128)(2,1)S(1)}, u32[]{:S(2)}, u32[]{:S(2)}) collective-permute-start(bf16[64,2048]{1,0:T(8,128)(2,1)S(1)} %add_convert_fusion.3), channel_id=1, source_target_pairs={{4,8},{6,10},{8,4},{10,6},{5,9},{7,11},{9,5},{11,7},{20,24},{22,26... | collective-permute-start | bytes 786440 | tf_op jit(solution)/shard_map/ppermute | solution.py:46
  77.1 9.6 %collective-permute-start.23 = (bf16[64,2048]{1,0:T(8,128)(2,1)S(1)}, bf16[64,2048]{1,0:T(8,128)(2,1)S(1)}, u32[]{:S(2)}, u32[]{:S(2)}) collective-permute-start(bf16[64,2048]{1,0:T(8,128)(2,1)S(1)} %add_convert_fusion.1), channel_id=1, source_target_pairs={{0,4},{2,6},{4,0},{6,2},{8,12},{10,14},{12,8},{14,10},{1,5},{3,7},... | collective-permute-start | bytes 786440 | tf_op jit(solution)/shard_map/ppermute | solution.py:46
  (6 other events, 25.8 us)

commit v5 on v3

--- a/solution.py
+++ b/solution.py
@@ -6,7 +6,7 @@
 from jax.sharding import PartitionSpec as P
 
 BLOCK = 128
-LIMIT = 16 << 20
+LIMIT = 8 << 20
 BF16 = jnp.bfloat16
 F32 = jnp.float32
 
@@ -55,22 +55,23 @@
     return lax.optimization_barrier((value, *others))[0]
 
 
-def gather(own, early):
+def gather(own, weights):
     pair = move(own, PAIR)
-    near = move(own, MIDDLE)
+    near_mid = move(own, MIDDLE)
     own_y = move(own, ACROSS)
-    far = move(pair, MIDDLE)
-    near_out = move(near, OUTWARD)
+    gate_w = weights(0)
+    far_mid = move(pair, MIDDLE)
+    near_out = move(near_mid, PAIR)
     pair_y = move(after(pair, own_y), ACROSS)
-    near = jnp.where(inner(), near, near_out)
-    far_first = far
-    far_out = move(far, OUTWARD)
+    up_w = weights(1, own_y, near_mid, pair)
+    near = jnp.where(inner(), near_mid, near_out)
+    far_out = move(far_mid, PAIR)
     near_y = move(after(near, pair_y), ACROSS)
-    far = jnp.where(inner(), far, far_out)
-    sums = early((own, own_y, pair, after(pair_y, far_first)))
-    far, near_y, *sums = lax.optimization_barrier((far, near_y, *sums))
+    down_w = weights(2, near, pair_y)
+    far = jnp.where(inner(), far_mid, far_out)
+    far, near_y, gate_w, up_w, down_w = lax.optimization_barrier((far, near_y, gate_w, up_w, down_w))
     far_y = move(far, ACROSS)
-    return sums, (near, near_y, far, far_y)
+    return (own, own_y, pair, pair_y, near, near_y), (far, far_y), (gate_w, up_w, down_w)
 
 
 def add(a, b):
@@ -80,12 +81,12 @@
 def scatter(own, own_y, pair, pair_y, near, near_y, far, far_y):
     far_in = move(far_y, ACROSS)
     near_in = move(near_y, ACROSS)
-    pair_in = move(after(pair_y, far_in), ACROSS)
+    pair_in = move(after(pair_y, near_in), ACROSS)
     own_in = move(after(own_y, near_in), ACROSS)
-    far_s = add(far, far_in).astype(BF16)
+    far_s = add(after(far, near), far_in).astype(BF16)
     near_s = add(after(near, far_s), near_in).astype(BF16)
-    far_s = add(far_s, move(far_s, INWARD)).astype(BF16)
-    near_s = add(near_s, move(near_s, INWARD)).astype(BF16)
+    far_s = add(far_s, move(far_s, PAIR)).astype(BF16)
+    near_s = add(near_s, move(near_s, PAIR)).astype(BF16)
     pair_s = (add(pair, pair_in) + move(far_s, MIDDLE).astype(F32)).astype(BF16)
     own_s = add(own, own_in) + move(near_s, MIDDLE).astype(F32)
     return add(own_s, move(pair_s, PAIR)).astype(BF16)
@@ -93,9 +94,9 @@
 
 SWAP = [(0, 1), (1, 0)]
 WHOLE = pl.BlockSpec(memory_space=pltpu.VMEM)
-SCALAR = pl.BlockSpec(memory_space=pltpu.SMEM)
 IN_HBM = pl.BlockSpec(memory_space=pltpu.HBM)
 PIECES = 8
+SCALAR = pl.BlockSpec(memory_space=pltpu.SMEM)
 
 
 def swap(value):
@@ -131,7 +132,7 @@
         out_specs=WHOLE,
         scratch_shapes=[pltpu.SemaphoreType.DMA((PIECES,))],
         compiler_params=pltpu.CompilerParams(vmem_limit_bytes=LIMIT),
-        cost_estimate=pl.CostEstimate(flops=0, bytes_accessed=2 * weight.size, transcendentals=0),
+        cost_estimate=pl.CostEstimate(flops=0, bytes_accessed=1024, transcendentals=0),
         name="prune",
     )(mask, pltpu.with_memory_space_constraint(weight, pltpu.HBM))
 
@@ -140,40 +141,47 @@
     return jnp.where(core == 0, first, second)
 
 
+def halves(core, blocks):
+    n = len(blocks) // 2
+    low, high = jnp.concatenate(blocks[:n]), jnp.concatenate(blocks[n:])
+    return of_core(core, high, low), of_core(core, low, high)
+
+
+def down(core, mine, theirs, down_w, n):
+    low, high = of_core(core, mine, theirs), of_core(core, theirs, mine)
+    return jnp.split(dot(jnp.concatenate([low, high]), down_w).astype(BF16), n)
+
+
+def activated(gate, up):
+    return (jax.nn.silu(gate) * up).astype(BF16)
+
+
 def lined(tokens, gate_weight, up_weight, down_weight, gate_mask, up_mask, down_mask):
     core = lax.axis_index("seq")
-    weights = []
-
-    def halves(blocks):
-        n = len(blocks) // 2
-        low, high = jnp.concatenate(blocks[:n]), jnp.concatenate(blocks[n:])
-        return of_core(core, high, low), of_core(core, low, high)
-
-    def early(blocks):
-        gate_w = prune(gate_weight, gate_mask)
-        up_w = prune(after(up_weight, blocks[1]), up_mask)
-        theirs, mine = halves(blocks)
-        return dot(theirs, gate_w), dot(theirs, up_w), mine, gate_w, up_w
-
-    def hidden(mine, gate_w, up_w, gate_in, up_in):
-        gate, up = dot(mine, gate_w) + gate_in, dot(mine, up_w) + up_in
-        return (jax.nn.silu(gate) * up).astype(BF16)
-
-    def down(mine, theirs, down_w, n):
-        low, high = of_core(core, mine, theirs), of_core(core, theirs, mine)
-        sums = dot(jnp.concatenate([low, high]), down_w).astype(BF16)
-        return jnp.split(sums, n)
-
-    (gate_out, up_out, mine, gate_w, up_w), blocks = gather(tokens, early)
-    down_w = prune(after(down_weight, blocks[1]), down_mask)
-    first = hidden(mine, gate_w, up_w, swap(gate_out), swap(up_out))
-    *blocks, first, down_w = lax.optimization_barrier((*blocks, first, down_w))
-    theirs, mine = halves(blocks)
+    stored = ((gate_weight, gate_mask), (up_weight, up_mask), (down_weight, down_mask))
+
+    def weights(i, *others):
+        weight, mask = stored[i]
+        return prune(after(weight, *others) if others else weight, mask)
+
+    first, last, (gate_w, up_w, down_w) = gather(tokens, weights)
+    theirs, mine = halves(core, first)
     gate_out, up_out = dot(theirs, gate_w), dot(theirs, up_w)
-    second = hidden(mine, gate_w, up_w, swap(gate_out), swap(up_out))
-    parts_far = down(second, swap(second), down_w, 4)
-    parts_near = down(first, swap(first), down_w, 4)
-    return scatter(*parts_near, *parts_far)
+    gate_in, up_in = swap(gate_out), swap(up_out)
+
+    last = (last[0], after(last[1], gate_out, up_out))
+    last_theirs, last_mine = halves(core, last)
+    rows = last_mine.shape[0]
+    last_rows = jnp.concatenate([last_theirs, last_mine])
+    last_gate, last_up = dot(last_rows, gate_w), dot(last_rows, up_w)
+    last_gate_in, last_up_in = swap(last_gate[:rows]), swap(last_up[:rows])
+    gate = dot(after(mine, last_gate, last_up), gate_w) + gate_in
+    last_hidden = activated(last_gate[rows:] + last_gate_in, last_up[rows:] + after(last_up_in, gate))
+    hidden = activated(gate, dot(after(mine, last_hidden), up_w) + up_in)
+
+    last_parts = down(core, last_hidden, after(swap(last_hidden), hidden), down_w, 2)
+    parts = down(core, hidden, swap(hidden), down_w, 6)
+    return scatter(*parts, *last_parts)
 
 
 def solution(mesh):

time: 96 us -> 82.6 us (0.86)
  waiting for transfers between devices: 34.9 us -> 24.3 us
  starting transfers between devices: 28.4 us -> 26 us
    ppermute x18, waiting for transfers between devices: 33.5 us -> 24 us  [move(): return lax.ppermute(value, 'tensor', perm)]
    ppermute x18, starting transfers between devices: 26.9 us -> 24.1 us  [move(): return lax.ppermute(value, 'tensor', perm)]
    ppermute x6, waiting for transfers between devices: 1.49 us -> 0.27 us  [swap(): return lax.ppermute(value, 'seq', SWAP)]
    dot_general x10 -> x8, matrix products: 16.2 us -> 15.6 us  [dot(): return jnp.dot(a, b, preferred_element_type=F32)]
  transfers between devices with their start and end apart: 24 -> 24, of which waited for: 10 -> 8; matrix products, arithmetic and copies ran while one was open for 12% -> 21% of each run, Pallas kernels for 14% -> 16%
where the time goes in v5:
time: 82.6 us; the launch traced here: 82.3 us
  starting transfers between devices  26 us (31%)
  waiting for transfers between devices  24.3 us (29%)
  matrix products  15.6 us (19%)
  Pallas kernels  13.3 us (16%)
  other arithmetic  1.91 us (2%)
  local copies, waits for them, and re-layouts  0.96 us (1%)
    ppermute x18, starting transfers between devices, move(): return lax.ppermute(value, 'tensor', perm)  24.1 us
    ppermute x18, waiting for transfers between devices, move(): return lax.ppermute(value, 'tensor', perm)  24 us
    dot_general x8, matrix products, dot(): return jnp.dot(a, b, preferred_element_type=F32)  15.6 us
    pallas_call x3, Pallas kernels, prune(): pl.pallas_call(prune_kernel, out_shape=pltpu.VMEM(weight.shape, BF16), in...  13.3 us
    ppermute x6, starting transfers between devices, swap(): return lax.ppermute(value, 'seq', SWAP)  1.84 us
  transfers between devices with their start and end apart: 24, of which 8 were waited for; matrix products, arithmetic and copies ran while one was open for 21% of the time, Pallas kernels for 16%

profile of v5, /device:TPU:0, one launch (start us, length us, event | category | flops | bytes accessed | tf_op | source)
XLA Modules:
  0.0 82.3 jit_solution(16477488350017851264)
XLA Ops:
  0.0 3.0 %collective-permute-start.1 = (bf16[64,2048]{1,0:T(8,128)(2,1)}, bf16[64,2048]{1,0:T(8,128)(2,1)S(1)}, u32[]{:S(2)}, u32[]{:S(2)}) collective-permute-start(bf16[64,2048]{1,0:T(8,128)(2,1)} %param.7), channel_id=1, source_target_pairs={{0,4},{2,6},{4,0},{6,2},{8,12},{10,14},{12,8},{14,10},{1,5},{3,7},... | collective-permute-start | bytes 786440 | tf_op jit(solution)/shard_map/ppermute | solution.py:46
  3.0 1.5 %collective-permute-start = (bf16[64,2048]{1,0:T(8,128)(2,1)}, bf16[64,2048]{1,0:T(8,128)(2,1)S(1)}, u32[]{:S(2)}, u32[]{:S(2)}) collective-permute-start(bf16[64,2048]{1,0:T(8,128)(2,1)} %param.7), channel_id=1, source_target_pairs={{0,2},{2,0},{4,6},{6,4},{8,10},{10,8},{12,14},{14,12},{1,3},{3,1},... | collective-permute-start | bytes 786440 | tf_op jit(solution)/shard_map/ppermute | solution.py:46
  5.9 4.4 %prune.3 = bf16[2048,2048]{1,0:T(8,128)(2,1)S(1)} custom-call(s32[16,16]{1,0:T(8,128)S(1)} %copy-done, bf16[2048,2048]{1,0:T(8,128)(2,1)} %weight.1), custom_call_target="tpu_custom_call" | custom-call | bytes 1024 | tf_op jit(solution)/shard_map/prune/pallas_call | solution.py:128
  11.0 1.5 %collective-permute-start.2 = (bf16[64,2048]{1,0:T(8,128)(2,1)S(1)}, bf16[64,2048]{1,0:T(8,128)(2,1)S(1)}, u32[]{:S(2)}, u32[]{:S(2)}) collective-permute-start(bf16[64,2048]{1,0:T(8,128)(2,1)S(1)} %collective-permute-done.1), channel_id=1, source_target_pairs={{0,2},{2,0},{4,6},{6,4},{8,10},{10,8},{12,14},{14,12},{1,3},{3,1},... | collective-permute-start | bytes 786440 | tf_op jit(solution)/shard_map/ppermute | solution.py:46
  13.2 4.4 %collective-permute-start.4 = (bf16[64,2048]{1,0:T(8,128)(2,1)S(1)}, bf16[64,2048]{1,0:T(8,128)(2,1)S(1)}, u32[]{:S(2)}, u32[]{:S(2)}) collective-permute-start(bf16[64,2048]{1,0:T(8,128)(2,1)S(1)} %collective-permute-done.3), channel_id=1, source_target_pairs={{0,4},{2,6},{4,0},{6,2},{8,12},{10,14},{12,8},{14,10},{1,5},{3,7},... | collective-permute-start | bytes 786440 | tf_op jit(solution)/shard_map/ppermute | solution.py:46
  17.7 4.4 %prune.4 = bf16[2048,2048]{1,0:T(8,128)(2,1)S(1)} custom-call(s32[16,16]{1,0:T(8,128)S(1)} %copy-done.1, bf16[2048,2048]{1,0:T(8,128)(2,1)} %weight.2), custom_call_target="tpu_custom_call" | custom-call | bytes 1024 | tf_op jit(solution)/shard_map/prune/pallas_call | solution.py:128
  22.1 2.0 %collective-permute-start.6 = (bf16[64,2048]{1,0:T(8,128)(2,1)S(1)}, bf16[64,2048]{1,0:T(8,128)(2,1)S(1)}, u32[]{:S(2)}, u32[]{:S(2)}) collective-permute-start(bf16[64,2048]{1,0:T(8,128)(2,1)S(1)} %collective-permute-done.5), channel_id=1, source_target_pairs={{0,4},{2,6},{4,0},{6,2},{8,12},{10,14},{12,8},{14,10},{1,5},{3,7},... | collective-permute-start | bytes 786440 | tf_op jit(solution)/shard_map/ppermute | solution.py:46
  24.2 1.6 %collective-permute-start.7 = (bf16[64,2048]{1,0:T(8,128)(2,1)S(1)}, bf16[64,2048]{1,0:T(8,128)(2,1)S(1)}, u32[]{:S(2)}, u32[]{:S(2)}) collective-permute-start(bf16[64,2048]{1,0:T(8,128)(2,1)S(1)} %broadcast_select_fusion.9), channel_id=1, source_target_pairs={{0,2},{2,0},{4,6},{6,4},{8,10},{10,8},{12,14},{14,12},{1,3},{3,1},... | collective-permute-start | bytes 786440 | tf_op jit(solution)/shard_map/ppermute | solution.py:46
  25.8 4.5 %prune.5 = bf16[2048,2048]{1,0:T(8,128)(2,1)S(1)} custom-call(s32[16,16]{1,0:T(8,128)S(1)} %copy-done.2, bf16[2048,2048]{1,0:T(8,128)(2,1)} %weight.3), custom_call_target="tpu_custom_call" | custom-call | bytes 1024 | tf_op jit(solution)/shard_map/prune/pallas_call | solution.py:128
  30.9 1.9 %collective-permute-start.8 = (bf16[64,2048]{1,0:T(8,128)(2,1)S(1)}, bf16[64,2048]{1,0:T(8,128)(2,1)S(1)}, u32[]{:S(2)}, u32[]{:S(2)}) collective-permute-start(bf16[64,2048]{1,0:T(8,128)(2,1)S(1)} %broadcast_select_fusion.8), channel_id=1, source_target_pairs={{0,2},{2,0},{4,6},{6,4},{8,10},{10,8},{12,14},{14,12},{1,3},{3,1},... | collective-permute-start | bytes 786440 | tf_op jit(solution)/shard_map/ppermute | solution.py:46
  32.9 1.9 %fusion.15 = f32[192,2048]{1,0:T(8,128)S(1)} fusion(bf16[2048,2048]{1,0:T(8,128)(2,1)S(1)} %prune.3, bf16[192,2048]{1,0:T(8,128)(2,1)S(1)} %constant_dynamic-update-slice_fusion, pred[]{:T(512)S(6)} %eq.6, bf16[64,2048]{1,0:T(8,128)(2,1)S(1)} %collective-permute-done.7, bf16[64,2048]{1,0:T(8,128)(2,1)S(1)} %broadcast_select_fusion.9, ...), kind=kOutput, calls=%fused_computation.43 | convolution fusion | flops 1613365248 | bytes 11534337 | tf_op jit(solution)/shard_map/dot_general | solution.py:22
  34.8 1.9 %fusion.14 = f32[192,2048]{1,0:T(8,128)S(1)} fusion(bf16[2048,2048]{1,0:T(8,128)(2,1)S(1)} %prune.4, bf16[192,2048]{1,0:T(8,128)(2,1)S(1)} %constant_dynamic-update-slice_fusion, pred[]{:T(512)S(6)} %eq.6, bf16[64,2048]{1,0:T(8,128)(2,1)S(1)} %collective-permute-done.7, bf16[64,2048]{1,0:T(8,128)(2,1)S(1)} %broadcast_select_fusion.9, ...), kind=kOutput, calls=%fused_computation.42 | convolution fusion | flops 1613365248 | bytes 11534337 | tf_op jit(solution)/shard_map/dot_general | solution.py:22
  37.7 1.3 %fusion.8 = f32[128,2048]{1,0:T(8,128)S(1)} fusion(bf16[2048,2048]{1,0:T(8,128)(2,1)S(1)} %prune.4, bf16[64,2048]{1,0:T(8,128)(2,1)S(1)} %get-tuple-element.52, bf16[64,2048]{1,0:T(8,128)(2,1)S(1)} %get-tuple-element.51), kind=kOutput, calls=%fused_computation.27 | convolution fusion | flops 1074790400 | bytes 9961472 | tf_op jit(solution)/shard_map/dot_general | solution.py:22
  41.0 1.9 %convolution_add_fusion.1 = f32[192,2048]{1,0:T(8,128)S(1)} fusion(f32[192,2048]{1,0:T(8,128)S(1)} %collective-permute-done.9, bf16[192,2048]{1,0:T(8,128)(2,1)S(1)} %broadcast_select_fusion.3, bf16[2048,2048]{1,0:T(8,128)(2,1)S(1)} %prune.3), kind=kOutput, calls=%fused_computation.2 | convolution fusion | flops 1611005952 | bytes 12320768 | tf_op jit(solution)/shard_map/dot_general | solution.py:22
  43.5 2.2 %multiply_convert_fusion = bf16[192,2048]{1,0:T(8,128)(2,1)S(1)} fusion(f32[192,2048]{1,0:T(8,128)S(1)} %convolution_add_fusion.1, f32[192,2048]{1,0:T(8,128)S(1)} %collective-permute-done.12, bf16[192,2048]{1,0:T(8,128)(2,1)S(1)} %broadcast_select_fusion.3, bf16[2048,2048]{1,0:T(8,128)(2,1)S(1)} %prune.4), kind=kOutput, calls=%fused_computation.7 | convolution fusion | flops 1613365248 | bytes 13107200 | tf_op jit(solution)/shard_map/dot_general | solution.py:22
  46.3 1.3 %convolution_convert_fusion.1 = bf16[128,2048]{1,0:T(8,128)(2,1)S(1)} fusion(bf16[2048,2048]{1,0:T(8,128)(2,1)S(1)} %prune.5, bf16[64,2048]{1,0:T(8,128)(2,1)S(1)} %get-tuple-element.50, bf16[64,2048]{1,0:T(8,128)(2,1)S(1)} %get-tuple-element.49), kind=kOutput, calls=%fused_computation.3 | convolution fusion | flops 1075052544 | bytes 9437184 | tf_op jit(solution)/shard_map/dot_general | solution.py:22
  47.6 1.7 %collective-permute-start.17 = (bf16[64,2048]{1,0:T(8,128)(2,1)S(1)}, bf16[64,2048]{1,0:T(8,128)(2,1)S(1)}, u32[]{:S(2)}, u32[]{:S(2)}) collective-permute-start(bf16[64,2048]{1,0:T(8,128)(2,1)S(1)} %get-tuple-element.48), channel_id=1, source_target_pairs={{0,2},{2,0},{4,6},{6,4},{8,10},{10,8},{12,14},{14,12},{1,3},{3,1},... | collective-permute-start | bytes 786440 | tf_op jit(solution)/shard_map/ppermute | solution.py:46
  49.4 3.7 %convolution_convert_fusion = bf16[384,2048]{1,0:T(8,128)(2,1)S(1)} fusion(bf16[2048,2048]{1,0:T(8,128)(2,1)S(1)} %prune.5, bf16[192,2048]{1,0:T(8,128)(2,1)S(1)} %get-tuple-element.46, bf16[192,2048]{1,0:T(8,128)(2,1)S(1)} %get-tuple-element.45), kind=kOutput, calls=%fused_computation | convolution fusion | flops 3225157632 | bytes 11534336 | tf_op jit(solution)/shard_map/dot_general | solution.py:22
  53.7 2.5 %collective-permute-done.17 = bf16[64,2048]{1,0:T(8,128)(2,1)S(1)} collective-permute-done((bf16[64,2048]{1,0:T(8,128)(2,1)S(1)}, bf16[64,2048]{1,0:T(8,128)(2,1)S(1)}, u32[]{:S(2)}, u32[]{:S(2)}) %collective-permute-start.17) | collective-permute-done | bytes 262176 | tf_op jit(solution)/shard_map/ppermute | solution.py:46
  56.5 5.2 %collective-permute-done.14 = bf16[64,2048]{1,0:T(8,128)(2,1)S(1)} collective-permute-done((bf16[64,2048]{1,0:T(8,128)(2,1)S(1)}, bf16[64,2048]{1,0:T(8,128)(2,1)S(1)}, u32[]{:S(2)}, u32[]{:S(2)}) %collective-permute-start.14) | collective-permute-done | bytes 262176 | tf_op jit(solution)/shard_map/ppermute | solution.py:46
  61.7 1.6 %collective-permute-start.15 = (bf16[64,2048]{1,0:T(8,128)(2,1)S(1)}, bf16[64,2048]{1,0:T(8,128)(2,1)S(1)}, u32[]{:S(2)}, u32[]{:S(2)}) collective-permute-start(bf16[64,2048]{1,0:T(8,128)(2,1)S(1)} %get-tuple-element.36), channel_id=1, source_target_pairs={{0,2},{2,0},{4,6},{6,4},{8,10},{10,8},{12,14},{14,12},{1,3},{3,1},... | collective-permute-start | bytes 786440 | tf_op jit(solution)/shard_map/ppermute | solution.py:46
  64.7 6.0 %collective-permute-done.18 = bf16[64,2048]{1,0:T(8,128)(2,1)S(1)} collective-permute-done((bf16[64,2048]{1,0:T(8,128)(2,1)S(1)}, bf16[64,2048]{1,0:T(8,128)(2,1)S(1)}, u32[]{:S(2)}, u32[]{:S(2)}) %collective-permute-start.18) | collective-permute-done | bytes 262176 | tf_op jit(solution)/shard_map/ppermute | solution.py:46
  71.4 3.4 %collective-permute-done.20 = bf16[64,2048]{1,0:T(8,128)(2,1)S(1)} collective-permute-done((bf16[64,2048]{1,0:T(8,128)(2,1)S(1)}, bf16[64,2048]{1,0:T(8,128)(2,1)S(1)}, u32[]{:S(2)}, u32[]{:S(2)}) %collective-permute-start.20) | collective-permute-done | bytes 262176 | tf_op jit(solution)/shard_map/ppermute | solution.py:46
  75.7 5.8 %collective-permute-done.23 = bf16[64,2048]{1,0:T(8,128)(2,1)S(1)} collective-permute-done((bf16[64,2048]{1,0:T(8,128)(2,1)S(1)}, bf16[64,2048]{1,0:T(8,128)(2,1)S(1)}, u32[]{:S(2)}, u32[]{:S(2)}) %collective-permute-start.23) | collective-permute-done | bytes 262176 | tf_op jit(solution)/shard_map/ppermute | solution.py:46
  (63 shorter events, 12.3 us)
Async XLA Ops:
  0.0 10.4 %collective-permute-start.1 = (bf16[64,2048]{1,0:T(8,128)(2,1)}, bf16[64,2048]{1,0:T(8,128)(2,1)S(1)}, u32[]{:S(2)}, u32[]{:S(2)}) collective-permute-start(bf16[64,2048]{1,0:T(8,128)(2,1)} %param.7), channel_id=1, source_target_pairs={{0,4},{2,6},{4,0},{6,2},{8,12},{10,14},{12,8},{14,10},{1,5},{3,7},... | collective-permute-start | bytes 786440 | tf_op jit(solution)/shard_map/ppermute | solution.py:46
  3.0 8.0 %collective-permute-start = (bf16[64,2048]{1,0:T(8,128)(2,1)}, bf16[64,2048]{1,0:T(8,128)(2,1)S(1)}, u32[]{:S(2)}, u32[]{:S(2)}) collective-permute-start(bf16[64,2048]{1,0:T(8,128)(2,1)} %param.7), channel_id=1, source_target_pairs={{0,2},{2,0},{4,6},{6,4},{8,10},{10,8},{12,14},{14,12},{1,3},{3,1},... | collective-permute-start | bytes 786440 | tf_op jit(solution)/shard_map/ppermute | solution.py:46
  4.5 8.7 %collective-permute-start.3 = (bf16[64,2048]{1,0:T(8,128)(2,1)}, bf16[64,2048]{1,0:T(8,128)(2,1)S(1)}, u32[]{:S(2)}, u32[]{:S(2)}) collective-permute-start(bf16[64,2048]{1,0:T(8,128)(2,1)} %param.7), channel_id=1, source_target_pairs={{4,8},{6,10},{8,4},{10,6},{5,9},{7,11},{9,5},{11,7},{20,24},{22,26... | collective-permute-start | bytes 786440 | tf_op jit(solution)/shard_map/ppermute | solution.py:46
  11.0 13.2 %collective-permute-start.2 = (bf16[64,2048]{1,0:T(8,128)(2,1)S(1)}, bf16[64,2048]{1,0:T(8,128)(2,1)S(1)}, u32[]{:S(2)}, u32[]{:S(2)}) collective-permute-start(bf16[64,2048]{1,0:T(8,128)(2,1)S(1)} %collective-permute-done.1), channel_id=1, source_target_pairs={{0,2},{2,0},{4,6},{6,4},{8,10},{10,8},{12,14},{14,12},{1,3},{3,1},... | collective-permute-start | bytes 786440 | tf_op jit(solution)/shard_map/ppermute | solution.py:46
  12.5 9.6 %collective-permute-start.5 = (bf16[64,2048]{1,0:T(8,128)(2,1)S(1)}, bf16[64,2048]{1,0:T(8,128)(2,1)S(1)}, u32[]{:S(2)}, u32[]{:S(2)}) collective-permute-start(bf16[64,2048]{1,0:T(8,128)(2,1)S(1)} %collective-permute-done.1), channel_id=1, source_target_pairs={{4,8},{6,10},{8,4},{10,6},{5,9},{7,11},{9,5},{11,7},{20,24},{22,26... | collective-permute-start | bytes 786440 | tf_op jit(solution)/shard_map/ppermute | solution.py:46
  13.2 11.0 %collective-permute-start.4 = (bf16[64,2048]{1,0:T(8,128)(2,1)S(1)}, bf16[64,2048]{1,0:T(8,128)(2,1)S(1)}, u32[]{:S(2)}, u32[]{:S(2)}) collective-permute-start(bf16[64,2048]{1,0:T(8,128)(2,1)S(1)} %collective-permute-done.3), channel_id=1, source_target_pairs={{0,4},{2,6},{4,0},{6,2},{8,12},{10,14},{12,8},{14,10},{1,5},{3,7},... | collective-permute-start | bytes 786440 | tf_op jit(solution)/shard_map/ppermute | solution.py:46
  22.1 8.2 %collective-permute-start.6 = (bf16[64,2048]{1,0:T(8,128)(2,1)S(1)}, bf16[64,2048]{1,0:T(8,128)(2,1)S(1)}, u32[]{:S(2)}, u32[]{:S(2)}) collective-permute-start(bf16[64,2048]{1,0:T(8,128)(2,1)S(1)} %collective-permute-done.5), channel_id=1, source_target_pairs={{0,4},{2,6},{4,0},{6,2},{8,12},{10,14},{12,8},{14,10},{1,5},{3,7},... | collective-permute-start | bytes 786440 | tf_op jit(solution)/shard_map/ppermute | solution.py:46
  24.2 6.7 %collective-permute-start.7 = (bf16[64,2048]{1,0:T(8,128)(2,1)S(1)}, bf16[64,2048]{1,0:T(8,128)(2,1)S(1)}, u32[]{:S(2)}, u32[]{:S(2)}) collective-permute-start(bf16[64,2048]{1,0:T(8,128)(2,1)S(1)} %broadcast_select_fusion.9), channel_id=1, source_target_pairs={{0,2},{2,0},{4,6},{6,4},{8,10},{10,8},{12,14},{14,12},{1,3},{3,1},... | collective-permute-start | bytes 786440 | tf_op jit(solution)/shard_map/ppermute | solution.py:46
  30.9 6.7 %collective-permute-start.8 = (bf16[64,2048]{1,0:T(8,128)(2,1)S(1)}, bf16[64,2048]{1,0:T(8,128)(2,1)S(1)}, u32[]{:S(2)}, u32[]{:S(2)}) collective-permute-start(bf16[64,2048]{1,0:T(8,128)(2,1)S(1)} %broadcast_select_fusion.8), channel_id=1, source_target_pairs={{0,2},{2,0},{4,6},{6,4},{8,10},{10,8},{12,14},{14,12},{1,3},{3,1},... | collective-permute-start | bytes 786440 | tf_op jit(solution)/shard_map/ppermute | solution.py:46
  34.8 6.2 %collective-permute-start.9 = (f32[192,2048]{1,0:T(8,128)S(1)}, f32[192,2048]{1,0:T(8,128)S(1)}, u32[]{:S(2)}, u32[]{:S(2)}) collective-permute-start(f32[192,2048]{1,0:T(8,128)S(1)} %fusion.15), channel_id=1, source_target_pairs={{0,1},{1,0},{2,3},{3,2},{4,5},{5,4},{6,7},{7,6},{8,9},{9,8},{10,11... | collective-permute-start | bytes 4718600 | tf_op jit(solution)/shard_map/ppermute | solution.py:103
  36.8 6.8 %collective-permute-start.12 = (f32[192,2048]{1,0:T(8,128)S(1)}, f32[192,2048]{1,0:T(8,128)S(1)}, u32[]{:S(2)}, u32[]{:S(2)}) collective-permute-start(f32[192,2048]{1,0:T(8,128)S(1)} %fusion.14), channel_id=1, source_target_pairs={{0,1},{1,0},{2,3},{3,2},{4,5},{5,4},{6,7},{7,6},{8,9},{9,8},{10,11... | collective-permute-start | bytes 4718600 | tf_op jit(solution)/shard_map/ppermute | solution.py:103
  40.4 2.5 %collective-permute-start.11 = (f32[64,2048]{1,0:T(8,128)S(1)}, f32[64,2048]{1,0:T(8,128)S(1)}, u32[]{:S(2)}, u32[]{:S(2)}) collective-permute-start(f32[64,2048]{1,0:T(8,128)S(1)} %slice.19), channel_id=1, source_target_pairs={{0,1},{1,0},{2,3},{3,2},{4,5},{5,4},{6,7},{7,6},{8,9},{9,8},{10,11... | collective-permute-start | bytes 1572872 | tf_op jit(solution)/shard_map/ppermute | solution.py:103
  40.5 2.6 %collective-permute-start.10 = (f32[64,2048]{1,0:T(8,128)S(1)}, f32[64,2048]{1,0:T(8,128)S(1)}, u32[]{:S(2)}, u32[]{:S(2)}) collective-permute-start(f32[64,2048]{1,0:T(8,128)S(1)} %slice.17), channel_id=1, source_target_pairs={{0,1},{1,0},{2,3},{3,2},{4,5},{5,4},{6,7},{7,6},{8,9},{9,8},{10,11... | collective-permute-start | bytes 1572872 | tf_op jit(solution)/shard_map/ppermute | solution.py:103
  43.3 2.9 %collective-permute-start.16 = (bf16[64,2048]{1,0:T(8,128)(2,1)S(1)}, bf16[64,2048]{1,0:T(8,128)(2,1)S(1)}, u32[]{:S(2)}, u32[]{:S(2)}) collective-permute-start(bf16[64,2048]{1,0:T(8,128)(2,1)S(1)} %fusion.4), channel_id=1, source_target_pairs={{0,1},{1,0},{2,3},{3,2},{4,5},{5,4},{6,7},{7,6},{8,9},{9,8},{10,11... | collective-permute-start | bytes 786440 | tf_op jit(solution)/shard_map/ppermute | solution.py:103
  45.8 3.5 %collective-permute-start.13 = (bf16[192,2048]{1,0:T(8,128)(2,1)S(1)}, bf16[192,2048]{1,0:T(8,128)(2,1)S(1)}, u32[]{:S(2)}, u32[]{:S(2)}) collective-permute-start(bf16[192,2048]{1,0:T(8,128)(2,1)S(1)} %multiply_convert_fusion), channel_id=1, source_target_pairs={{0,1},{1,0},{2,3},{3,2},{4,5},{5,4},{6,7},{7,6},{8,9},{9,8},{10,11... | collective-permute-start | bytes 2359304 | tf_op jit(solution)/shard_map/ppermute | solution.py:103
  47.6 8.6 %collective-permute-start.17 = (bf16[64,2048]{1,0:T(8,128)(2,1)S(1)}, bf16[64,2048]{1,0:T(8,128)(2,1)S(1)}, u32[]{:S(2)}, u32[]{:S(2)}) collective-permute-start(bf16[64,2048]{1,0:T(8,128)(2,1)S(1)} %get-tuple-element.48), channel_id=1, source_target_pairs={{0,2},{2,0},{4,6},{6,4},{8,10},{10,8},{12,14},{14,12},{1,3},{3,1},... | collective-permute-start | bytes 786440 | tf_op jit(solution)/shard_map/ppermute | solution.py:46
  53.2 8.4 %collective-permute-start.14 = (bf16[64,2048]{1,0:T(8,128)(2,1)S(1)}, bf16[64,2048]{1,0:T(8,128)(2,1)S(1)}, u32[]{:S(2)}, u32[]{:S(2)}) collective-permute-start(bf16[64,2048]{1,0:T(8,128)(2,1)S(1)} %get-tuple-element.44), channel_id=1, source_target_pairs={{0,2},{2,0},{4,6},{6,4},{8,10},{10,8},{12,14},{14,12},{1,3},{3,1},... | collective-permute-start | bytes 786440 | tf_op jit(solution)/shard_map/ppermute | solution.py:46
  56.3 7.6 %collective-permute-start.21 = (bf16[64,2048]{1,0:T(8,128)(2,1)S(1)}, bf16[64,2048]{1,0:T(8,128)(2,1)S(1)}, u32[]{:S(2)}, u32[]{:S(2)}) collective-permute-start(bf16[64,2048]{1,0:T(8,128)(2,1)S(1)} %add_convert_fusion.5), channel_id=1, source_target_pairs={{0,4},{2,6},{4,0},{6,2},{8,12},{10,14},{12,8},{14,10},{1,5},{3,7},... | collective-permute-start | bytes 786440 | tf_op jit(solution)/shard_map/ppermute | solution.py:46
  61.7 14.1 %collective-permute-start.15 = (bf16[64,2048]{1,0:T(8,128)(2,1)S(1)}, bf16[64,2048]{1,0:T(8,128)(2,1)S(1)}, u32[]{:S(2)}, u32[]{:S(2)}) collective-permute-start(bf16[64,2048]{1,0:T(8,128)(2,1)S(1)} %get-tuple-element.36), channel_id=1, source_target_pairs={{0,2},{2,0},{4,6},{6,4},{8,10},{10,8},{12,14},{14,12},{1,3},{3,1},... | collective-permute-start | bytes 786440 | tf_op jit(solution)/shard_map/ppermute | solution.py:46
  63.3 7.3 %collective-permute-start.18 = (bf16[64,2048]{1,0:T(8,128)(2,1)S(1)}, bf16[64,2048]{1,0:T(8,128)(2,1)S(1)}, u32[]{:S(2)}, u32[]{:S(2)}) collective-permute-start(bf16[64,2048]{1,0:T(8,128)(2,1)S(1)} %add_convert_fusion.4), channel_id=1, source_target_pairs={{0,4},{2,6},{4,0},{6,2},{8,12},{10,14},{12,8},{14,10},{1,5},{3,7},... | collective-permute-start | bytes 786440 | tf_op jit(solution)/shard_map/ppermute | solution.py:46
  63.5 11.2 %collective-permute-start.20 = (bf16[64,2048]{1,0:T(8,128)(2,1)S(1)}, bf16[64,2048]{1,0:T(8,128)(2,1)S(1)}, u32[]{:S(2)}, u32[]{:S(2)}) collective-permute-start(bf16[64,2048]{1,0:T(8,128)(2,1)S(1)} %get-tuple-element.40), channel_id=1, source_target_pairs={{0,2},{2,0},{4,6},{6,4},{8,10},{10,8},{12,14},{14,12},{1,3},{3,1},... | collective-permute-start | bytes 786440 | tf_op jit(solution)/shard_map/ppermute | solution.py:46
  64.0 10.8 %collective-permute-start.22 = (bf16[64,2048]{1,0:T(8,128)(2,1)S(1)}, bf16[64,2048]{1,0:T(8,128)(2,1)S(1)}, u32[]{:S(2)}, u32[]{:S(2)}) collective-permute-start(bf16[64,2048]{1,0:T(8,128)(2,1)S(1)} %add_convert_fusion.2), channel_id=1, source_target_pairs={{4,8},{6,10},{8,4},{10,6},{5,9},{7,11},{9,5},{11,7},{20,24},{22,26... | collective-permute-start | bytes 786440 | tf_op jit(solution)/shard_map/ppermute | solution.py:46
  70.7 5.0 %collective-permute-start.19 = (bf16[64,2048]{1,0:T(8,128)(2,1)S(1)}, bf16[64,2048]{1,0:T(8,128)(2,1)S(1)}, u32[]{:S(2)}, u32[]{:S(2)}) collective-permute-start(bf16[64,2048]{1,0:T(8,128)(2,1)S(1)} %add_convert_fusion.3), channel_id=1, source_target_pairs={{4,8},{6,10},{8,4},{10,6},{5,9},{7,11},{9,5},{11,7},{20,24},{22,26... | collective-permute-start | bytes 786440 | tf_op jit(solution)/shard_map/ppermute | solution.py:46
  74.9 6.6 %collective-permute-start.23 = (bf16[64,2048]{1,0:T(8,128)(2,1)S(1)}, bf16[64,2048]{1,0:T(8,128)(2,1)S(1)}, u32[]{:S(2)}, u32[]{:S(2)}) collective-permute-start(bf16[64,2048]{1,0:T(8,128)(2,1)S(1)} %add_convert_fusion.1), channel_id=1, source_target_pairs={{0,4},{2,6},{4,0},{6,2},{8,12},{10,14},{12,8},{14,10},{1,5},{3,7},... | collective-permute-start | bytes 786440 | tf_op jit(solution)/shard_map/ppermute | solution.py:46
  (4 other events, 24.9 us)

commit v6 on v5

--- a/solution.py
+++ b/solution.py
@@ -81,14 +81,14 @@
 def scatter(own, own_y, pair, pair_y, near, near_y, far, far_y):
     far_in = move(far_y, ACROSS)
     near_in = move(near_y, ACROSS)
-    pair_in = move(after(pair_y, near_in), ACROSS)
-    own_in = move(after(own_y, near_in), ACROSS)
     far_s = add(after(far, near), far_in).astype(BF16)
+    far_t = add(far_s, move(far_s, PAIR)).astype(BF16)
     near_s = add(after(near, far_s), near_in).astype(BF16)
-    far_s = add(far_s, move(far_s, PAIR)).astype(BF16)
-    near_s = add(near_s, move(near_s, PAIR)).astype(BF16)
-    pair_s = (add(pair, pair_in) + move(far_s, MIDDLE).astype(F32)).astype(BF16)
-    own_s = add(own, own_in) + move(near_s, MIDDLE).astype(F32)
+    pair_in = move(after(pair_y, far_s), ACROSS)
+    near_t = add(near_s, move(near_s, PAIR)).astype(BF16)
+    own_in = move(after(own_y, far_t), ACROSS)
+    pair_s = (add(pair, pair_in) + move(far_t, MIDDLE).astype(F32)).astype(BF16)
+    own_s = add(own, own_in) + move(near_t, MIDDLE).astype(F32)
     return add(own_s, move(pair_s, PAIR)).astype(BF16)
 
 

time: 82.6 us -> 80.3 us (0.972)
  waiting for transfers between devices: 24.3 us -> 16.1 us
  starting transfers between devices: 26 us -> 31.8 us
    ppermute x18, waiting for transfers between devices: 24 us -> 15.9 us  [move(): return lax.ppermute(value, 'tensor', perm)]
    ppermute x18, starting transfers between devices: 24.1 us -> 29.9 us  [move(): return lax.ppermute(value, 'tensor', perm)]
  transfers between devices with their start and end apart: 24 -> 24, of which waited for: 8 -> 8; matrix products, arithmetic and copies ran while one was open for 21% -> 21% of each run, Pallas kernels for 16% -> 17%
where the time goes in v6:
time: 80.3 us; the launch traced here: 80.1 us
  starting transfers between devices  31.8 us (40%)
  waiting for transfers between devices  16.1 us (20%)
  matrix products  15.6 us (19%)
  Pallas kernels  13.3 us (17%)
  other arithmetic  1.91 us (2%)
  local copies, waits for them, and re-layouts  0.96 us (1%)
    ppermute x18, starting transfers between devices, move(): return lax.ppermute(value, 'tensor', perm)  29.9 us
    ppermute x18, waiting for transfers between devices, move(): return lax.ppermute(value, 'tensor', perm)  15.9 us
    dot_general x8, matrix products, dot(): return jnp.dot(a, b, preferred_element_type=F32)  15.6 us
    pallas_call x3, Pallas kernels, prune(): pl.pallas_call(prune_kernel, out_shape=pltpu.VMEM(weight.shape, BF16), in...  13.3 us
    ppermute x6, starting transfers between devices, swap(): return lax.ppermute(value, 'seq', SWAP)  1.84 us
  transfers between devices with their start and end apart: 24, of which 8 were waited for; matrix products, arithmetic and copies ran while one was open for 21% of the time, Pallas kernels for 17%

profile of v6, /device:TPU:0, one launch (start us, length us, event | category | flops | bytes accessed | tf_op | source)
XLA Modules:
  0.0 80.1 jit_solution(14400431658983710431)
XLA Ops:
  0.0 3.0 %collective-permute-start.1 = (bf16[64,2048]{1,0:T(8,128)(2,1)}, bf16[64,2048]{1,0:T(8,128)(2,1)S(1)}, u32[]{:S(2)}, u32[]{:S(2)}) collective-permute-start(bf16[64,2048]{1,0:T(8,128)(2,1)} %param.7), channel_id=1, source_target_pairs={{0,4},{2,6},{4,0},{6,2},{8,12},{10,14},{12,8},{14,10},{1,5},{3,7},... | collective-permute-start | bytes 786440 | tf_op jit(solution)/shard_map/ppermute | solution.py:46
  3.0 1.5 %collective-permute-start = (bf16[64,2048]{1,0:T(8,128)(2,1)}, bf16[64,2048]{1,0:T(8,128)(2,1)S(1)}, u32[]{:S(2)}, u32[]{:S(2)}) collective-permute-start(bf16[64,2048]{1,0:T(8,128)(2,1)} %param.7), channel_id=1, source_target_pairs={{0,2},{2,0},{4,6},{6,4},{8,10},{10,8},{12,14},{14,12},{1,3},{3,1},... | collective-permute-start | bytes 786440 | tf_op jit(solution)/shard_map/ppermute | solution.py:46
  5.9 4.4 %prune.3 = bf16[2048,2048]{1,0:T(8,128)(2,1)S(1)} custom-call(s32[16,16]{1,0:T(8,128)S(1)} %copy-done, bf16[2048,2048]{1,0:T(8,128)(2,1)} %weight.1), custom_call_target="tpu_custom_call" | custom-call | bytes 1024 | tf_op jit(solution)/shard_map/prune/pallas_call | solution.py:128
  11.0 1.5 %collective-permute-start.2 = (bf16[64,2048]{1,0:T(8,128)(2,1)S(1)}, bf16[64,2048]{1,0:T(8,128)(2,1)S(1)}, u32[]{:S(2)}, u32[]{:S(2)}) collective-permute-start(bf16[64,2048]{1,0:T(8,128)(2,1)S(1)} %collective-permute-done.1), channel_id=1, source_target_pairs={{0,2},{2,0},{4,6},{6,4},{8,10},{10,8},{12,14},{14,12},{1,3},{3,1},... | collective-permute-start | bytes 786440 | tf_op jit(solution)/shard_map/ppermute | solution.py:46
  13.2 4.4 %collective-permute-start.4 = (bf16[64,2048]{1,0:T(8,128)(2,1)S(1)}, bf16[64,2048]{1,0:T(8,128)(2,1)S(1)}, u32[]{:S(2)}, u32[]{:S(2)}) collective-permute-start(bf16[64,2048]{1,0:T(8,128)(2,1)S(1)} %collective-permute-done.3), channel_id=1, source_target_pairs={{0,4},{2,6},{4,0},{6,2},{8,12},{10,14},{12,8},{14,10},{1,5},{3,7},... | collective-permute-start | bytes 786440 | tf_op jit(solution)/shard_map/ppermute | solution.py:46
  17.7 4.4 %prune.4 = bf16[2048,2048]{1,0:T(8,128)(2,1)S(1)} custom-call(s32[16,16]{1,0:T(8,128)S(1)} %copy-done.1, bf16[2048,2048]{1,0:T(8,128)(2,1)} %weight.2), custom_call_target="tpu_custom_call" | custom-call | bytes 1024 | tf_op jit(solution)/shard_map/prune/pallas_call | solution.py:128
  22.1 1.9 %collective-permute-start.6 = (bf16[64,2048]{1,0:T(8,128)(2,1)S(1)}, bf16[64,2048]{1,0:T(8,128)(2,1)S(1)}, u32[]{:S(2)}, u32[]{:S(2)}) collective-permute-start(bf16[64,2048]{1,0:T(8,128)(2,1)S(1)} %collective-permute-done.5), channel_id=1, source_target_pairs={{0,4},{2,6},{4,0},{6,2},{8,12},{10,14},{12,8},{14,10},{1,5},{3,7},... | collective-permute-start | bytes 786440 | tf_op jit(solution)/shard_map/ppermute | solution.py:46
  24.1 1.6 %collective-permute-start.7 = (bf16[64,2048]{1,0:T(8,128)(2,1)S(1)}, bf16[64,2048]{1,0:T(8,128)(2,1)S(1)}, u32[]{:S(2)}, u32[]{:S(2)}) collective-permute-start(bf16[64,2048]{1,0:T(8,128)(2,1)S(1)} %broadcast_select_fusion.9), channel_id=1, source_target_pairs={{0,2},{2,0},{4,6},{6,4},{8,10},{10,8},{12,14},{14,12},{1,3},{3,1},... | collective-permute-start | bytes 786440 | tf_op jit(solution)/shard_map/ppermute | solution.py:46
  25.8 4.5 %prune.5 = bf16[2048,2048]{1,0:T(8,128)(2,1)S(1)} custom-call(s32[16,16]{1,0:T(8,128)S(1)} %copy-done.2, bf16[2048,2048]{1,0:T(8,128)(2,1)} %weight.3), custom_call_target="tpu_custom_call" | custom-call | bytes 1024 | tf_op jit(solution)/shard_map/prune/pallas_call | solution.py:128
  30.9 2.0 %collective-permute-start.8 = (bf16[64,2048]{1,0:T(8,128)(2,1)S(1)}, bf16[64,2048]{1,0:T(8,128)(2,1)S(1)}, u32[]{:S(2)}, u32[]{:S(2)}) collective-permute-start(bf16[64,2048]{1,0:T(8,128)(2,1)S(1)} %broadcast_select_fusion.8), channel_id=1, source_target_pairs={{0,2},{2,0},{4,6},{6,4},{8,10},{10,8},{12,14},{14,12},{1,3},{3,1},... | collective-permute-start | bytes 786440 | tf_op jit(solution)/shard_map/ppermute | solution.py:46
  32.8 1.9 %fusion.15 = f32[192,2048]{1,0:T(8,128)S(1)} fusion(bf16[2048,2048]{1,0:T(8,128)(2,1)S(1)} %prune.3, bf16[192,2048]{1,0:T(8,128)(2,1)S(1)} %constant_dynamic-update-slice_fusion, pred[]{:T(512)S(6)} %eq.6, bf16[64,2048]{1,0:T(8,128)(2,1)S(1)} %collective-permute-done.7, bf16[64,2048]{1,0:T(8,128)(2,1)S(1)} %broadcast_select_fusion.9, ...), kind=kOutput, calls=%fused_computation.43 | convolution fusion | flops 1613365248 | bytes 11534337 | tf_op jit(solution)/shard_map/dot_general | solution.py:22
  34.8 1.9 %fusion.14 = f32[192,2048]{1,0:T(8,128)S(1)} fusion(bf16[2048,2048]{1,0:T(8,128)(2,1)S(1)} %prune.4, bf16[192,2048]{1,0:T(8,128)(2,1)S(1)} %constant_dynamic-update-slice_fusion, pred[]{:T(512)S(6)} %eq.6, bf16[64,2048]{1,0:T(8,128)(2,1)S(1)} %collective-permute-done.7, bf16[64,2048]{1,0:T(8,128)(2,1)S(1)} %broadcast_select_fusion.9, ...), kind=kOutput, calls=%fused_computation.42 | convolution fusion | flops 1613365248 | bytes 11534337 | tf_op jit(solution)/shard_map/dot_general | solution.py:22
  39.0 1.3 %fusion.9 = f32[128,2048]{1,0:T(8,128)S(1)} fusion(bf16[2048,2048]{1,0:T(8,128)(2,1)S(1)} %prune.3, bf16[64,2048]{1,0:T(8,128)(2,1)S(1)} %get-tuple-element.52, bf16[64,2048]{1,0:T(8,128)(2,1)S(1)} %get-tuple-element.51), kind=kOutput, calls=%fused_computation.28 | convolution fusion | flops 1074790400 | bytes 9961472 | tf_op jit(solution)/shard_map/dot_general | solution.py:22
  40.9 1.9 %convolution_add_fusion.1 = f32[192,2048]{1,0:T(8,128)S(1)} fusion(f32[192,2048]{1,0:T(8,128)S(1)} %collective-permute-done.9, bf16[192,2048]{1,0:T(8,128)(2,1)S(1)} %broadcast_select_fusion.3, bf16[2048,2048]{1,0:T(8,128)(2,1)S(1)} %prune.3), kind=kOutput, calls=%fused_computation.2 | convolution fusion | flops 1611005952 | bytes 12320768 | tf_op jit(solution)/shard_map/dot_general | solution.py:22
  43.5 2.2 %multiply_convert_fusion = bf16[192,2048]{1,0:T(8,128)(2,1)S(1)} fusion(f32[192,2048]{1,0:T(8,128)S(1)} %convolution_add_fusion.1, f32[192,2048]{1,0:T(8,128)S(1)} %collective-permute-done.12, bf16[192,2048]{1,0:T(8,128)(2,1)S(1)} %broadcast_select_fusion.3, bf16[2048,2048]{1,0:T(8,128)(2,1)S(1)} %prune.4), kind=kOutput, calls=%fused_computation.7 | convolution fusion | flops 1613365248 | bytes 13107200 | tf_op jit(solution)/shard_map/dot_general | solution.py:22
  47.6 1.7 %collective-permute-start.15 = (bf16[64,2048]{1,0:T(8,128)(2,1)S(1)}, bf16[64,2048]{1,0:T(8,128)(2,1)S(1)}, u32[]{:S(2)}, u32[]{:S(2)}) collective-permute-start(bf16[64,2048]{1,0:T(8,128)(2,1)S(1)} %get-tuple-element.48), channel_id=1, source_target_pairs={{0,2},{2,0},{4,6},{6,4},{8,10},{10,8},{12,14},{14,12},{1,3},{3,1},... | collective-permute-start | bytes 786440 | tf_op jit(solution)/shard_map/ppermute | solution.py:46
  49.4 3.7 %convolution_convert_fusion = bf16[384,2048]{1,0:T(8,128)(2,1)S(1)} fusion(bf16[2048,2048]{1,0:T(8,128)(2,1)S(1)} %prune.5, bf16[192,2048]{1,0:T(8,128)(2,1)S(1)} %get-tuple-element.46, bf16[192,2048]{1,0:T(8,128)(2,1)S(1)} %get-tuple-element.45), kind=kOutput, calls=%fused_computation | convolution fusion | flops 3225157632 | bytes 11534336 | tf_op jit(solution)/shard_map/dot_general | solution.py:22
  53.7 2.5 %collective-permute-done.15 = bf16[64,2048]{1,0:T(8,128)(2,1)S(1)} collective-permute-done((bf16[64,2048]{1,0:T(8,128)(2,1)S(1)}, bf16[64,2048]{1,0:T(8,128)(2,1)S(1)}, u32[]{:S(2)}, u32[]{:S(2)}) %collective-permute-start.15) | collective-permute-done | bytes 262176 | tf_op jit(solution)/shard_map/ppermute | solution.py:46
  56.5 2.2 %collective-permute-start.21 = (bf16[64,2048]{1,0:T(8,128)(2,1)S(1)}, bf16[64,2048]{1,0:T(8,128)(2,1)S(1)}, u32[]{:S(2)}, u32[]{:S(2)}) collective-permute-start(bf16[64,2048]{1,0:T(8,128)(2,1)S(1)} %get-tuple-element.40), channel_id=1, source_target_pairs={{0,2},{2,0},{4,6},{6,4},{8,10},{10,8},{12,14},{14,12},{1,3},{3,1},... | collective-permute-start | bytes 786440 | tf_op jit(solution)/shard_map/ppermute | solution.py:46
  58.7 3.8 %collective-permute-done.18 = bf16[64,2048]{1,0:T(8,128)(2,1)S(1)} collective-permute-done((bf16[64,2048]{1,0:T(8,128)(2,1)S(1)}, bf16[64,2048]{1,0:T(8,128)(2,1)S(1)}, u32[]{:S(2)}, u32[]{:S(2)}) %collective-permute-start.18) | collective-permute-done | bytes 262176 | tf_op jit(solution)/shard_map/ppermute | solution.py:46
  64.4 1.7 %collective-permute-start.17 = (bf16[64,2048]{1,0:T(8,128)(2,1)S(1)}, bf16[64,2048]{1,0:T(8,128)(2,1)S(1)}, u32[]{:S(2)}, u32[]{:S(2)}) collective-permute-start(bf16[64,2048]{1,0:T(8,128)(2,1)S(1)} %get-tuple-element.38), channel_id=1, source_target_pairs={{0,2},{2,0},{4,6},{6,4},{8,10},{10,8},{12,14},{14,12},{1,3},{3,1},... | collective-permute-start | bytes 786440 | tf_op jit(solution)/shard_map/ppermute | solution.py:46
  66.1 3.2 %collective-permute-done.19 = bf16[64,2048]{1,0:T(8,128)(2,1)S(1)} collective-permute-done((bf16[64,2048]{1,0:T(8,128)(2,1)S(1)}, bf16[64,2048]{1,0:T(8,128)(2,1)S(1)}, u32[]{:S(2)}, u32[]{:S(2)}) %collective-permute-start.19) | collective-permute-done | bytes 262176 | tf_op jit(solution)/shard_map/ppermute | solution.py:46
  70.2 4.7 %collective-permute-start.23 = (bf16[64,2048]{1,0:T(8,128)(2,1)S(1)}, bf16[64,2048]{1,0:T(8,128)(2,1)S(1)}, u32[]{:S(2)}, u32[]{:S(2)}) collective-permute-start(bf16[64,2048]{1,0:T(8,128)(2,1)S(1)} %add_convert_fusion.1), channel_id=1, source_target_pairs={{0,4},{2,6},{4,0},{6,2},{8,12},{10,14},{12,8},{14,10},{1,5},{3,7},... | collective-permute-start | bytes 786440 | tf_op jit(solution)/shard_map/ppermute | solution.py:46
  74.9 4.3 %collective-permute-done.23 = bf16[64,2048]{1,0:T(8,128)(2,1)S(1)} collective-permute-done((bf16[64,2048]{1,0:T(8,128)(2,1)S(1)}, bf16[64,2048]{1,0:T(8,128)(2,1)S(1)}, u32[]{:S(2)}, u32[]{:S(2)}) %collective-permute-start.23) | collective-permute-done | bytes 262176 | tf_op jit(solution)/shard_map/ppermute | solution.py:46
  (63 shorter events, 13.3 us)
Async XLA Ops:
  0.0 10.4 %collective-permute-start.1 = (bf16[64,2048]{1,0:T(8,128)(2,1)}, bf16[64,2048]{1,0:T(8,128)(2,1)S(1)}, u32[]{:S(2)}, u32[]{:S(2)}) collective-permute-start(bf16[64,2048]{1,0:T(8,128)(2,1)} %param.7), channel_id=1, source_target_pairs={{0,4},{2,6},{4,0},{6,2},{8,12},{10,14},{12,8},{14,10},{1,5},{3,7},... | collective-permute-start | bytes 786440 | tf_op jit(solution)/shard_map/ppermute | solution.py:46
  3.0 8.0 %collective-permute-start = (bf16[64,2048]{1,0:T(8,128)(2,1)}, bf16[64,2048]{1,0:T(8,128)(2,1)S(1)}, u32[]{:S(2)}, u32[]{:S(2)}) collective-permute-start(bf16[64,2048]{1,0:T(8,128)(2,1)} %param.7), channel_id=1, source_target_pairs={{0,2},{2,0},{4,6},{6,4},{8,10},{10,8},{12,14},{14,12},{1,3},{3,1},... | collective-permute-start | bytes 786440 | tf_op jit(solution)/shard_map/ppermute | solution.py:46
  4.5 8.7 %collective-permute-start.3 = (bf16[64,2048]{1,0:T(8,128)(2,1)}, bf16[64,2048]{1,0:T(8,128)(2,1)S(1)}, u32[]{:S(2)}, u32[]{:S(2)}) collective-permute-start(bf16[64,2048]{1,0:T(8,128)(2,1)} %param.7), channel_id=1, source_target_pairs={{4,8},{6,10},{8,4},{10,6},{5,9},{7,11},{9,5},{11,7},{20,24},{22,26... | collective-permute-start | bytes 786440 | tf_op jit(solution)/shard_map/ppermute | solution.py:46
  11.0 13.1 %collective-permute-start.2 = (bf16[64,2048]{1,0:T(8,128)(2,1)S(1)}, bf16[64,2048]{1,0:T(8,128)(2,1)S(1)}, u32[]{:S(2)}, u32[]{:S(2)}) collective-permute-start(bf16[64,2048]{1,0:T(8,128)(2,1)S(1)} %collective-permute-done.1), channel_id=1, source_target_pairs={{0,2},{2,0},{4,6},{6,4},{8,10},{10,8},{12,14},{14,12},{1,3},{3,1},... | collective-permute-start | bytes 786440 | tf_op jit(solution)/shard_map/ppermute | solution.py:46
  12.5 9.6 %collective-permute-start.5 = (bf16[64,2048]{1,0:T(8,128)(2,1)S(1)}, bf16[64,2048]{1,0:T(8,128)(2,1)S(1)}, u32[]{:S(2)}, u32[]{:S(2)}) collective-permute-start(bf16[64,2048]{1,0:T(8,128)(2,1)S(1)} %collective-permute-done.1), channel_id=1, source_target_pairs={{4,8},{6,10},{8,4},{10,6},{5,9},{7,11},{9,5},{11,7},{20,24},{22,26... | collective-permute-start | bytes 786440 | tf_op jit(solution)/shard_map/ppermute | solution.py:46
  13.2 10.9 %collective-permute-start.4 = (bf16[64,2048]{1,0:T(8,128)(2,1)S(1)}, bf16[64,2048]{1,0:T(8,128)(2,1)S(1)}, u32[]{:S(2)}, u32[]{:S(2)}) collective-permute-start(bf16[64,2048]{1,0:T(8,128)(2,1)S(1)} %collective-permute-done.3), channel_id=1, source_target_pairs={{0,4},{2,6},{4,0},{6,2},{8,12},{10,14},{12,8},{14,10},{1,5},{3,7},... | collective-permute-start | bytes 786440 | tf_op jit(solution)/shard_map/ppermute | solution.py:46
  22.1 8.2 %collective-permute-start.6 = (bf16[64,2048]{1,0:T(8,128)(2,1)S(1)}, bf16[64,2048]{1,0:T(8,128)(2,1)S(1)}, u32[]{:S(2)}, u32[]{:S(2)}) collective-permute-start(bf16[64,2048]{1,0:T(8,128)(2,1)S(1)} %collective-permute-done.5), channel_id=1, source_target_pairs={{0,4},{2,6},{4,0},{6,2},{8,12},{10,14},{12,8},{14,10},{1,5},{3,7},... | collective-permute-start | bytes 786440 | tf_op jit(solution)/shard_map/ppermute | solution.py:46
  24.1 6.7 %collective-permute-start.7 = (bf16[64,2048]{1,0:T(8,128)(2,1)S(1)}, bf16[64,2048]{1,0:T(8,128)(2,1)S(1)}, u32[]{:S(2)}, u32[]{:S(2)}) collective-permute-start(bf16[64,2048]{1,0:T(8,128)(2,1)S(1)} %broadcast_select_fusion.9), channel_id=1, source_target_pairs={{0,2},{2,0},{4,6},{6,4},{8,10},{10,8},{12,14},{14,12},{1,3},{3,1},... | collective-permute-start | bytes 786440 | tf_op jit(solution)/shard_map/ppermute | solution.py:46
  30.9 6.7 %collective-permute-start.8 = (bf16[64,2048]{1,0:T(8,128)(2,1)S(1)}, bf16[64,2048]{1,0:T(8,128)(2,1)S(1)}, u32[]{:S(2)}, u32[]{:S(2)}) collective-permute-start(bf16[64,2048]{1,0:T(8,128)(2,1)S(1)} %broadcast_select_fusion.8), channel_id=1, source_target_pairs={{0,2},{2,0},{4,6},{6,4},{8,10},{10,8},{12,14},{14,12},{1,3},{3,1},... | collective-permute-start | bytes 786440 | tf_op jit(solution)/shard_map/ppermute | solution.py:46
  34.7 6.2 %collective-permute-start.9 = (f32[192,2048]{1,0:T(8,128)S(1)}, f32[192,2048]{1,0:T(8,128)S(1)}, u32[]{:S(2)}, u32[]{:S(2)}) collective-permute-start(f32[192,2048]{1,0:T(8,128)S(1)} %fusion.15), channel_id=1, source_target_pairs={{0,1},{1,0},{2,3},{3,2},{4,5},{5,4},{6,7},{7,6},{8,9},{9,8},{10,11... | collective-permute-start | bytes 4718600 | tf_op jit(solution)/shard_map/ppermute | solution.py:103
  36.7 6.8 %collective-permute-start.12 = (f32[192,2048]{1,0:T(8,128)S(1)}, f32[192,2048]{1,0:T(8,128)S(1)}, u32[]{:S(2)}, u32[]{:S(2)}) collective-permute-start(f32[192,2048]{1,0:T(8,128)S(1)} %fusion.14), channel_id=1, source_target_pairs={{0,1},{1,0},{2,3},{3,2},{4,5},{5,4},{6,7},{7,6},{8,9},{9,8},{10,11... | collective-permute-start | bytes 4718600 | tf_op jit(solution)/shard_map/ppermute | solution.py:103
  40.4 2.5 %collective-permute-start.11 = (f32[64,2048]{1,0:T(8,128)S(1)}, f32[64,2048]{1,0:T(8,128)S(1)}, u32[]{:S(2)}, u32[]{:S(2)}) collective-permute-start(f32[64,2048]{1,0:T(8,128)S(1)} %slice.19), channel_id=1, source_target_pairs={{0,1},{1,0},{2,3},{3,2},{4,5},{5,4},{6,7},{7,6},{8,9},{9,8},{10,11... | collective-permute-start | bytes 1572872 | tf_op jit(solution)/shard_map/ppermute | solution.py:103
  40.4 2.6 %collective-permute-start.10 = (f32[64,2048]{1,0:T(8,128)S(1)}, f32[64,2048]{1,0:T(8,128)S(1)}, u32[]{:S(2)}, u32[]{:S(2)}) collective-permute-start(f32[64,2048]{1,0:T(8,128)S(1)} %slice.17), channel_id=1, source_target_pairs={{0,1},{1,0},{2,3},{3,2},{4,5},{5,4},{6,7},{7,6},{8,9},{9,8},{10,11... | collective-permute-start | bytes 1572872 | tf_op jit(solution)/shard_map/ppermute | solution.py:103
  43.3 2.9 %collective-permute-start.14 = (bf16[64,2048]{1,0:T(8,128)(2,1)S(1)}, bf16[64,2048]{1,0:T(8,128)(2,1)S(1)}, u32[]{:S(2)}, u32[]{:S(2)}) collective-permute-start(bf16[64,2048]{1,0:T(8,128)(2,1)S(1)} %fusion.4), channel_id=1, source_target_pairs={{0,1},{1,0},{2,3},{3,2},{4,5},{5,4},{6,7},{7,6},{8,9},{9,8},{10,11... | collective-permute-start | bytes 786440 | tf_op jit(solution)/shard_map/ppermute | solution.py:103
  45.7 3.5 %collective-permute-start.13 = (bf16[192,2048]{1,0:T(8,128)(2,1)S(1)}, bf16[192,2048]{1,0:T(8,128)(2,1)S(1)}, u32[]{:S(2)}, u32[]{:S(2)}) collective-permute-start(bf16[192,2048]{1,0:T(8,128)(2,1)S(1)} %multiply_convert_fusion), channel_id=1, source_target_pairs={{0,1},{1,0},{2,3},{3,2},{4,5},{5,4},{6,7},{7,6},{8,9},{9,8},{10,11... | collective-permute-start | bytes 2359304 | tf_op jit(solution)/shard_map/ppermute | solution.py:103
  47.6 8.6 %collective-permute-start.15 = (bf16[64,2048]{1,0:T(8,128)(2,1)S(1)}, bf16[64,2048]{1,0:T(8,128)(2,1)S(1)}, u32[]{:S(2)}, u32[]{:S(2)}) collective-permute-start(bf16[64,2048]{1,0:T(8,128)(2,1)S(1)} %get-tuple-element.48), channel_id=1, source_target_pairs={{0,2},{2,0},{4,6},{6,4},{8,10},{10,8},{12,14},{14,12},{1,3},{3,1},... | collective-permute-start | bytes 786440 | tf_op jit(solution)/shard_map/ppermute | solution.py:46
  53.2 9.3 %collective-permute-start.18 = (bf16[64,2048]{1,0:T(8,128)(2,1)S(1)}, bf16[64,2048]{1,0:T(8,128)(2,1)S(1)}, u32[]{:S(2)}, u32[]{:S(2)}) collective-permute-start(bf16[64,2048]{1,0:T(8,128)(2,1)S(1)} %get-tuple-element.43), channel_id=1, source_target_pairs={{0,2},{2,0},{4,6},{6,4},{8,10},{10,8},{12,14},{14,12},{1,3},{3,1},... | collective-permute-start | bytes 786440 | tf_op jit(solution)/shard_map/ppermute | solution.py:46
  56.3 7.4 %collective-permute-start.16 = (bf16[64,2048]{1,0:T(8,128)(2,1)S(1)}, bf16[64,2048]{1,0:T(8,128)(2,1)S(1)}, u32[]{:S(2)}, u32[]{:S(2)}) collective-permute-start(bf16[64,2048]{1,0:T(8,128)(2,1)S(1)} %add_convert_fusion.5), channel_id=1, source_target_pairs={{0,4},{2,6},{4,0},{6,2},{8,12},{10,14},{12,8},{14,10},{1,5},{3,7},... | collective-permute-start | bytes 786440 | tf_op jit(solution)/shard_map/ppermute | solution.py:46
  56.5 13.6 %collective-permute-start.21 = (bf16[64,2048]{1,0:T(8,128)(2,1)S(1)}, bf16[64,2048]{1,0:T(8,128)(2,1)S(1)}, u32[]{:S(2)}, u32[]{:S(2)}) collective-permute-start(bf16[64,2048]{1,0:T(8,128)(2,1)S(1)} %get-tuple-element.40), channel_id=1, source_target_pairs={{0,2},{2,0},{4,6},{6,4},{8,10},{10,8},{12,14},{14,12},{1,3},{3,1},... | collective-permute-start | bytes 786440 | tf_op jit(solution)/shard_map/ppermute | solution.py:46
  62.5 6.7 %collective-permute-start.19 = (bf16[64,2048]{1,0:T(8,128)(2,1)S(1)}, bf16[64,2048]{1,0:T(8,128)(2,1)S(1)}, u32[]{:S(2)}, u32[]{:S(2)}) collective-permute-start(bf16[64,2048]{1,0:T(8,128)(2,1)S(1)} %add_convert_fusion.3), channel_id=1, source_target_pairs={{0,4},{2,6},{4,0},{6,2},{8,12},{10,14},{12,8},{14,10},{1,5},{3,7},... | collective-permute-start | bytes 786440 | tf_op jit(solution)/shard_map/ppermute | solution.py:46
  63.7 6.3 %collective-permute-start.22 = (bf16[64,2048]{1,0:T(8,128)(2,1)S(1)}, bf16[64,2048]{1,0:T(8,128)(2,1)S(1)}, u32[]{:S(2)}, u32[]{:S(2)}) collective-permute-start(bf16[64,2048]{1,0:T(8,128)(2,1)S(1)} %add_convert_fusion.4), channel_id=1, source_target_pairs={{4,8},{6,10},{8,4},{10,6},{5,9},{7,11},{9,5},{11,7},{20,24},{22,26... | collective-permute-start | bytes 786440 | tf_op jit(solution)/shard_map/ppermute | solution.py:46
  64.4 10.5 %collective-permute-start.17 = (bf16[64,2048]{1,0:T(8,128)(2,1)S(1)}, bf16[64,2048]{1,0:T(8,128)(2,1)S(1)}, u32[]{:S(2)}, u32[]{:S(2)}) collective-permute-start(bf16[64,2048]{1,0:T(8,128)(2,1)S(1)} %get-tuple-element.38), channel_id=1, source_target_pairs={{0,2},{2,0},{4,6},{6,4},{8,10},{10,8},{12,14},{14,12},{1,3},{3,1},... | collective-permute-start | bytes 786440 | tf_op jit(solution)/shard_map/ppermute | solution.py:46
  69.4 5.5 %collective-permute-start.20 = (bf16[64,2048]{1,0:T(8,128)(2,1)S(1)}, bf16[64,2048]{1,0:T(8,128)(2,1)S(1)}, u32[]{:S(2)}, u32[]{:S(2)}) collective-permute-start(bf16[64,2048]{1,0:T(8,128)(2,1)S(1)} %add_convert_fusion.2), channel_id=1, source_target_pairs={{4,8},{6,10},{8,4},{10,6},{5,9},{7,11},{9,5},{11,7},{20,24},{22,26... | collective-permute-start | bytes 786440 | tf_op jit(solution)/shard_map/ppermute | solution.py:46
  70.2 9.1 %collective-permute-start.23 = (bf16[64,2048]{1,0:T(8,128)(2,1)S(1)}, bf16[64,2048]{1,0:T(8,128)(2,1)S(1)}, u32[]{:S(2)}, u32[]{:S(2)}) collective-permute-start(bf16[64,2048]{1,0:T(8,128)(2,1)S(1)} %add_convert_fusion.1), channel_id=1, source_target_pairs={{0,4},{2,6},{4,0},{6,2},{8,12},{10,14},{12,8},{14,10},{1,5},{3,7},... | collective-permute-start | bytes 786440 | tf_op jit(solution)/shard_map/ppermute | solution.py:46
  (4 other events, 24.9 us)

commit v7 on v6

--- a/solution.py
+++ b/solution.py
@@ -137,6 +137,32 @@
     )(mask, pltpu.with_memory_space_constraint(weight, pltpu.HBM))
 
 
+def copy_kernel(mask, weight, out):
+    for k in range(out.shape[0] // BLOCK):
+        for j in range(out.shape[1] // BLOCK):
+            at = (slice(k * BLOCK, (k + 1) * BLOCK), slice(j * BLOCK, (j + 1) * BLOCK))
+
+            @pl.when(mask[k, j] != 0)
+            def _():
+                out[at] = weight[at]
+
+            @pl.when(mask[k, j] == 0)
+            def _():
+                out[at] = jnp.zeros((BLOCK, BLOCK), BF16)
+
+
+def prune_fetched(weight, mask):
+    return pl.pallas_call(
+        copy_kernel,
+        out_shape=pltpu.VMEM(weight.shape, BF16),
+        in_specs=[SCALAR, WHOLE],
+        out_specs=WHOLE,
+        compiler_params=pltpu.CompilerParams(vmem_limit_bytes=LIMIT),
+        cost_estimate=pl.CostEstimate(flops=0, bytes_accessed=1024, transcendentals=0),
+        name="prune_fetched",
+    )(mask, weight)
+
+
 def of_core(core, first, second):
     return jnp.where(core == 0, first, second)
 
@@ -162,7 +188,7 @@
 
     def weights(i, *others):
         weight, mask = stored[i]
-        return prune(after(weight, *others) if others else weight, mask)
+        return (prune_fetched if i == 2 else prune)(after(weight, *others) if others else weight, mask)
 
     first, last, (gate_w, up_w, down_w) = gather(tokens, weights)
     theirs, mine = halves(core, first)

time: 80.3 us -> 79.8 us (level)
  starting transfers between devices: 31.8 us -> 27.3 us
  waiting for transfers between devices: 16.1 us -> 18.7 us
  Pallas kernels: 13.3 us -> 14.7 us
    pallas_call x0 -> x1, Pallas kernels: none -> 5.61 us  [prune_fetched(): pl.pallas_call(copy_kernel, out_shape=pltpu.VMEM(weight.shape, BF16), in_...]
    ppermute x18, starting transfers between devices: 29.9 us -> 25.4 us  [move(): return lax.ppermute(value, 'tensor', perm)]
    pallas_call x3 -> x2, Pallas kernels: 13.3 us -> 9.1 us  [prune(): pl.pallas_call(prune_kernel, out_shape=pltpu.VMEM(weight.shape, BF16), in...]
    ppermute x18, waiting for transfers between devices: 15.9 us -> 18.4 us  [move(): return lax.ppermute(value, 'tensor', perm)]
  transfers between devices with their start and end apart: 24 -> 24, of which waited for: 8 -> 8; matrix products, arithmetic and copies ran while one was open for 21% -> 21% of each run, Pallas kernels for 17% -> 18%
where the time goes in v7:
time: 79.8 us; the launch traced here: 79.6 us
  starting transfers between devices  27.3 us (34%)
  waiting for transfers between devices  18.7 us (23%)
  matrix products  15.6 us (20%)
  Pallas kernels  14.7 us (18%)
  other arithmetic  1.91 us (2%)
  local copies, waits for them, and re-layouts  0.97 us (1%)
    ppermute x18, starting transfers between devices, move(): return lax.ppermute(value, 'tensor', perm)  25.4 us
    ppermute x18, waiting for transfers between devices, move(): return lax.ppermute(value, 'tensor', perm)  18.4 us
    dot_general x8, matrix products, dot(): return jnp.dot(a, b, preferred_element_type=F32)  15.6 us
    pallas_call x2, Pallas kernels, prune(): pl.pallas_call(prune_kernel, out_shape=pltpu.VMEM(weight.shape, BF16), in...  9.1 us
    pallas_call x1, Pallas kernels, prune_fetched(): pl.pallas_call(copy_kernel, out_shape=pltpu.VMEM(weight.shape, BF16), in_...  5.61 us
    ppermute x6, starting transfers between devices, swap(): return lax.ppermute(value, 'seq', SWAP)  1.84 us
  transfers between devices with their start and end apart: 24, of which 8 were waited for; matrix products, arithmetic and copies ran while one was open for 21% of the time, Pallas kernels for 18%

profile of v7, /device:TPU:0, one launch (start us, length us, event | category | flops | bytes accessed | tf_op | source)
XLA Modules:
  0.0 79.6 jit_solution(17611537837977638457)
XLA Ops:
  0.0 3.0 %collective-permute-start.1 = (bf16[64,2048]{1,0:T(8,128)(2,1)}, bf16[64,2048]{1,0:T(8,128)(2,1)S(1)}, u32[]{:S(2)}, u32[]{:S(2)}) collective-permute-start(bf16[64,2048]{1,0:T(8,128)(2,1)} %param.7), channel_id=1, source_target_pairs={{0,4},{2,6},{4,0},{6,2},{8,12},{10,14},{12,8},{14,10},{1,5},{3,7},... | collective-permute-start | bytes 786440 | tf_op jit(solution)/shard_map/ppermute | solution.py:46
  3.0 1.5 %collective-permute-start = (bf16[64,2048]{1,0:T(8,128)(2,1)}, bf16[64,2048]{1,0:T(8,128)(2,1)S(1)}, u32[]{:S(2)}, u32[]{:S(2)}) collective-permute-start(bf16[64,2048]{1,0:T(8,128)(2,1)} %param.7), channel_id=1, source_target_pairs={{0,2},{2,0},{4,6},{6,4},{8,10},{10,8},{12,14},{14,12},{1,3},{3,1},... | collective-permute-start | bytes 786440 | tf_op jit(solution)/shard_map/ppermute | solution.py:46
  5.9 4.4 %prune.2 = bf16[2048,2048]{1,0:T(8,128)(2,1)S(1)} custom-call(s32[16,16]{1,0:T(8,128)S(1)} %copy-done, bf16[2048,2048]{1,0:T(8,128)(2,1)} %weight.1), custom_call_target="tpu_custom_call" | custom-call | bytes 1024 | tf_op jit(solution)/shard_map/prune/pallas_call | solution.py:128
  11.0 1.5 %collective-permute-start.2 = (bf16[64,2048]{1,0:T(8,128)(2,1)S(1)}, bf16[64,2048]{1,0:T(8,128)(2,1)S(1)}, u32[]{:S(2)}, u32[]{:S(2)}) collective-permute-start(bf16[64,2048]{1,0:T(8,128)(2,1)S(1)} %collective-permute-done.1), channel_id=1, source_target_pairs={{0,2},{2,0},{4,6},{6,4},{8,10},{10,8},{12,14},{14,12},{1,3},{3,1},... | collective-permute-start | bytes 786440 | tf_op jit(solution)/shard_map/ppermute | solution.py:46
  13.2 4.4 %collective-permute-start.4 = (bf16[64,2048]{1,0:T(8,128)(2,1)S(1)}, bf16[64,2048]{1,0:T(8,128)(2,1)S(1)}, u32[]{:S(2)}, u32[]{:S(2)}) collective-permute-start(bf16[64,2048]{1,0:T(8,128)(2,1)S(1)} %collective-permute-done.3), channel_id=1, source_target_pairs={{0,4},{2,6},{4,0},{6,2},{8,12},{10,14},{12,8},{14,10},{1,5},{3,7},... | collective-permute-start | bytes 786440 | tf_op jit(solution)/shard_map/ppermute | solution.py:46
  17.7 4.7 %prune.3 = bf16[2048,2048]{1,0:T(8,128)(2,1)S(1)} custom-call(s32[16,16]{1,0:T(8,128)S(1)} %copy-done.1, bf16[2048,2048]{1,0:T(8,128)(2,1)} %weight.2), custom_call_target="tpu_custom_call" | custom-call | bytes 1024 | tf_op jit(solution)/shard_map/prune/pallas_call | solution.py:128
  22.5 1.7 %collective-permute-start.6 = (bf16[64,2048]{1,0:T(8,128)(2,1)S(1)}, bf16[64,2048]{1,0:T(8,128)(2,1)S(1)}, u32[]{:S(2)}, u32[]{:S(2)}) collective-permute-start(bf16[64,2048]{1,0:T(8,128)(2,1)S(1)} %collective-permute-done.5), channel_id=1, source_target_pairs={{0,4},{2,6},{4,0},{6,2},{8,12},{10,14},{12,8},{14,10},{1,5},{3,7},... | collective-permute-start | bytes 786440 | tf_op jit(solution)/shard_map/ppermute | solution.py:46
  24.2 1.6 %collective-permute-start.7 = (bf16[64,2048]{1,0:T(8,128)(2,1)S(1)}, bf16[64,2048]{1,0:T(8,128)(2,1)S(1)}, u32[]{:S(2)}, u32[]{:S(2)}) collective-permute-start(bf16[64,2048]{1,0:T(8,128)(2,1)S(1)} %broadcast_select_fusion.9), channel_id=1, source_target_pairs={{0,2},{2,0},{4,6},{6,4},{8,10},{10,8},{12,14},{14,12},{1,3},{3,1},... | collective-permute-start | bytes 786440 | tf_op jit(solution)/shard_map/ppermute | solution.py:46
  25.8 5.6 %prune_fetched.1 = bf16[2048,2048]{1,0:T(8,128)(2,1)S(1)} custom-call(s32[16,16]{1,0:T(8,128)S(1)} %copy-done.2, bf16[2048,2048]{1,0:T(8,128)(2,1)S(1)} %bitcast.11), custom_call_target="tpu_custom_call" | custom-call | bytes 1024 | tf_op jit(solution)/shard_map/prune_fetched/pallas_call | solution.py:155
  32.4 1.9 %fusion.15 = f32[192,2048]{1,0:T(8,128)S(1)} fusion(bf16[2048,2048]{1,0:T(8,128)(2,1)S(1)} %prune.2, bf16[192,2048]{1,0:T(8,128)(2,1)S(1)} %constant_dynamic-update-slice_fusion, pred[]{:T(512)S(6)} %eq.6, bf16[64,2048]{1,0:T(8,128)(2,1)S(1)} %collective-permute-done.7, bf16[64,2048]{1,0:T(8,128)(2,1)S(1)} %broadcast_select_fusion.9, ...), kind=kOutput, calls=%fused_computation.43 | convolution fusion | flops 1613365248 | bytes 11534337 | tf_op jit(solution)/shard_map/dot_general | solution.py:22
  34.4 1.9 %fusion.14 = f32[192,2048]{1,0:T(8,128)S(1)} fusion(bf16[2048,2048]{1,0:T(8,128)(2,1)S(1)} %prune.3, bf16[192,2048]{1,0:T(8,128)(2,1)S(1)} %constant_dynamic-update-slice_fusion, pred[]{:T(512)S(6)} %eq.6, bf16[64,2048]{1,0:T(8,128)(2,1)S(1)} %collective-permute-done.7, bf16[64,2048]{1,0:T(8,128)(2,1)S(1)} %broadcast_select_fusion.9, ...), kind=kOutput, calls=%fused_computation.42 | convolution fusion | flops 1613365248 | bytes 11534337 | tf_op jit(solution)/shard_map/dot_general | solution.py:22
  38.0 1.3 %fusion.8 = f32[128,2048]{1,0:T(8,128)S(1)} fusion(bf16[2048,2048]{1,0:T(8,128)(2,1)S(1)} %prune.3, bf16[64,2048]{1,0:T(8,128)(2,1)S(1)} %get-tuple-element.52, bf16[64,2048]{1,0:T(8,128)(2,1)S(1)} %get-tuple-element.51), kind=kOutput, calls=%fused_computation.27 | convolution fusion | flops 1074790400 | bytes 9961472 | tf_op jit(solution)/shard_map/dot_general | solution.py:22
  39.3 1.3 %fusion.9 = f32[128,2048]{1,0:T(8,128)S(1)} fusion(bf16[2048,2048]{1,0:T(8,128)(2,1)S(1)} %prune.2, bf16[64,2048]{1,0:T(8,128)(2,1)S(1)} %get-tuple-element.52, bf16[64,2048]{1,0:T(8,128)(2,1)S(1)} %get-tuple-element.51), kind=kOutput, calls=%fused_computation.28 | convolution fusion | flops 1074790400 | bytes 9961472 | tf_op jit(solution)/shard_map/dot_general | solution.py:22
  41.3 1.9 %convolution_add_fusion.1 = f32[192,2048]{1,0:T(8,128)S(1)} fusion(f32[192,2048]{1,0:T(8,128)S(1)} %collective-permute-done.9, bf16[192,2048]{1,0:T(8,128)(2,1)S(1)} %broadcast_select_fusion.3, bf16[2048,2048]{1,0:T(8,128)(2,1)S(1)} %prune.2), kind=kOutput, calls=%fused_computation.2 | convolution fusion | flops 1611005952 | bytes 12320768 | tf_op jit(solution)/shard_map/dot_general | solution.py:22
  43.8 2.2 %multiply_convert_fusion = bf16[192,2048]{1,0:T(8,128)(2,1)S(1)} fusion(f32[192,2048]{1,0:T(8,128)S(1)} %convolution_add_fusion.1, f32[192,2048]{1,0:T(8,128)S(1)} %collective-permute-done.12, bf16[192,2048]{1,0:T(8,128)(2,1)S(1)} %broadcast_select_fusion.3, bf16[2048,2048]{1,0:T(8,128)(2,1)S(1)} %prune.3), kind=kOutput, calls=%fused_computation.7 | convolution fusion | flops 1613365248 | bytes 13107200 | tf_op jit(solution)/shard_map/dot_general | solution.py:22
  46.6 1.3 %convolution_convert_fusion.1 = bf16[128,2048]{1,0:T(8,128)(2,1)S(1)} fusion(bf16[2048,2048]{1,0:T(8,128)(2,1)S(1)} %prune_fetched.1, bf16[64,2048]{1,0:T(8,128)(2,1)S(1)} %get-tuple-element.50, bf16[64,2048]{1,0:T(8,128)(2,1)S(1)} %get-tuple-element.49), kind=kOutput, calls=%fused_computation.3 | convolution fusion | flops 1075052544 | bytes 9437184 | tf_op jit(solution)/shard_map/dot_general | solution.py:22
  49.0 3.7 %convolution_convert_fusion = bf16[384,2048]{1,0:T(8,128)(2,1)S(1)} fusion(bf16[2048,2048]{1,0:T(8,128)(2,1)S(1)} %prune_fetched.1, bf16[192,2048]{1,0:T(8,128)(2,1)S(1)} %get-tuple-element.46, bf16[192,2048]{1,0:T(8,128)(2,1)S(1)} %get-tuple-element.45), kind=kOutput, calls=%fused_computation | convolution fusion | flops 3225157632 | bytes 11534336 | tf_op jit(solution)/shard_map/dot_general | solution.py:22
  52.8 1.2 %collective-permute-start.18 = (bf16[64,2048]{1,0:T(8,128)(2,1)S(1)}, bf16[64,2048]{1,0:T(8,128)(2,1)S(1)}, u32[]{:S(2)}, u32[]{:S(2)}) collective-permute-start(bf16[64,2048]{1,0:T(8,128)(2,1)S(1)} %get-tuple-element.43), channel_id=1, source_target_pairs={{0,2},{2,0},{4,6},{6,4},{8,10},{10,8},{12,14},{14,12},{1,3},{3,1},... | collective-permute-start | bytes 786440 | tf_op jit(solution)/shard_map/ppermute | solution.py:46
  54.0 3.1 %collective-permute-done.15 = bf16[64,2048]{1,0:T(8,128)(2,1)S(1)} collective-permute-done((bf16[64,2048]{1,0:T(8,128)(2,1)S(1)}, bf16[64,2048]{1,0:T(8,128)(2,1)S(1)}, u32[]{:S(2)}, u32[]{:S(2)}) %collective-permute-start.15) | collective-permute-done | bytes 262176 | tf_op jit(solution)/shard_map/ppermute | solution.py:46
  58.2 4.6 %collective-permute-done.18 = bf16[64,2048]{1,0:T(8,128)(2,1)S(1)} collective-permute-done((bf16[64,2048]{1,0:T(8,128)(2,1)S(1)}, bf16[64,2048]{1,0:T(8,128)(2,1)S(1)}, u32[]{:S(2)}, u32[]{:S(2)}) %collective-permute-start.18) | collective-permute-done | bytes 262176 | tf_op jit(solution)/shard_map/ppermute | solution.py:46
  62.9 1.1 %collective-permute-done.16 = bf16[64,2048]{1,0:T(8,128)(2,1)S(1)} collective-permute-done((bf16[64,2048]{1,0:T(8,128)(2,1)S(1)}, bf16[64,2048]{1,0:T(8,128)(2,1)S(1)}, u32[]{:S(2)}, u32[]{:S(2)}) %collective-permute-start.16) | collective-permute-done | bytes 262176 | tf_op jit(solution)/shard_map/ppermute | solution.py:46
  65.7 3.9 %collective-permute-done.19 = bf16[64,2048]{1,0:T(8,128)(2,1)S(1)} collective-permute-done((bf16[64,2048]{1,0:T(8,128)(2,1)S(1)}, bf16[64,2048]{1,0:T(8,128)(2,1)S(1)}, u32[]{:S(2)}, u32[]{:S(2)}) %collective-permute-start.19) | collective-permute-done | bytes 262176 | tf_op jit(solution)/shard_map/ppermute | solution.py:46
  70.5 3.9 %collective-permute-start.23 = (bf16[64,2048]{1,0:T(8,128)(2,1)S(1)}, bf16[64,2048]{1,0:T(8,128)(2,1)S(1)}, u32[]{:S(2)}, u32[]{:S(2)}) collective-permute-start(bf16[64,2048]{1,0:T(8,128)(2,1)S(1)} %add_convert_fusion.1), channel_id=1, source_target_pairs={{0,4},{2,6},{4,0},{6,2},{8,12},{10,14},{12,8},{14,10},{1,5},{3,7},... | collective-permute-start | bytes 786440 | tf_op jit(solution)/shard_map/ppermute | solution.py:46
  74.4 4.3 %collective-permute-done.23 = bf16[64,2048]{1,0:T(8,128)(2,1)S(1)} collective-permute-done((bf16[64,2048]{1,0:T(8,128)(2,1)S(1)}, bf16[64,2048]{1,0:T(8,128)(2,1)S(1)}, u32[]{:S(2)}, u32[]{:S(2)}) %collective-permute-start.23) | collective-permute-done | bytes 262176 | tf_op jit(solution)/shard_map/ppermute | solution.py:46
  (68 shorter events, 13.0 us)
Async XLA Ops:
  0.0 10.4 %collective-permute-start.1 = (bf16[64,2048]{1,0:T(8,128)(2,1)}, bf16[64,2048]{1,0:T(8,128)(2,1)S(1)}, u32[]{:S(2)}, u32[]{:S(2)}) collective-permute-start(bf16[64,2048]{1,0:T(8,128)(2,1)} %param.7), channel_id=1, source_target_pairs={{0,4},{2,6},{4,0},{6,2},{8,12},{10,14},{12,8},{14,10},{1,5},{3,7},... | collective-permute-start | bytes 786440 | tf_op jit(solution)/shard_map/ppermute | solution.py:46
  3.0 8.0 %collective-permute-start = (bf16[64,2048]{1,0:T(8,128)(2,1)}, bf16[64,2048]{1,0:T(8,128)(2,1)S(1)}, u32[]{:S(2)}, u32[]{:S(2)}) collective-permute-start(bf16[64,2048]{1,0:T(8,128)(2,1)} %param.7), channel_id=1, source_target_pairs={{0,2},{2,0},{4,6},{6,4},{8,10},{10,8},{12,14},{14,12},{1,3},{3,1},... | collective-permute-start | bytes 786440 | tf_op jit(solution)/shard_map/ppermute | solution.py:46
  4.5 8.7 %collective-permute-start.3 = (bf16[64,2048]{1,0:T(8,128)(2,1)}, bf16[64,2048]{1,0:T(8,128)(2,1)S(1)}, u32[]{:S(2)}, u32[]{:S(2)}) collective-permute-start(bf16[64,2048]{1,0:T(8,128)(2,1)} %param.7), channel_id=1, source_target_pairs={{4,8},{6,10},{8,4},{10,6},{5,9},{7,11},{9,5},{11,7},{20,24},{22,26... | collective-permute-start | bytes 786440 | tf_op jit(solution)/shard_map/ppermute | solution.py:46
  11.0 13.2 %collective-permute-start.2 = (bf16[64,2048]{1,0:T(8,128)(2,1)S(1)}, bf16[64,2048]{1,0:T(8,128)(2,1)S(1)}, u32[]{:S(2)}, u32[]{:S(2)}) collective-permute-start(bf16[64,2048]{1,0:T(8,128)(2,1)S(1)} %collective-permute-done.1), channel_id=1, source_target_pairs={{0,2},{2,0},{4,6},{6,4},{8,10},{10,8},{12,14},{14,12},{1,3},{3,1},... | collective-permute-start | bytes 786440 | tf_op jit(solution)/shard_map/ppermute | solution.py:46
  12.5 9.9 %collective-permute-start.5 = (bf16[64,2048]{1,0:T(8,128)(2,1)S(1)}, bf16[64,2048]{1,0:T(8,128)(2,1)S(1)}, u32[]{:S(2)}, u32[]{:S(2)}) collective-permute-start(bf16[64,2048]{1,0:T(8,128)(2,1)S(1)} %collective-permute-done.1), channel_id=1, source_target_pairs={{4,8},{6,10},{8,4},{10,6},{5,9},{7,11},{9,5},{11,7},{20,24},{22,26... | collective-permute-start | bytes 786440 | tf_op jit(solution)/shard_map/ppermute | solution.py:46
  13.2 11.0 %collective-permute-start.4 = (bf16[64,2048]{1,0:T(8,128)(2,1)S(1)}, bf16[64,2048]{1,0:T(8,128)(2,1)S(1)}, u32[]{:S(2)}, u32[]{:S(2)}) collective-permute-start(bf16[64,2048]{1,0:T(8,128)(2,1)S(1)} %collective-permute-done.3), channel_id=1, source_target_pairs={{0,4},{2,6},{4,0},{6,2},{8,12},{10,14},{12,8},{14,10},{1,5},{3,7},... | collective-permute-start | bytes 786440 | tf_op jit(solution)/shard_map/ppermute | solution.py:46
  22.5 9.0 %collective-permute-start.6 = (bf16[64,2048]{1,0:T(8,128)(2,1)S(1)}, bf16[64,2048]{1,0:T(8,128)(2,1)S(1)}, u32[]{:S(2)}, u32[]{:S(2)}) collective-permute-start(bf16[64,2048]{1,0:T(8,128)(2,1)S(1)} %collective-permute-done.5), channel_id=1, source_target_pairs={{0,4},{2,6},{4,0},{6,2},{8,12},{10,14},{12,8},{14,10},{1,5},{3,7},... | collective-permute-start | bytes 786440 | tf_op jit(solution)/shard_map/ppermute | solution.py:46
  24.2 7.3 %collective-permute-start.7 = (bf16[64,2048]{1,0:T(8,128)(2,1)S(1)}, bf16[64,2048]{1,0:T(8,128)(2,1)S(1)}, u32[]{:S(2)}, u32[]{:S(2)}) collective-permute-start(bf16[64,2048]{1,0:T(8,128)(2,1)S(1)} %broadcast_select_fusion.9), channel_id=1, source_target_pairs={{0,2},{2,0},{4,6},{6,4},{8,10},{10,8},{12,14},{14,12},{1,3},{3,1},... | collective-permute-start | bytes 786440 | tf_op jit(solution)/shard_map/ppermute | solution.py:46
  31.5 6.4 %collective-permute-start.8 = (bf16[64,2048]{1,0:T(8,128)(2,1)S(1)}, bf16[64,2048]{1,0:T(8,128)(2,1)S(1)}, u32[]{:S(2)}, u32[]{:S(2)}) collective-permute-start(bf16[64,2048]{1,0:T(8,128)(2,1)S(1)} %broadcast_select_fusion.8), channel_id=1, source_target_pairs={{0,2},{2,0},{4,6},{6,4},{8,10},{10,8},{12,14},{14,12},{1,3},{3,1},... | collective-permute-start | bytes 786440 | tf_op jit(solution)/shard_map/ppermute | solution.py:46
  34.4 6.9 %collective-permute-start.9 = (f32[192,2048]{1,0:T(8,128)S(1)}, f32[192,2048]{1,0:T(8,128)S(1)}, u32[]{:S(2)}, u32[]{:S(2)}) collective-permute-start(f32[192,2048]{1,0:T(8,128)S(1)} %fusion.15), channel_id=1, source_target_pairs={{0,1},{1,0},{2,3},{3,2},{4,5},{5,4},{6,7},{7,6},{8,9},{9,8},{10,11... | collective-permute-start | bytes 4718600 | tf_op jit(solution)/shard_map/ppermute | solution.py:103
  36.3 7.5 %collective-permute-start.12 = (f32[192,2048]{1,0:T(8,128)S(1)}, f32[192,2048]{1,0:T(8,128)S(1)}, u32[]{:S(2)}, u32[]{:S(2)}) collective-permute-start(f32[192,2048]{1,0:T(8,128)S(1)} %fusion.14), channel_id=1, source_target_pairs={{0,1},{1,0},{2,3},{3,2},{4,5},{5,4},{6,7},{7,6},{8,9},{9,8},{10,11... | collective-permute-start | bytes 4718600 | tf_op jit(solution)/shard_map/ppermute | solution.py:103
  40.7 2.5 %collective-permute-start.11 = (f32[64,2048]{1,0:T(8,128)S(1)}, f32[64,2048]{1,0:T(8,128)S(1)}, u32[]{:S(2)}, u32[]{:S(2)}) collective-permute-start(f32[64,2048]{1,0:T(8,128)S(1)} %slice.19), channel_id=1, source_target_pairs={{0,1},{1,0},{2,3},{3,2},{4,5},{5,4},{6,7},{7,6},{8,9},{9,8},{10,11... | collective-permute-start | bytes 1572872 | tf_op jit(solution)/shard_map/ppermute | solution.py:103
  40.8 2.6 %collective-permute-start.10 = (f32[64,2048]{1,0:T(8,128)S(1)}, f32[64,2048]{1,0:T(8,128)S(1)}, u32[]{:S(2)}, u32[]{:S(2)}) collective-permute-start(f32[64,2048]{1,0:T(8,128)S(1)} %slice.17), channel_id=1, source_target_pairs={{0,1},{1,0},{2,3},{3,2},{4,5},{5,4},{6,7},{7,6},{8,9},{9,8},{10,11... | collective-permute-start | bytes 1572872 | tf_op jit(solution)/shard_map/ppermute | solution.py:103
  43.6 2.9 %collective-permute-start.14 = (bf16[64,2048]{1,0:T(8,128)(2,1)S(1)}, bf16[64,2048]{1,0:T(8,128)(2,1)S(1)}, u32[]{:S(2)}, u32[]{:S(2)}) collective-permute-start(bf16[64,2048]{1,0:T(8,128)(2,1)S(1)} %fusion.4), channel_id=1, source_target_pairs={{0,1},{1,0},{2,3},{3,2},{4,5},{5,4},{6,7},{7,6},{8,9},{9,8},{10,11... | collective-permute-start | bytes 786440 | tf_op jit(solution)/shard_map/ppermute | solution.py:103
  46.1 2.8 %collective-permute-start.13 = (bf16[192,2048]{1,0:T(8,128)(2,1)S(1)}, bf16[192,2048]{1,0:T(8,128)(2,1)S(1)}, u32[]{:S(2)}, u32[]{:S(2)}) collective-permute-start(bf16[192,2048]{1,0:T(8,128)(2,1)S(1)} %multiply_convert_fusion), channel_id=1, source_target_pairs={{0,1},{1,0},{2,3},{3,2},{4,5},{5,4},{6,7},{7,6},{8,9},{9,8},{10,11... | collective-permute-start | bytes 2359304 | tf_op jit(solution)/shard_map/ppermute | solution.py:103
  47.9 9.2 %collective-permute-start.15 = (bf16[64,2048]{1,0:T(8,128)(2,1)S(1)}, bf16[64,2048]{1,0:T(8,128)(2,1)S(1)}, u32[]{:S(2)}, u32[]{:S(2)}) collective-permute-start(bf16[64,2048]{1,0:T(8,128)(2,1)S(1)} %get-tuple-element.48), channel_id=1, source_target_pairs={{0,2},{2,0},{4,6},{6,4},{8,10},{10,8},{12,14},{14,12},{1,3},{3,1},... | collective-permute-start | bytes 786440 | tf_op jit(solution)/shard_map/ppermute | solution.py:46
  52.8 10.0 %collective-permute-start.18 = (bf16[64,2048]{1,0:T(8,128)(2,1)S(1)}, bf16[64,2048]{1,0:T(8,128)(2,1)S(1)}, u32[]{:S(2)}, u32[]{:S(2)}) collective-permute-start(bf16[64,2048]{1,0:T(8,128)(2,1)S(1)} %get-tuple-element.43), channel_id=1, source_target_pairs={{0,2},{2,0},{4,6},{6,4},{8,10},{10,8},{12,14},{14,12},{1,3},{3,1},... | collective-permute-start | bytes 786440 | tf_op jit(solution)/shard_map/ppermute | solution.py:46
  57.2 6.8 %collective-permute-start.16 = (bf16[64,2048]{1,0:T(8,128)(2,1)S(1)}, bf16[64,2048]{1,0:T(8,128)(2,1)S(1)}, u32[]{:S(2)}, u32[]{:S(2)}) collective-permute-start(bf16[64,2048]{1,0:T(8,128)(2,1)S(1)} %add_convert_fusion.5), channel_id=1, source_target_pairs={{0,4},{2,6},{4,0},{6,2},{8,12},{10,14},{12,8},{14,10},{1,5},{3,7},... | collective-permute-start | bytes 786440 | tf_op jit(solution)/shard_map/ppermute | solution.py:46
  57.3 13.1 %collective-permute-start.21 = (bf16[64,2048]{1,0:T(8,128)(2,1)S(1)}, bf16[64,2048]{1,0:T(8,128)(2,1)S(1)}, u32[]{:S(2)}, u32[]{:S(2)}) collective-permute-start(bf16[64,2048]{1,0:T(8,128)(2,1)S(1)} %get-tuple-element.40), channel_id=1, source_target_pairs={{0,2},{2,0},{4,6},{6,4},{8,10},{10,8},{12,14},{14,12},{1,3},{3,1},... | collective-permute-start | bytes 786440 | tf_op jit(solution)/shard_map/ppermute | solution.py:46
  62.8 6.8 %collective-permute-start.19 = (bf16[64,2048]{1,0:T(8,128)(2,1)S(1)}, bf16[64,2048]{1,0:T(8,128)(2,1)S(1)}, u32[]{:S(2)}, u32[]{:S(2)}) collective-permute-start(bf16[64,2048]{1,0:T(8,128)(2,1)S(1)} %add_convert_fusion.3), channel_id=1, source_target_pairs={{0,4},{2,6},{4,0},{6,2},{8,12},{10,14},{12,8},{14,10},{1,5},{3,7},... | collective-permute-start | bytes 786440 | tf_op jit(solution)/shard_map/ppermute | solution.py:46
  64.1 6.3 %collective-permute-start.22 = (bf16[64,2048]{1,0:T(8,128)(2,1)S(1)}, bf16[64,2048]{1,0:T(8,128)(2,1)S(1)}, u32[]{:S(2)}, u32[]{:S(2)}) collective-permute-start(bf16[64,2048]{1,0:T(8,128)(2,1)S(1)} %add_convert_fusion.4), channel_id=1, source_target_pairs={{4,8},{6,10},{8,4},{10,6},{5,9},{7,11},{9,5},{11,7},{20,24},{22,26... | collective-permute-start | bytes 786440 | tf_op jit(solution)/shard_map/ppermute | solution.py:46
  64.8 9.6 %collective-permute-start.17 = (bf16[64,2048]{1,0:T(8,128)(2,1)S(1)}, bf16[64,2048]{1,0:T(8,128)(2,1)S(1)}, u32[]{:S(2)}, u32[]{:S(2)}) collective-permute-start(bf16[64,2048]{1,0:T(8,128)(2,1)S(1)} %get-tuple-element.38), channel_id=1, source_target_pairs={{0,2},{2,0},{4,6},{6,4},{8,10},{10,8},{12,14},{14,12},{1,3},{3,1},... | collective-permute-start | bytes 786440 | tf_op jit(solution)/shard_map/ppermute | solution.py:46
  69.7 4.7 %collective-permute-start.20 = (bf16[64,2048]{1,0:T(8,128)(2,1)S(1)}, bf16[64,2048]{1,0:T(8,128)(2,1)S(1)}, u32[]{:S(2)}, u32[]{:S(2)}) collective-permute-start(bf16[64,2048]{1,0:T(8,128)(2,1)S(1)} %add_convert_fusion.2), channel_id=1, source_target_pairs={{4,8},{6,10},{8,4},{10,6},{5,9},{7,11},{9,5},{11,7},{20,24},{22,26... | collective-permute-start | bytes 786440 | tf_op jit(solution)/shard_map/ppermute | solution.py:46
  70.5 8.2 %collective-permute-start.23 = (bf16[64,2048]{1,0:T(8,128)(2,1)S(1)}, bf16[64,2048]{1,0:T(8,128)(2,1)S(1)}, u32[]{:S(2)}, u32[]{:S(2)}) collective-permute-start(bf16[64,2048]{1,0:T(8,128)(2,1)S(1)} %add_convert_fusion.1), channel_id=1, source_target_pairs={{0,4},{2,6},{4,0},{6,2},{8,12},{10,14},{12,8},{14,10},{1,5},{3,7},... | collective-permute-start | bytes 786440 | tf_op jit(solution)/shard_map/ppermute | solution.py:46
  (6 other events, 41.2 us)

commit v8 on v7

--- a/solution.py
+++ b/solution.py
@@ -61,11 +61,11 @@
     own_y = move(own, ACROSS)
     gate_w = weights(0)
     far_mid = move(pair, MIDDLE)
-    near_out = move(near_mid, PAIR)
+    near_out = move(near_mid, OUTWARD)
     pair_y = move(after(pair, own_y), ACROSS)
     up_w = weights(1, own_y, near_mid, pair)
     near = jnp.where(inner(), near_mid, near_out)
-    far_out = move(far_mid, PAIR)
+    far_out = move(far_mid, OUTWARD)
     near_y = move(after(near, pair_y), ACROSS)
     down_w = weights(2, near, pair_y)
     far = jnp.where(inner(), far_mid, far_out)

time: 79.8 us -> 80 us (level)
  no operation moved by 1% of the time
where the time goes in v8:
time: 80 us; the launch traced here: 79.7 us
  starting transfers between devices  27.1 us (34%)
  waiting for transfers between devices  19.2 us (24%)
  matrix products  15.6 us (20%)
  Pallas kernels  14.5 us (18%)
  other arithmetic  1.91 us (2%)
  local copies, waits for them, and re-layouts  0.98 us (1%)
    ppermute x18, starting transfers between devices, move(): return lax.ppermute(value, 'tensor', perm)  25.3 us
    ppermute x18, waiting for transfers between devices, move(): return lax.ppermute(value, 'tensor', perm)  18.9 us
    dot_general x8, matrix products, dot(): return jnp.dot(a, b, preferred_element_type=F32)  15.6 us
    pallas_call x2, Pallas kernels, prune(): pl.pallas_call(prune_kernel, out_shape=pltpu.VMEM(weight.shape, BF16), in...  9.12 us
    pallas_call x1, Pallas kernels, prune_fetched(): pl.pallas_call(copy_kernel, out_shape=pltpu.VMEM(weight.shape, BF16), in_...  5.41 us
    ppermute x6, starting transfers between devices, swap(): return lax.ppermute(value, 'seq', SWAP)  1.83 us
  transfers between devices with their start and end apart: 24, of which 8 were waited for; matrix products, arithmetic and copies ran while one was open for 21% of the time, Pallas kernels for 18%

profile of v8, /device:TPU:0, one launch (start us, length us, event | category | flops | bytes accessed | tf_op | source)
XLA Modules:
  0.0 79.7 jit_solution(9841524154931983941)
XLA Ops:
  0.0 3.0 %collective-permute-start.1 = (bf16[64,2048]{1,0:T(8,128)(2,1)}, bf16[64,2048]{1,0:T(8,128)(2,1)S(1)}, u32[]{:S(2)}, u32[]{:S(2)}) collective-permute-start(bf16[64,2048]{1,0:T(8,128)(2,1)} %param.7), channel_id=1, source_target_pairs={{0,4},{2,6},{4,0},{6,2},{8,12},{10,14},{12,8},{14,10},{1,5},{3,7},... | collective-permute-start | bytes 786440 | tf_op jit(solution)/shard_map/ppermute | solution.py:46
  3.0 1.5 %collective-permute-start = (bf16[64,2048]{1,0:T(8,128)(2,1)}, bf16[64,2048]{1,0:T(8,128)(2,1)S(1)}, u32[]{:S(2)}, u32[]{:S(2)}) collective-permute-start(bf16[64,2048]{1,0:T(8,128)(2,1)} %param.7), channel_id=1, source_target_pairs={{0,2},{2,0},{4,6},{6,4},{8,10},{10,8},{12,14},{14,12},{1,3},{3,1},... | collective-permute-start | bytes 786440 | tf_op jit(solution)/shard_map/ppermute | solution.py:46
  5.9 4.4 %prune.2 = bf16[2048,2048]{1,0:T(8,128)(2,1)S(1)} custom-call(s32[16,16]{1,0:T(8,128)S(1)} %copy-done, bf16[2048,2048]{1,0:T(8,128)(2,1)} %weight.1), custom_call_target="tpu_custom_call" | custom-call | bytes 1024 | tf_op jit(solution)/shard_map/prune/pallas_call | solution.py:128
  11.0 1.5 %collective-permute-start.2 = (bf16[64,2048]{1,0:T(8,128)(2,1)S(1)}, bf16[64,2048]{1,0:T(8,128)(2,1)S(1)}, u32[]{:S(2)}, u32[]{:S(2)}) collective-permute-start(bf16[64,2048]{1,0:T(8,128)(2,1)S(1)} %collective-permute-done.1), channel_id=1, source_target_pairs={{0,2},{2,0},{4,6},{6,4},{8,10},{10,8},{12,14},{14,12},{1,3},{3,1},... | collective-permute-start | bytes 786440 | tf_op jit(solution)/shard_map/ppermute | solution.py:46
  14.6 4.7 %prune.3 = bf16[2048,2048]{1,0:T(8,128)(2,1)S(1)} custom-call(s32[16,16]{1,0:T(8,128)S(1)} %copy-done.1, bf16[2048,2048]{1,0:T(8,128)(2,1)} %weight.2), custom_call_target="tpu_custom_call" | custom-call | bytes 1024 | tf_op jit(solution)/shard_map/prune/pallas_call | solution.py:128
  19.4 1.4 %collective-permute-start.6 = (bf16[64,2048]{1,0:T(8,128)(2,1)S(1)}, bf16[64,2048]{1,0:T(8,128)(2,1)S(1)}, u32[]{:S(2)}, u32[]{:S(2)}) collective-permute-start(bf16[64,2048]{1,0:T(8,128)(2,1)S(1)} %collective-permute-done.5), channel_id=1, source_target_pairs={{4,0},{6,2},{8,12},{10,14},{5,1},{7,3},{9,13},{11,15},{20,16},{22,... | collective-permute-start | bytes 786440 | tf_op jit(solution)/shard_map/ppermute | solution.py:46
  20.8 2.9 %collective-permute-done.4 = bf16[64,2048]{1,0:T(8,128)(2,1)S(1)} collective-permute-done((bf16[64,2048]{1,0:T(8,128)(2,1)S(1)}, bf16[64,2048]{1,0:T(8,128)(2,1)S(1)}, u32[]{:S(2)}, u32[]{:S(2)}) %collective-permute-start.4) | collective-permute-done | bytes 262176 | tf_op jit(solution)/shard_map/ppermute | solution.py:46
  23.8 1.6 %collective-permute-start.7 = (bf16[64,2048]{1,0:T(8,128)(2,1)S(1)}, bf16[64,2048]{1,0:T(8,128)(2,1)S(1)}, u32[]{:S(2)}, u32[]{:S(2)}) collective-permute-start(bf16[64,2048]{1,0:T(8,128)(2,1)S(1)} %broadcast_select_fusion.9), channel_id=1, source_target_pairs={{0,2},{2,0},{4,6},{6,4},{8,10},{10,8},{12,14},{14,12},{1,3},{3,1},... | collective-permute-start | bytes 786440 | tf_op jit(solution)/shard_map/ppermute | solution.py:46
  25.4 5.4 %prune_fetched.1 = bf16[2048,2048]{1,0:T(8,128)(2,1)S(1)} custom-call(s32[16,16]{1,0:T(8,128)S(1)} %copy-done.2, bf16[2048,2048]{1,0:T(8,128)(2,1)S(1)} %bitcast.11), custom_call_target="tpu_custom_call" | custom-call | bytes 1024 | tf_op jit(solution)/shard_map/prune_fetched/pallas_call | solution.py:155
  31.7 1.9 %fusion.15 = f32[192,2048]{1,0:T(8,128)S(1)} fusion(bf16[2048,2048]{1,0:T(8,128)(2,1)S(1)} %prune.2, bf16[192,2048]{1,0:T(8,128)(2,1)S(1)} %constant_dynamic-update-slice_fusion, pred[]{:T(512)S(6)} %eq.6, bf16[64,2048]{1,0:T(8,128)(2,1)S(1)} %collective-permute-done.7, bf16[64,2048]{1,0:T(8,128)(2,1)S(1)} %broadcast_select_fusion.9, ...), kind=kOutput, calls=%fused_computation.43 | convolution fusion | flops 1613365248 | bytes 11534337 | tf_op jit(solution)/shard_map/dot_general | solution.py:22
  33.7 1.9 %fusion.14 = f32[192,2048]{1,0:T(8,128)S(1)} fusion(bf16[2048,2048]{1,0:T(8,128)(2,1)S(1)} %prune.3, bf16[192,2048]{1,0:T(8,128)(2,1)S(1)} %constant_dynamic-update-slice_fusion, pred[]{:T(512)S(6)} %eq.6, bf16[64,2048]{1,0:T(8,128)(2,1)S(1)} %collective-permute-done.7, bf16[64,2048]{1,0:T(8,128)(2,1)S(1)} %broadcast_select_fusion.9, ...), kind=kOutput, calls=%fused_computation.42 | convolution fusion | flops 1613365248 | bytes 11534337 | tf_op jit(solution)/shard_map/dot_general | solution.py:22
  37.3 1.3 %fusion.8 = f32[128,2048]{1,0:T(8,128)S(1)} fusion(bf16[2048,2048]{1,0:T(8,128)(2,1)S(1)} %prune.3, bf16[64,2048]{1,0:T(8,128)(2,1)S(1)} %get-tuple-element.52, bf16[64,2048]{1,0:T(8,128)(2,1)S(1)} %get-tuple-element.51), kind=kOutput, calls=%fused_computation.27 | convolution fusion | flops 1074790400 | bytes 9961472 | tf_op jit(solution)/shard_map/dot_general | solution.py:22
  38.7 1.3 %fusion.9 = f32[128,2048]{1,0:T(8,128)S(1)} fusion(bf16[2048,2048]{1,0:T(8,128)(2,1)S(1)} %prune.2, bf16[64,2048]{1,0:T(8,128)(2,1)S(1)} %get-tuple-element.52, bf16[64,2048]{1,0:T(8,128)(2,1)S(1)} %get-tuple-element.51), kind=kOutput, calls=%fused_computation.28 | convolution fusion | flops 1074790400 | bytes 9961472 | tf_op jit(solution)/shard_map/dot_general | solution.py:22
  40.7 1.9 %convolution_add_fusion.1 = f32[192,2048]{1,0:T(8,128)S(1)} fusion(f32[192,2048]{1,0:T(8,128)S(1)} %collective-permute-done.9, bf16[192,2048]{1,0:T(8,128)(2,1)S(1)} %broadcast_select_fusion.3, bf16[2048,2048]{1,0:T(8,128)(2,1)S(1)} %prune.2), kind=kOutput, calls=%fused_computation.2 | convolution fusion | flops 1611005952 | bytes 12320768 | tf_op jit(solution)/shard_map/dot_general | solution.py:22
  43.2 2.2 %multiply_convert_fusion = bf16[192,2048]{1,0:T(8,128)(2,1)S(1)} fusion(f32[192,2048]{1,0:T(8,128)S(1)} %convolution_add_fusion.1, f32[192,2048]{1,0:T(8,128)S(1)} %collective-permute-done.12, bf16[192,2048]{1,0:T(8,128)(2,1)S(1)} %broadcast_select_fusion.3, bf16[2048,2048]{1,0:T(8,128)(2,1)S(1)} %prune.3), kind=kOutput, calls=%fused_computation.7 | convolution fusion | flops 1613365248 | bytes 13107200 | tf_op jit(solution)/shard_map/dot_general | solution.py:22
  45.9 1.3 %convolution_convert_fusion.1 = bf16[128,2048]{1,0:T(8,128)(2,1)S(1)} fusion(bf16[2048,2048]{1,0:T(8,128)(2,1)S(1)} %prune_fetched.1, bf16[64,2048]{1,0:T(8,128)(2,1)S(1)} %get-tuple-element.50, bf16[64,2048]{1,0:T(8,128)(2,1)S(1)} %get-tuple-element.49), kind=kOutput, calls=%fused_computation.3 | convolution fusion | flops 1075052544 | bytes 9437184 | tf_op jit(solution)/shard_map/dot_general | solution.py:22
  48.3 3.7 %convolution_convert_fusion = bf16[384,2048]{1,0:T(8,128)(2,1)S(1)} fusion(bf16[2048,2048]{1,0:T(8,128)(2,1)S(1)} %prune_fetched.1, bf16[192,2048]{1,0:T(8,128)(2,1)S(1)} %get-tuple-element.46, bf16[192,2048]{1,0:T(8,128)(2,1)S(1)} %get-tuple-element.45), kind=kOutput, calls=%fused_computation | convolution fusion | flops 3225157632 | bytes 11534336 | tf_op jit(solution)/shard_map/dot_general | solution.py:22
  53.4 3.1 %collective-permute-done.15 = bf16[64,2048]{1,0:T(8,128)(2,1)S(1)} collective-permute-done((bf16[64,2048]{1,0:T(8,128)(2,1)S(1)}, bf16[64,2048]{1,0:T(8,128)(2,1)S(1)}, u32[]{:S(2)}, u32[]{:S(2)}) %collective-permute-start.15) | collective-permute-done | bytes 262176 | tf_op jit(solution)/shard_map/ppermute | solution.py:46
  56.6 2.0 %collective-permute-start.16 = (bf16[64,2048]{1,0:T(8,128)(2,1)S(1)}, bf16[64,2048]{1,0:T(8,128)(2,1)S(1)}, u32[]{:S(2)}, u32[]{:S(2)}) collective-permute-start(bf16[64,2048]{1,0:T(8,128)(2,1)S(1)} %add_convert_fusion.5), channel_id=1, source_target_pairs={{0,4},{2,6},{4,0},{6,2},{8,12},{10,14},{12,8},{14,10},{1,5},{3,7},... | collective-permute-start | bytes 786440 | tf_op jit(solution)/shard_map/ppermute | solution.py:46
  58.9 3.3 %collective-permute-done.18 = bf16[64,2048]{1,0:T(8,128)(2,1)S(1)} collective-permute-done((bf16[64,2048]{1,0:T(8,128)(2,1)S(1)}, bf16[64,2048]{1,0:T(8,128)(2,1)S(1)}, u32[]{:S(2)}, u32[]{:S(2)}) %collective-permute-start.18) | collective-permute-done | bytes 262176 | tf_op jit(solution)/shard_map/ppermute | solution.py:46
  62.2 2.0 %collective-permute-start.19 = (bf16[64,2048]{1,0:T(8,128)(2,1)S(1)}, bf16[64,2048]{1,0:T(8,128)(2,1)S(1)}, u32[]{:S(2)}, u32[]{:S(2)}) collective-permute-start(bf16[64,2048]{1,0:T(8,128)(2,1)S(1)} %add_convert_fusion.3), channel_id=1, source_target_pairs={{0,4},{2,6},{4,0},{6,2},{8,12},{10,14},{12,8},{14,10},{1,5},{3,7},... | collective-permute-start | bytes 786440 | tf_op jit(solution)/shard_map/ppermute | solution.py:46
  65.5 3.7 %collective-permute-done.19 = bf16[64,2048]{1,0:T(8,128)(2,1)S(1)} collective-permute-done((bf16[64,2048]{1,0:T(8,128)(2,1)S(1)}, bf16[64,2048]{1,0:T(8,128)(2,1)S(1)}, u32[]{:S(2)}, u32[]{:S(2)}) %collective-permute-start.19) | collective-permute-done | bytes 262176 | tf_op jit(solution)/shard_map/ppermute | solution.py:46
  70.1 4.4 %collective-permute-start.23 = (bf16[64,2048]{1,0:T(8,128)(2,1)S(1)}, bf16[64,2048]{1,0:T(8,128)(2,1)S(1)}, u32[]{:S(2)}, u32[]{:S(2)}) collective-permute-start(bf16[64,2048]{1,0:T(8,128)(2,1)S(1)} %add_convert_fusion.1), channel_id=1, source_target_pairs={{0,4},{2,6},{4,0},{6,2},{8,12},{10,14},{12,8},{14,10},{1,5},{3,7},... | collective-permute-start | bytes 786440 | tf_op jit(solution)/shard_map/ppermute | solution.py:46
  74.5 4.3 %collective-permute-done.23 = bf16[64,2048]{1,0:T(8,128)(2,1)S(1)} collective-permute-done((bf16[64,2048]{1,0:T(8,128)(2,1)S(1)}, bf16[64,2048]{1,0:T(8,128)(2,1)S(1)}, u32[]{:S(2)}, u32[]{:S(2)}) %collective-permute-start.23) | collective-permute-done | bytes 262176 | tf_op jit(solution)/shard_map/ppermute | solution.py:46
  (68 shorter events, 14.3 us)
Async XLA Ops:
  0.0 10.4 %collective-permute-start.1 = (bf16[64,2048]{1,0:T(8,128)(2,1)}, bf16[64,2048]{1,0:T(8,128)(2,1)S(1)}, u32[]{:S(2)}, u32[]{:S(2)}) collective-permute-start(bf16[64,2048]{1,0:T(8,128)(2,1)} %param.7), channel_id=1, source_target_pairs={{0,4},{2,6},{4,0},{6,2},{8,12},{10,14},{12,8},{14,10},{1,5},{3,7},... | collective-permute-start | bytes 786440 | tf_op jit(solution)/shard_map/ppermute | solution.py:46
  3.0 8.0 %collective-permute-start = (bf16[64,2048]{1,0:T(8,128)(2,1)}, bf16[64,2048]{1,0:T(8,128)(2,1)S(1)}, u32[]{:S(2)}, u32[]{:S(2)}) collective-permute-start(bf16[64,2048]{1,0:T(8,128)(2,1)} %param.7), channel_id=1, source_target_pairs={{0,2},{2,0},{4,6},{6,4},{8,10},{10,8},{12,14},{14,12},{1,3},{3,1},... | collective-permute-start | bytes 786440 | tf_op jit(solution)/shard_map/ppermute | solution.py:46
  4.5 8.7 %collective-permute-start.3 = (bf16[64,2048]{1,0:T(8,128)(2,1)}, bf16[64,2048]{1,0:T(8,128)(2,1)S(1)}, u32[]{:S(2)}, u32[]{:S(2)}) collective-permute-start(bf16[64,2048]{1,0:T(8,128)(2,1)} %param.7), channel_id=1, source_target_pairs={{4,8},{6,10},{8,4},{10,6},{5,9},{7,11},{9,5},{11,7},{20,24},{22,26... | collective-permute-start | bytes 786440 | tf_op jit(solution)/shard_map/ppermute | solution.py:46
  11.0 12.8 %collective-permute-start.2 = (bf16[64,2048]{1,0:T(8,128)(2,1)S(1)}, bf16[64,2048]{1,0:T(8,128)(2,1)S(1)}, u32[]{:S(2)}, u32[]{:S(2)}) collective-permute-start(bf16[64,2048]{1,0:T(8,128)(2,1)S(1)} %collective-permute-done.1), channel_id=1, source_target_pairs={{0,2},{2,0},{4,6},{6,4},{8,10},{10,8},{12,14},{14,12},{1,3},{3,1},... | collective-permute-start | bytes 786440 | tf_op jit(solution)/shard_map/ppermute | solution.py:46
  12.5 6.8 %collective-permute-start.5 = (bf16[64,2048]{1,0:T(8,128)(2,1)S(1)}, bf16[64,2048]{1,0:T(8,128)(2,1)S(1)}, u32[]{:S(2)}, u32[]{:S(2)}) collective-permute-start(bf16[64,2048]{1,0:T(8,128)(2,1)S(1)} %collective-permute-done.1), channel_id=1, source_target_pairs={{4,8},{6,10},{8,4},{10,6},{5,9},{7,11},{9,5},{11,7},{20,24},{22,26... | collective-permute-start | bytes 786440 | tf_op jit(solution)/shard_map/ppermute | solution.py:46
  13.2 10.5 %collective-permute-start.4 = (bf16[64,2048]{1,0:T(8,128)(2,1)S(1)}, bf16[64,2048]{1,0:T(8,128)(2,1)S(1)}, u32[]{:S(2)}, u32[]{:S(2)}) collective-permute-start(bf16[64,2048]{1,0:T(8,128)(2,1)S(1)} %collective-permute-done.3), channel_id=1, source_target_pairs={{4,0},{6,2},{8,12},{10,14},{5,1},{7,3},{9,13},{11,15},{20,16},{22,... | collective-permute-start | bytes 786440 | tf_op jit(solution)/shard_map/ppermute | solution.py:46
  19.4 11.4 %collective-permute-start.6 = (bf16[64,2048]{1,0:T(8,128)(2,1)S(1)}, bf16[64,2048]{1,0:T(8,128)(2,1)S(1)}, u32[]{:S(2)}, u32[]{:S(2)}) collective-permute-start(bf16[64,2048]{1,0:T(8,128)(2,1)S(1)} %collective-permute-done.5), channel_id=1, source_target_pairs={{4,0},{6,2},{8,12},{10,14},{5,1},{7,3},{9,13},{11,15},{20,16},{22,... | collective-permute-start | bytes 786440 | tf_op jit(solution)/shard_map/ppermute | solution.py:46
  23.8 7.1 %collective-permute-start.7 = (bf16[64,2048]{1,0:T(8,128)(2,1)S(1)}, bf16[64,2048]{1,0:T(8,128)(2,1)S(1)}, u32[]{:S(2)}, u32[]{:S(2)}) collective-permute-start(bf16[64,2048]{1,0:T(8,128)(2,1)S(1)} %broadcast_select_fusion.9), channel_id=1, source_target_pairs={{0,2},{2,0},{4,6},{6,4},{8,10},{10,8},{12,14},{14,12},{1,3},{3,1},... | collective-permute-start | bytes 786440 | tf_op jit(solution)/shard_map/ppermute | solution.py:46
  30.9 6.4 %collective-permute-start.8 = (bf16[64,2048]{1,0:T(8,128)(2,1)S(1)}, bf16[64,2048]{1,0:T(8,128)(2,1)S(1)}, u32[]{:S(2)}, u32[]{:S(2)}) collective-permute-start(bf16[64,2048]{1,0:T(8,128)(2,1)S(1)} %broadcast_select_fusion.8), channel_id=1, source_target_pairs={{0,2},{2,0},{4,6},{6,4},{8,10},{10,8},{12,14},{14,12},{1,3},{3,1},... | collective-permute-start | bytes 786440 | tf_op jit(solution)/shard_map/ppermute | solution.py:46
  33.7 7.0 %collective-permute-start.9 = (f32[192,2048]{1,0:T(8,128)S(1)}, f32[192,2048]{1,0:T(8,128)S(1)}, u32[]{:S(2)}, u32[]{:S(2)}) collective-permute-start(f32[192,2048]{1,0:T(8,128)S(1)} %fusion.15), channel_id=1, source_target_pairs={{0,1},{1,0},{2,3},{3,2},{4,5},{5,4},{6,7},{7,6},{8,9},{9,8},{10,11... | collective-permute-start | bytes 4718600 | tf_op jit(solution)/shard_map/ppermute | solution.py:103
  35.7 7.6 %collective-permute-start.12 = (f32[192,2048]{1,0:T(8,128)S(1)}, f32[192,2048]{1,0:T(8,128)S(1)}, u32[]{:S(2)}, u32[]{:S(2)}) collective-permute-start(f32[192,2048]{1,0:T(8,128)S(1)} %fusion.14), channel_id=1, source_target_pairs={{0,1},{1,0},{2,3},{3,2},{4,5},{5,4},{6,7},{7,6},{8,9},{9,8},{10,11... | collective-permute-start | bytes 4718600 | tf_op jit(solution)/shard_map/ppermute | solution.py:103
  40.1 2.5 %collective-permute-start.11 = (f32[64,2048]{1,0:T(8,128)S(1)}, f32[64,2048]{1,0:T(8,128)S(1)}, u32[]{:S(2)}, u32[]{:S(2)}) collective-permute-start(f32[64,2048]{1,0:T(8,128)S(1)} %slice.19), channel_id=1, source_target_pairs={{0,1},{1,0},{2,3},{3,2},{4,5},{5,4},{6,7},{7,6},{8,9},{9,8},{10,11... | collective-permute-start | bytes 1572872 | tf_op jit(solution)/shard_map/ppermute | solution.py:103
  40.2 2.6 %collective-permute-start.10 = (f32[64,2048]{1,0:T(8,128)S(1)}, f32[64,2048]{1,0:T(8,128)S(1)}, u32[]{:S(2)}, u32[]{:S(2)}) collective-permute-start(f32[64,2048]{1,0:T(8,128)S(1)} %slice.17), channel_id=1, source_target_pairs={{0,1},{1,0},{2,3},{3,2},{4,5},{5,4},{6,7},{7,6},{8,9},{9,8},{10,11... | collective-permute-start | bytes 1572872 | tf_op jit(solution)/shard_map/ppermute | solution.py:103
  43.0 2.9 %collective-permute-start.14 = (bf16[64,2048]{1,0:T(8,128)(2,1)S(1)}, bf16[64,2048]{1,0:T(8,128)(2,1)S(1)}, u32[]{:S(2)}, u32[]{:S(2)}) collective-permute-start(bf16[64,2048]{1,0:T(8,128)(2,1)S(1)} %fusion.4), channel_id=1, source_target_pairs={{0,1},{1,0},{2,3},{3,2},{4,5},{5,4},{6,7},{7,6},{8,9},{9,8},{10,11... | collective-permute-start | bytes 786440 | tf_op jit(solution)/shard_map/ppermute | solution.py:103
  45.5 2.7 %collective-permute-start.13 = (bf16[192,2048]{1,0:T(8,128)(2,1)S(1)}, bf16[192,2048]{1,0:T(8,128)(2,1)S(1)}, u32[]{:S(2)}, u32[]{:S(2)}) collective-permute-start(bf16[192,2048]{1,0:T(8,128)(2,1)S(1)} %multiply_convert_fusion), channel_id=1, source_target_pairs={{0,1},{1,0},{2,3},{3,2},{4,5},{5,4},{6,7},{7,6},{8,9},{9,8},{10,11... | collective-permute-start | bytes 2359304 | tf_op jit(solution)/shard_map/ppermute | solution.py:103
  47.3 9.2 %collective-permute-start.15 = (bf16[64,2048]{1,0:T(8,128)(2,1)S(1)}, bf16[64,2048]{1,0:T(8,128)(2,1)S(1)}, u32[]{:S(2)}, u32[]{:S(2)}) collective-permute-start(bf16[64,2048]{1,0:T(8,128)(2,1)S(1)} %get-tuple-element.48), channel_id=1, source_target_pairs={{0,2},{2,0},{4,6},{6,4},{8,10},{10,8},{12,14},{14,12},{1,3},{3,1},... | collective-permute-start | bytes 786440 | tf_op jit(solution)/shard_map/ppermute | solution.py:46
  52.1 10.0 %collective-permute-start.18 = (bf16[64,2048]{1,0:T(8,128)(2,1)S(1)}, bf16[64,2048]{1,0:T(8,128)(2,1)S(1)}, u32[]{:S(2)}, u32[]{:S(2)}) collective-permute-start(bf16[64,2048]{1,0:T(8,128)(2,1)S(1)} %get-tuple-element.43), channel_id=1, source_target_pairs={{0,2},{2,0},{4,6},{6,4},{8,10},{10,8},{12,14},{14,12},{1,3},{3,1},... | collective-permute-start | bytes 786440 | tf_op jit(solution)/shard_map/ppermute | solution.py:46
  56.6 7.6 %collective-permute-start.16 = (bf16[64,2048]{1,0:T(8,128)(2,1)S(1)}, bf16[64,2048]{1,0:T(8,128)(2,1)S(1)}, u32[]{:S(2)}, u32[]{:S(2)}) collective-permute-start(bf16[64,2048]{1,0:T(8,128)(2,1)S(1)} %add_convert_fusion.5), channel_id=1, source_target_pairs={{0,4},{2,6},{4,0},{6,2},{8,12},{10,14},{12,8},{14,10},{1,5},{3,7},... | collective-permute-start | bytes 786440 | tf_op jit(solution)/shard_map/ppermute | solution.py:46
  58.6 11.4 %collective-permute-start.21 = (bf16[64,2048]{1,0:T(8,128)(2,1)S(1)}, bf16[64,2048]{1,0:T(8,128)(2,1)S(1)}, u32[]{:S(2)}, u32[]{:S(2)}) collective-permute-start(bf16[64,2048]{1,0:T(8,128)(2,1)S(1)} %get-tuple-element.40), channel_id=1, source_target_pairs={{0,2},{2,0},{4,6},{6,4},{8,10},{10,8},{12,14},{14,12},{1,3},{3,1},... | collective-permute-start | bytes 786440 | tf_op jit(solution)/shard_map/ppermute | solution.py:46
  62.2 7.0 %collective-permute-start.19 = (bf16[64,2048]{1,0:T(8,128)(2,1)S(1)}, bf16[64,2048]{1,0:T(8,128)(2,1)S(1)}, u32[]{:S(2)}, u32[]{:S(2)}) collective-permute-start(bf16[64,2048]{1,0:T(8,128)(2,1)S(1)} %add_convert_fusion.3), channel_id=1, source_target_pairs={{0,4},{2,6},{4,0},{6,2},{8,12},{10,14},{12,8},{14,10},{1,5},{3,7},... | collective-permute-start | bytes 786440 | tf_op jit(solution)/shard_map/ppermute | solution.py:46
  64.3 5.7 %collective-permute-start.22 = (bf16[64,2048]{1,0:T(8,128)(2,1)S(1)}, bf16[64,2048]{1,0:T(8,128)(2,1)S(1)}, u32[]{:S(2)}, u32[]{:S(2)}) collective-permute-start(bf16[64,2048]{1,0:T(8,128)(2,1)S(1)} %add_convert_fusion.4), channel_id=1, source_target_pairs={{4,8},{6,10},{8,4},{10,6},{5,9},{7,11},{9,5},{11,7},{20,24},{22,26... | collective-permute-start | bytes 786440 | tf_op jit(solution)/shard_map/ppermute | solution.py:46
  65.0 9.5 %collective-permute-start.17 = (bf16[64,2048]{1,0:T(8,128)(2,1)S(1)}, bf16[64,2048]{1,0:T(8,128)(2,1)S(1)}, u32[]{:S(2)}, u32[]{:S(2)}) collective-permute-start(bf16[64,2048]{1,0:T(8,128)(2,1)S(1)} %get-tuple-element.38), channel_id=1, source_target_pairs={{0,2},{2,0},{4,6},{6,4},{8,10},{10,8},{12,14},{14,12},{1,3},{3,1},... | collective-permute-start | bytes 786440 | tf_op jit(solution)/shard_map/ppermute | solution.py:46
  69.3 5.2 %collective-permute-start.20 = (bf16[64,2048]{1,0:T(8,128)(2,1)S(1)}, bf16[64,2048]{1,0:T(8,128)(2,1)S(1)}, u32[]{:S(2)}, u32[]{:S(2)}) collective-permute-start(bf16[64,2048]{1,0:T(8,128)(2,1)S(1)} %add_convert_fusion.2), channel_id=1, source_target_pairs={{4,8},{6,10},{8,4},{10,6},{5,9},{7,11},{9,5},{11,7},{20,24},{22,26... | collective-permute-start | bytes 786440 | tf_op jit(solution)/shard_map/ppermute | solution.py:46
  70.1 8.8 %collective-permute-start.23 = (bf16[64,2048]{1,0:T(8,128)(2,1)S(1)}, bf16[64,2048]{1,0:T(8,128)(2,1)S(1)}, u32[]{:S(2)}, u32[]{:S(2)}) collective-permute-start(bf16[64,2048]{1,0:T(8,128)(2,1)S(1)} %add_convert_fusion.1), channel_id=1, source_target_pairs={{0,4},{2,6},{4,0},{6,2},{8,12},{10,14},{12,8},{14,10},{1,5},{3,7},... | collective-permute-start | bytes 786440 | tf_op jit(solution)/shard_map/ppermute | solution.py:46
  (6 other events, 46.2 us)
